TPU v7x, 32 devices: a whole 2x2x4 slice. The times are simulated.
32 devices in a mesh: blk: 2 (over x), head: 4 (over y, core), batch: 4 (over z).
Axes of the slice: x: 2, y: 2, z: 4, core: 2. Of those that a mesh axis runs over, the one named last changes fastest.
Arguments:
- query_rows: bfloat16 [2048, 3072], P(('batch', 'blk'), 'head'), parts along dimension 0, may hold values from -6 to 6
- key_rows: bfloat16 [2048, 3072], P(('batch', 'blk'), 'head'), parts along dimension 0, may hold values from -6 to 6
- value_rows: bfloat16 [2048, 3072], P(('batch', 'blk'), 'head'), parts along dimension 0, may hold values from -6 to 6
- query_tangent: bfloat16 [2048, 3072], P(('batch', 'blk'), 'head'), parts along dimension 0, may hold values from -6 to 6
- key_tangent: bfloat16 [2048, 3072], P(('batch', 'blk'), 'head'), parts along dimension 0, may hold values from -6 to 6
- value_tangent: bfloat16 [2048, 3072], P(('batch', 'blk'), 'head'), parts along dimension 0, may hold values from -6 to 6
Outputs:
- attended: bfloat16 [2048, 3072], P(('batch', 'blk', 'head')), parts along dimension 0
- attended_tangent: bfloat16 [2048, 3072], P(('batch', 'blk', 'head')), parts along dimension 0
There are 4 independent parts, one for each index of `batch`. A program takes and returns all parts, laid end to end along the dimension named above; each array names one. Nothing has to cross between parts.
All inputs are finite; a program needn't handle non-finite values.
Results may differ from a plain program's by a relative error of at most 0.011.
Values may be sent and summed in bfloat16 or wider, within the bound.
No kernel may reach another device: no remote copies, remote signals or barrier semaphores. Data moves between devices by JAX's collectives and lax.ppermute only.
A program may use at most 128 MiB of HBM per device.

v0:
```python
from functools import partial

import jax
import jax.numpy as jnp
from jax import lax
from jax.sharding import PartitionSpec as P

HD = 128


LOWEST = -1e30


def score_pair(query_heads, tangent_heads, key_block, key_change, scaling):
    scores = (
        jnp.einsum("qhd,khd->qhk", query_heads, key_block, preferred_element_type=jnp.float32)
        * scaling
    )
    score_change = (
        jnp.einsum("qhd,khd->qhk", tangent_heads, key_block, preferred_element_type=jnp.float32)
        + jnp.einsum("qhd,khd->qhk", query_heads, key_change, preferred_element_type=jnp.float32)
    ) * scaling
    return (scores, score_change)


def block_update(running, members, query_heads, tangent_heads, scaling):
    row_max, row_total, row_shift, numerator, tangent_numerator = running
    key_block, value_block, key_change, value_change = members
    scores, score_change = score_pair(query_heads, tangent_heads, key_block, key_change, scaling)
    new_max = jnp.maximum(row_max, jnp.max(scores, axis=2))
    shrink = jnp.exp(row_max - new_max)
    weights = jnp.exp(scores - new_max[:, :, None])
    mixed_terms = weights * score_change
    row_total = row_total * shrink + jnp.sum(weights, axis=2)
    row_shift = row_shift * shrink + jnp.sum(mixed_terms, axis=2)
    weights_low = weights.astype(jnp.bfloat16)
    mixed_low = mixed_terms.astype(jnp.bfloat16)
    numerator = numerator * shrink[:, :, None] + jnp.einsum(
        "qhk,khd->qhd", weights_low, value_block, preferred_element_type=jnp.float32
    )
    tangent_numerator = (
        tangent_numerator * shrink[:, :, None]
        + jnp.einsum("qhk,khd->qhd", mixed_low, value_block, preferred_element_type=jnp.float32)
        + jnp.einsum("qhk,khd->qhd", weights_low, value_change, preferred_element_type=jnp.float32)
    )
    return (new_max, row_total, row_shift, numerator, tangent_numerator)


def fold_keys(running, pieces, start, query_heads, tangent_heads):
    key_count = pieces[0].shape[0]
    head_count = query_heads.shape[1]
    head_width = query_heads.shape[2]
    block_rows = key_count
    while block_rows > 1024 and block_rows % 2 == 0:
        block_rows = block_rows // 2
    stacked = tuple(
        (
            member.reshape(key_count // block_rows, block_rows, head_count, head_width)
            for member in pieces
        )
    )
    scaling = head_width ** (-0.5)

    def advance(carried, members):
        return (block_update(carried, members, query_heads, tangent_heads, scaling), None)

    running, unused = lax.scan(advance, running, stacked)
    return running


def prepare(query_rows, query_tangent):
    query_heads = query_rows.reshape(query_rows.shape[0], -1, HD)
    tangent_heads = query_tangent.reshape(query_tangent.shape[0], -1, HD)
    rows_here = query_heads.shape[0]
    head_count = query_heads.shape[1]
    zero_stats = jnp.zeros((rows_here, head_count), jnp.float32)
    zero_rows = jnp.zeros((rows_here, head_count, HD), jnp.float32)
    initial = (
        jnp.full((rows_here, head_count), LOWEST, jnp.float32),
        zero_stats,
        zero_stats,
        zero_rows,
        zero_rows,
    )
    folder = partial(fold_keys, query_heads=query_heads, tangent_heads=tangent_heads)
    return (folder, initial)


def finish(running):
    row_max, row_total, row_shift, numerator, tangent_numerator = running
    attended = numerator / row_total[:, :, None]
    attended_tangent = (
        tangent_numerator / row_total[:, :, None] - (row_shift / row_total)[:, :, None] * attended
    )
    rows_here = attended.shape[0]
    return (
        attended.reshape(rows_here, -1).astype(jnp.bfloat16),
        attended_tangent.reshape(rows_here, -1).astype(jnp.bfloat16),
    )


def local(query_rows, key_rows, value_rows, query_tangent, key_tangent, value_tangent):
    folder, initial = prepare(query_rows, query_tangent)
    running = folder(
        initial,
        (
            lax.all_gather(key_rows, "blk", axis=0, tiled=True),
            lax.all_gather(value_rows, "blk", axis=0, tiled=True),
            lax.all_gather(key_tangent, "blk", axis=0, tiled=True),
            lax.all_gather(value_tangent, "blk", axis=0, tiled=True),
        ),
        jnp.int32(0),
    )
    result_rows, result_tangent = finish(running)
    attended, attended_tangent = (
        lax.all_to_all(result_rows, "head", split_axis=0, concat_axis=1, tiled=True),
        lax.all_to_all(result_tangent, "head", split_axis=0, concat_axis=1, tiled=True),
    )
    return (attended, attended_tangent)


def solution(mesh):
    return jax.shard_map(
        local,
        mesh=mesh,
        in_specs=(
            P(("batch", "blk"), "head"),
            P(("batch", "blk"), "head"),
            P(("batch", "blk"), "head"),
            P(("batch", "blk"), "head"),
            P(("batch", "blk"), "head"),
            P(("batch", "blk"), "head"),
        ),
        out_specs=(P(("batch", "blk", "head"), None), P(("batch", "blk", "head"), None)),
        check_vma=False,
    )
```

profile of v0, /device:TPU:0, one launch (start us, length us, event | category | flops | bytes accessed | tf_op | source)
XLA Modules:
  0.0 92.8 jit_solution(13744085068160464138)
XLA Ops:
  0.6 1.2 %copy.34 = bf16[256,768]{0,1:T(8,128)(2,1)S(1)} copy(bf16[256,768]{1,0:T(8,128)(2,1)} %param.7) | data formatting | bytes 786432 | tf_op args[1]
  1.8 12.8 %all_gather.12 = bf16[512,768]{0,1:T(8,128)(2,1)} all-gather(bf16[256,768]{0,1:T(8,128)(2,1)S(1)} %copy.34), channel_id=1, replica_groups=mesh['blk'=2,'head'=4,'batch'=4] {'blk'}, dimensions={0}, use_global_device_ids=true | all-gather | bytes 1179648 | tf_op jit(solution)/shard_map/all_gather | solution.py:107
  14.6 1.2 %copy.35 = bf16[256,768]{0,1:T(8,128)(2,1)S(1)} copy(bf16[256,768]{1,0:T(8,128)(2,1)} %param.6) | data formatting | bytes 786432 | tf_op args[0]
  15.8 1.8 %bitcast_reduce_fusion = (f32[256,6]{0,1:T(8,128)S(1)}, f32[6,512,256]{2,1,0:T(8,128)S(1)}) fusion(bf16[512,6,128]{0,2,1:T(8,128)(2,1)} %bitcast.59, bf16[256,6,128]{0,2,1:T(8,128)(2,1)S(1)} %bitcast.61), kind=kOutput, calls=%fused_computation.2 | convolution fusion | flops 202897920 | bytes 4331520 | tf_op jit(solution)/shard_map/while/body/eval_jaxpr/qhd,khd->qhk/dot_general | solution.py:16
  17.6 1.9 %copy.43 = bf16[256,768]{0,1:T(8,128)(2,1)} copy(bf16[256,768]{1,0:T(8,128)(2,1)} %param.9) | data formatting | bytes 786432 | tf_op args[3]
  19.5 3.5 %fusion.32 = f32[6,512,256]{2,1,0:T(8,128)} fusion(bf16[512,6,128]{0,2,1:T(8,128)(2,1)} %bitcast.60, bf16[256,6,128]{0,2,1:T(8,128)(2,1)} %bitcast.67), kind=kOutput, calls=%fused_computation.26 | convolution fusion | flops 201326592 | bytes 4325376 | tf_op jit(solution)/shard_map/while/body/eval_jaxpr/qhd,khd->qhk/dot_general | solution.py:20
  23.0 1.9 %copy.46 = bf16[256,768]{0,1:T(8,128)(2,1)} copy(bf16[256,768]{1,0:T(8,128)(2,1)} %param.10) | data formatting | bytes 786432 | tf_op args[4]
  24.9 12.7 %all_gather.14 = bf16[512,768]{0,1:T(8,128)(2,1)} all-gather(bf16[256,768]{0,1:T(8,128)(2,1)} %copy.46), channel_id=1, replica_groups=mesh['blk'=2,'head'=4,'batch'=4] {'blk'}, dimensions={0}, use_global_device_ids=true | all-gather | bytes 1179648 | tf_op jit(solution)/shard_map/all_gather | solution.py:109
  37.6 1.9 %copy.38 = bf16[256,768]{0,1:T(8,128)(2,1)} copy(bf16[256,768]{1,0:T(8,128)(2,1)} %param.8) | data formatting | bytes 786432 | tf_op args[2]
  39.5 11.2 %all_gather.13 = bf16[512,768]{0,1:T(8,128)(2,1)} all-gather(bf16[256,768]{0,1:T(8,128)(2,1)} %copy.38), channel_id=1, replica_groups=mesh['blk'=2,'head'=4,'batch'=4] {'blk'}, dimensions={0}, use_global_device_ids=true | all-gather | bytes 1179648 | tf_op jit(solution)/shard_map/all_gather | solution.py:108
  50.6 1.9 %copy.51 = bf16[256,768]{0,1:T(8,128)(2,1)} copy(bf16[256,768]{1,0:T(8,128)(2,1)} %param.11) | data formatting | bytes 786432 | tf_op args[5]
  52.6 9.8 %all_gather.15 = bf16[512,768]{0,1:T(8,128)(2,1)S(1)} all-gather(bf16[256,768]{0,1:T(8,128)(2,1)} %copy.51), channel_id=1, replica_groups=mesh['blk'=2,'head'=4,'batch'=4] {'blk'}, dimensions={0}, use_global_device_ids=true | all-gather | bytes 1179648 | tf_op jit(solution)/shard_map/all_gather | solution.py:110
  62.4 0.5 fusion.1
  62.9 0.0 copy-start
  62.9 0.0 copy-start.1
  62.9 0.8 convolution_bitcast_fusion
  63.7 1.1 %copy-done = f32[6,512,256]{2,1,0:T(8,128)S(1)} copy-done((f32[6,512,256]{2,1,0:T(8,128)S(1)}, f32[6,512,256]{2,1,0:T(8,128)}, u32[]{:S(2)}) %copy-start) | copy-done | bytes 3145752
  64.8 0.2 copy-done.1
  65.0 0.0 copy-start.2
  65.0 1.2 %fusion.30 = (f32[256,6]{0,1:T(8,128)S(1)}, bf16[256,6,512]{0,2,1:T(8,128)(2,1)S(1)}) fusion(f32[6,512,256]{2,1,0:T(8,128)S(1)} %copy-done, bf16[512,6,128]{0,2,1:T(8,128)(2,1)S(1)} %bitcast.63, bf16[256,6,128]{0,2,1:T(8,128)(2,1)S(1)} %bitcast.62, f32[256,6]{0,1:T(8,128)S(1)} %broadcast_maximum_fusion, f32[6,512,256]{2,1,0:T(8,128)S(1)} %get-tuple-element.30), kind=kOutput, calls=%fused_computation.24 | convolution fusion | flops 206830080 | bytes 9056256 | tf_op jit(solution)/shard_map/while/body/eval_jaxpr/qhd,khd->qhk/dot_general | solution.py:21
  66.3 0.0 copy-done.2
  66.3 1.3 %fusion.31 = (bf16[256,6,128]{2,0,1:T(8,128)(2,1)S(1)}, f32[256,6,128]{2,0,1:T(8,128)S(1)}) fusion(f32[256,6]{0,1:T(8,128)S(1)} %get-tuple-element.27, bf16[512,6,128]{0,2,1:T(8,128)(2,1)S(1)} %bitcast.68, f32[6,512,256]{2,1,0:T(8,128)S(1)} %get-tuple-element.30, f32[256,6]{0,1:T(8,128)S(1)} %broadcast_maximum_fusion, f32[256,6]{0,1:T(8,128)S(1)} %get-tuple-element.28), kind=kOutput, calls=%fused_computation.25 | convolution fusion | flops 204275712 | bytes 5130240 | tf_op jit(solution)/shard_map/while/body/eval_jaxpr/qhk,khd->qhd/dot_general | solution.py:38
  67.6 1.3 %fusion.22 = bf16[256,6,128]{2,0,1:T(8,128)(2,1)S(1)} fusion(f32[256,6,128]{2,0,1:T(8,128)S(1)} %convolution_bitcast_fusion, bf16[512,6,128]{0,2,1:T(8,128)(2,1)S(1)} %bitcast.69, bf16[256,6,512]{0,2,1:T(8,128)(2,1)S(1)} %get-tuple-element.32, f32[256,6,128]{2,0,1:T(8,128)S(1)} %get-tuple-element.34, f32[256,6]{0,1:T(8,128)S(1)} %get-tuple-element.26, ...), kind=kOutput, calls=%fused_computation.17 | convolution fusion | flops 202506240 | bytes 4343808 | tf_op jit(solution)/shard_map/while/body/eval_jaxpr/qhk,khd->qhd/dot_general | solution.py:43
  68.8 0.3 copy.54
  69.1 1.2 %convert_element_type.27 = bf16[4,64,768]{2,1,0:T(8,128)(2,1)} reshape(bf16[256,6,128]{2,1,0:T(8,128)(2,1)S(1)} %copy.54) | data formatting | bytes 786432 | tf_op jit(solution)/shard_map/convert_element_type | solution.py:98
  70.3 3.5 %all-to-all-start.1 = ((bf16[4,64,768]{2,1,0:T(8,128)(2,1)}), bf16[4,64,768]{2,1,0:T(8,128)(2,1)S(1)}, u32[]{:S(2)}, u32[]{:S(2)}) async-start(bf16[4,64,768]{2,1,0:T(8,128)(2,1)} %convert_element_type.27), calls=%async_computation.1 | async-start | bytes 786432 | tf_op jit(solution)/shard_map/all_to_all | solution.py:117
  73.8 0.3 copy.41
  74.1 1.2 %convert_element_type.24 = bf16[4,64,768]{2,1,0:T(8,128)(2,1)} reshape(bf16[256,6,128]{2,1,0:T(8,128)(2,1)S(1)} %copy.41) | data formatting | bytes 786432 | tf_op jit(solution)/shard_map/convert_element_type | solution.py:97
  75.3 5.9 %all-to-all-done.1 = bf16[4,64,768]{2,1,0:T(8,128)(2,1)S(1)} async-done(((bf16[4,64,768]{2,1,0:T(8,128)(2,1)}), bf16[4,64,768]{2,1,0:T(8,128)(2,1)S(1)}, u32[]{:S(2)}, u32[]{:S(2)}) %all-to-all-start.1) | async-done | bytes 393248 | tf_op jit(solution)/shard_map/all_to_all | solution.py:117
  81.2 3.5 %all-to-all-start = ((bf16[4,64,768]{2,1,0:T(8,128)(2,1)}), bf16[4,64,768]{2,1,0:T(8,128)(2,1)S(1)}, u32[]{:S(2)}, u32[]{:S(2)}) async-start(bf16[4,64,768]{2,1,0:T(8,128)(2,1)} %convert_element_type.24), calls=%async_computation | async-start | bytes 786432 | tf_op jit(solution)/shard_map/all_to_all | solution.py:116
  84.6 0.8 copy.69
  85.4 6.6 %all-to-all-done = bf16[4,64,768]{2,1,0:T(8,128)(2,1)S(1)} async-done(((bf16[4,64,768]{2,1,0:T(8,128)(2,1)}), bf16[4,64,768]{2,1,0:T(8,128)(2,1)S(1)}, u32[]{:S(2)}, u32[]{:S(2)}) %all-to-all-start) | async-done | bytes 393248 | tf_op jit(solution)/shard_map/all_to_all | solution.py:116
  92.1 0.8 copy.68
  (2 shorter events, 0.0 us)
Async XLA Ops:
  62.9 1.9 %copy-start = (f32[6,512,256]{2,1,0:T(8,128)S(1)}, f32[6,512,256]{2,1,0:T(8,128)}, u32[]{:S(2)}) copy-start(f32[6,512,256]{2,1,0:T(8,128)} %fusion.32) | copy-start | bytes 9437188
  62.9 2.1 %copy-start.1 = (bf16[512,768]{0,1:T(8,128)(2,1)S(1)}, bf16[512,768]{0,1:T(8,128)(2,1)}, u32[]{:S(2)}) copy-start(bf16[512,768]{0,1:T(8,128)(2,1)} %all_gather.14) | copy-start | bytes 2359300
  65.0 1.3 %copy-start.2 = (bf16[512,768]{0,1:T(8,128)(2,1)S(1)}, bf16[512,768]{0,1:T(8,128)(2,1)}, u32[]{:S(2)}) copy-start(bf16[512,768]{0,1:T(8,128)(2,1)} %all_gather.13) | copy-start | bytes 2359300
  70.3 10.9 %all-to-all-start.1 = ((bf16[4,64,768]{2,1,0:T(8,128)(2,1)}), bf16[4,64,768]{2,1,0:T(8,128)(2,1)S(1)}, u32[]{:S(2)}, u32[]{:S(2)}) async-start(bf16[4,64,768]{2,1,0:T(8,128)(2,1)} %convert_element_type.27), calls=%async_computation.1 | async-start | bytes 786432 | tf_op jit(solution)/shard_map/all_to_all | solution.py:117
  81.2 10.9 %all-to-all-start = ((bf16[4,64,768]{2,1,0:T(8,128)(2,1)}), bf16[4,64,768]{2,1,0:T(8,128)(2,1)S(1)}, u32[]{:S(2)}, u32[]{:S(2)}) async-start(bf16[4,64,768]{2,1,0:T(8,128)(2,1)} %convert_element_type.24), calls=%async_computation | async-start | bytes 786432 | tf_op jit(solution)/shard_map/all_to_all | solution.py:116
where the time goes:
time: 93.5 us; the launch traced here: 92.8 us
  blocking collectives  46.5 us (50%)
  local copies, waits for them, and re-layouts  15.8 us (17%)
  waiting for transfers between devices  12.5 us (13%)
  matrix products  9.84 us (11%)
  starting transfers between devices  6.92 us (7%)
    all_gather x1, blocking collectives, local(): lax.all_gather(key_rows, 'blk', axis=0, tiled=True)  12.8 us
    all_gather x1, blocking collectives, local(): lax.all_gather(key_tangent, 'blk', axis=0, tiled=True)  12.7 us
    unnamed x12, local copies, waits for them, and re-layouts  11.2 us
    all_gather x1, blocking collectives, local(): lax.all_gather(value_rows, 'blk', axis=0, tiled=True)  11.2 us
    all_gather x1, blocking collectives, local(): lax.all_gather(value_tangent, 'blk', axis=0, tiled=True)  9.83 us
    all_to_all x1, waiting for transfers between devices, local(): lax.all_to_all(result_rows, 'head', split_axis=0, concat_axis=1, tiled=True)  6.63 us
    all_to_all x1, waiting for transfers between devices, local(): lax.all_to_all(result_tangent, 'head', split_axis=0, concat_axis=1, tiled...  5.92 us
    dot_general x1, matrix products, score_pair(): jnp.einsum('qhd,khd->qhk', tangent_heads, key_block, preferred_element_ty...  3.5 us
  transfers between devices with their start and end apart: 2, of which 2 were waited for; matrix products, arithmetic and copies ran while one was open for 2% of the time, Pallas kernels for 0%

commit v1 on v0

--- a/solution.py
+++ b/solution.py
@@ -3,6 +3,8 @@
 import jax
 import jax.numpy as jnp
 from jax import lax
+from jax.experimental import pallas as pl
+from jax.experimental.pallas import tpu as pltpu
 from jax.sharding import PartitionSpec as P
 
 HD = 128
@@ -119,9 +121,343 @@
     return (attended, attended_tangent)
 
 
+def _dot(a, b, dims):
+    return lax.dot_general(a, b, (dims, ((), ())), preferred_element_type=jnp.float32)
+
+
+def _nt(a, b):
+    return _dot(a, b, ((1,), (1,)))
+
+
+def _nn(a, b):
+    return _dot(a, b, ((1,), (0,)))
+
+
+def _params(mib=24):
+    return pltpu.CompilerParams(vmem_limit_bytes=mib * 2**20)
+
+
+def _weights(q, dq, k, dk):
+    scaling = HD ** (-0.5)
+    scores = _nt(q, k)
+    change = _nt(jnp.concatenate([dq, q], axis=1), jnp.concatenate([k, dk], axis=1))
+    peak = jnp.max(scores, axis=1, keepdims=True)
+    weights = jnp.exp((scores - peak) * scaling)
+    mixed = weights * (change * scaling)
+    total = jnp.sum(weights, axis=1, keepdims=True)
+    shift = jnp.sum(mixed, axis=1, keepdims=True)
+    return weights.astype(jnp.bfloat16), mixed.astype(jnp.bfloat16), total, shift
+
+
+def _col(head):
+    return pl.ds(pl.multiple_of(head * HD, HD), HD)
+
+
+def pack_whole(arrays, g, which):
+    rows = arrays[0].shape[0]
+    n = len(arrays)
+
+    def kernel(*refs):
+        ins, out, sems = refs[:n], refs[n], refs[n + 1]
+        other = 1 - lax.axis_index("blk")
+        copies = [
+            pltpu.make_async_copy(
+                ins[a].at[:, _col(other * g + which)], out.at[a], sems.at[a]
+            )
+            for a in range(n)
+        ]
+        for c in copies:
+            c.start()
+        for c in copies:
+            c.wait()
+
+    return pl.pallas_call(
+        kernel,
+        out_shape=jax.ShapeDtypeStruct((n, rows, HD), jnp.bfloat16),
+        in_specs=[pl.BlockSpec(memory_space=pl.ANY)] * n,
+        out_specs=pl.BlockSpec(memory_space=pl.ANY),
+        scratch_shapes=[pltpu.SemaphoreType.DMA((n,))],
+        compiler_params=_params(),
+        name="pack_whole",
+    )(*arrays)
+
+
+def pack_shared(arrays, first, count):
+    rows = arrays[0].shape[0]
+    n = len(arrays)
+
+    def kernel(*refs):
+        ins, out, sems = refs[:n], refs[n], refs[n + 1]
+        copies = [
+            pltpu.make_async_copy(
+                ins[a].at[:, pl.ds(first * HD, count * HD)], out.at[a], sems.at[a]
+            )
+            for a in range(n)
+        ]
+        for c in copies:
+            c.start()
+        for c in copies:
+            c.wait()
+
+    return pl.pallas_call(
+        kernel,
+        out_shape=jax.ShapeDtypeStruct((n, rows, count * HD), jnp.bfloat16),
+        in_specs=[pl.BlockSpec(memory_space=pl.ANY)] * n,
+        out_specs=pl.BlockSpec(memory_space=pl.ANY),
+        scratch_shapes=[pltpu.SemaphoreType.DMA((n,))],
+        compiler_params=_params(),
+        name="pack_shared",
+    )(*arrays)
+
+
+def whole_head(own, received, g, which, n_head):
+    rows = own[0].shape[0]
+    piece = rows // n_head
+    n = len(own)
+
+    def kernel(*refs):
+        ins, got, outs = refs[:n], refs[n], refs[n + 1 : n + 1 + n_head]
+        mine, both, sems = refs[n + 1 + n_head :]
+        head = lax.axis_index("blk") * g + which
+        copies = [
+            pltpu.make_async_copy(ins[a].at[:, _col(head)], mine.at[a], sems.at[a])
+            for a in range(n)
+        ]
+        for c in copies:
+            c.start()
+        for c in copies:
+            c.wait()
+        k, dk, v, dv = (
+            jnp.concatenate([mine[a], got[a]], axis=0) for a in (2, 3, 4, 5)
+        )
+        vdv = jnp.concatenate([v, dv], axis=1)
+        for block, source in enumerate((mine, got)):
+            weights, mixed, total, shift = _weights(source[0], source[1], k, dk)
+            plain = _nn(weights, vdv)
+            numerator, extra = plain[:, :HD], plain[:, HD:]
+            inverse = 1.0 / total
+            attended = numerator * inverse
+            tangent = (_nn(mixed, v) + extra) * inverse - (shift * inverse) * attended
+            both[block, :, :HD] = attended.astype(jnp.bfloat16)
+            both[block, :, HD:] = tangent.astype(jnp.bfloat16)
+        me = lax.axis_index("head")
+        for s in range(n_head):
+            at = pl.ds(pl.multiple_of((me ^ s) * piece, piece), piece)
+            for block in range(2):
+                outs[s][block] = both[block, at, :]
+
+    vmem = pl.BlockSpec(memory_space=pltpu.VMEM)
+    return pl.pallas_call(
+        kernel,
+        out_shape=[jax.ShapeDtypeStruct((2, piece, 2 * HD), jnp.bfloat16)] * n_head,
+        in_specs=[pl.BlockSpec(memory_space=pl.ANY)] * n + [vmem],
+        out_specs=[vmem] * n_head,
+        scratch_shapes=[
+            pltpu.VMEM((n, rows, HD), jnp.bfloat16),
+            pltpu.VMEM((2, rows, 2 * HD), jnp.bfloat16),
+            pltpu.SemaphoreType.DMA((n,)),
+        ],
+        compiler_params=_params(),
+        name="whole_head",
+    )(*own, received)
+
+
+def shared_first(own, received, first, count):
+    rows = own[0].shape[0]
+    n = len(own)
+    width = count * HD
+
+    def kernel(*refs):
+        ins, got = refs[:n], refs[n]
+        att, base, inv, far = refs[n + 1 : n + 5]
+        mine, sems = refs[n + 5 :]
+        copies = [
+            pltpu.make_async_copy(
+                ins[a].at[:, pl.ds(first * HD, width)], mine.at[a], sems.at[a]
+            )
+            for a in range(n)
+        ]
+        for c in copies:
+            c.start()
+        for c in copies:
+            c.wait()
+        for i in range(count):
+            cols = slice(i * HD, (i + 1) * HD)
+            q, dq, dv = mine[0, :, cols], mine[1, :, cols], mine[5, :, cols]
+            k, dk, v = (
+                jnp.concatenate([mine[2 + a, :, cols], got[a, :, cols]], axis=0)
+                for a in range(3)
+            )
+            weights, mixed, total, shift = _weights(q, dq, k, dk)
+            inverse = 1.0 / total
+            attended = _nn(weights, v) * inverse
+            tangent = _nn(mixed, v) + _nn(weights[:, :rows], dv)
+            att[:, cols] = attended.astype(jnp.bfloat16)
+            base[:, cols] = tangent * inverse - (shift * inverse) * attended
+            inv[:, cols] = jnp.broadcast_to(inverse, (rows, HD))
+            far[i] = weights[:, rows:]
+
+    vmem = pl.BlockSpec(memory_space=pltpu.VMEM)
+    return pl.pallas_call(
+        kernel,
+        out_shape=[
+            jax.ShapeDtypeStruct((rows, width), jnp.bfloat16),
+            jax.ShapeDtypeStruct((rows, width), jnp.float32),
+            jax.ShapeDtypeStruct((rows, width), jnp.float32),
+            jax.ShapeDtypeStruct((count, rows, rows), jnp.bfloat16),
+        ],
+        in_specs=[pl.BlockSpec(memory_space=pl.ANY)] * n + [vmem],
+        out_specs=[vmem] * 4,
+        scratch_shapes=[
+            pltpu.VMEM((n, rows, width), jnp.bfloat16),
+            pltpu.SemaphoreType.DMA((n,)),
+        ],
+        compiler_params=_params(),
+        name="shared_first",
+    )(*own, received)
+
+
+def shared_last(parts, received, count, n_head):
+    att, base, inv, far = parts
+    rows, width = att.shape
+    piece = rows // n_head
+
+    def kernel(att, base, inv, far, got, *rest):
+        outs, both = rest[:n_head], rest[n_head]
+        both[:, :width] = att[...]
+        for i in range(count):
+            cols = slice(i * HD, (i + 1) * HD)
+            tangent = base[:, cols] + _nn(far[i], got[0, :, cols]) * inv[:, cols]
+            both[:, width + i * HD : width + (i + 1) * HD] = tangent.astype(jnp.bfloat16)
+        me = lax.axis_index("head")
+        for s in range(n_head):
+            at = pl.ds(pl.multiple_of((me ^ s) * piece, piece), piece)
+            outs[s][...] = both[at, :]
+
+    vmem = pl.BlockSpec(memory_space=pltpu.VMEM)
+    return pl.pallas_call(
+        kernel,
+        out_shape=[jax.ShapeDtypeStruct((piece, 2 * width), jnp.bfloat16)] * n_head,
+        in_specs=[vmem] * 5,
+        out_specs=[vmem] * n_head,
+        scratch_shapes=[pltpu.VMEM((rows, 2 * width), jnp.bfloat16)],
+        compiler_params=_params(),
+        name="shared_last",
+    )(att, base, inv, far, received)
+
+
+def gather_far(pieces, g, n_head):
+    piece = pieces[0][0].shape[1]
+    flat = [p for per_head in pieces for p in per_head]
+
+    def kernel(*refs):
+        ins, out, sems = refs[:-2], refs[-2], refs[-1]
+        copies = [
+            pltpu.make_async_copy(
+                ref.at[1], out.at[at // n_head, at % n_head], sems.at[at]
+            )
+            for at, ref in enumerate(ins)
+        ]
+        for c in copies:
+            c.start()
+        for c in copies:
+            c.wait()
+
+    return pl.pallas_call(
+        kernel,
+        out_shape=jax.ShapeDtypeStruct((g, n_head, piece, 2 * HD), jnp.bfloat16),
+        in_specs=[pl.BlockSpec(memory_space=pl.ANY)] * len(flat),
+        out_specs=pl.BlockSpec(memory_space=pl.ANY),
+        scratch_shapes=[pltpu.SemaphoreType.DMA((len(flat),))],
+        compiler_params=_params(),
+        name="gather_far",
+    )(*flat)
+
+
+def assemble(pieces, crossed, shared, g, heads, n_head):
+    piece = pieces[0][0].shape[1]
+    flat = [p for per_head in pieces for p in per_head]
+    n_flat, width = len(flat), g * HD
+    total_width = n_head * heads * HD
+
+    def kernel(*refs):
+        near, far = refs[:n_flat], refs[n_flat]
+        ours = refs[n_flat + 1 : n_flat + 1 + n_head]
+        outs = refs[n_flat + 1 + n_head : n_flat + 3 + n_head]
+        sems = refs[-1]
+        me, blk = lax.axis_index("head"), lax.axis_index("blk")
+        copies = []
+
+        def put(source, out, column, size):
+            at = pl.ds(pl.multiple_of(column * HD, HD), size)
+            copies.append(
+                pltpu.make_async_copy(source, out.at[:, at], sems.at[len(copies)])
+            )
+
+        for s in range(n_head):
+            start = (me ^ s) * heads
+            for o in range(2):
+                for i in range(g):
+                    lanes = pl.ds(o * HD, HD)
+                    put(near[i * n_head + s].at[0, :, lanes], outs[o], start + blk * g + i, HD)
+                    put(far.at[i, s, :, lanes], outs[o], start + (1 - blk) * g + i, HD)
+                put(ours[s].at[:, pl.ds(o * width, width)], outs[o], start + 2 * g, width)
+        for c in copies:
+            c.start()
+        for c in copies:
+            c.wait()
+
+    n_copies = n_head * 2 * (2 * g + 1)
+    return pl.pallas_call(
+        kernel,
+        out_shape=[jax.ShapeDtypeStruct((piece, total_width), jnp.bfloat16)] * 2,
+        in_specs=[pl.BlockSpec(memory_space=pl.ANY)] * (n_flat + 1 + n_head),
+        out_specs=[pl.BlockSpec(memory_space=pl.ANY)] * 2,
+        scratch_shapes=[pltpu.SemaphoreType.DMA((n_copies,))],
+        compiler_params=_params(),
+        name="assemble",
+    )(*flat, crossed, *shared)
+
+
+def paired(n_head, query_rows, key_rows, value_rows, query_tangent, key_tangent, value_tangent):
+    heads = query_rows.shape[1] // HD
+    g = heads // 3
+    own = (query_rows, query_tangent, key_rows, key_tangent, value_rows, value_tangent)
+
+    def cross(x):
+        return lax.ppermute(x, "blk", [(0, 1), (1, 0)])
+
+    def along(x, s):
+        return lax.ppermute(x, "head", [(i, i ^ s) for i in range(n_head)])
+
+    def spread(parts):
+        return [parts[0]] + [along(parts[s], s) for s in range(1, n_head)]
+
+    whole_in = [cross(pack_whole(own, g, i)) for i in range(g)]
+    shared_in = cross(pack_shared(own[2:5], 2 * g, g))
+    last_in = cross(pack_shared(own[5:], 2 * g, g))
+    pieces = [spread(whole_head(own, whole_in[i], g, i, n_head)) for i in range(g)]
+    far = gather_far(pieces, g, n_head)
+    far, shared_in = lax.optimization_barrier((far, shared_in))
+    crossed = cross(far)
+    parts = shared_first(own, shared_in, 2 * g, g)
+    shared = spread(shared_last(parts, last_in, g, n_head))
+    return assemble(pieces, crossed, shared, g, heads, n_head)
+
+
 def solution(mesh):
+    n_head = mesh.shape["head"]
+
+    def one_device(*arrays):
+        heads = arrays[0].shape[1] // HD
+        rows = arrays[0].shape[0]
+        two = mesh.shape["blk"] == 2 and n_head & (n_head - 1) == 0
+        if two and heads % 3 == 0 and rows % (16 * n_head) == 0:
+            return paired(n_head, *arrays)
+        return local(*arrays)
+
     return jax.shard_map(
-        local,
+        one_device,
         mesh=mesh,
         in_specs=(
             P(("batch", "blk"), "head"),

time: 93.5 us -> 55 us (0.59)
  blocking collectives: 46.5 us -> 0 us
  waiting for transfers between devices: 12.5 us -> 28.2 us
  matrix products: 9.84 us -> 0 us
  local copies, waits for them, and re-layouts: 15.8 us -> 5.99 us
  starting transfers between devices: 6.92 us -> 13.9 us
  Pallas kernels: 0 us -> 5.81 us
    all_gather x4 -> x0, blocking collectives: 46.5 us -> none  [the longest x1 12.8 us: local(): lax.all_gather(key_rows, 'blk', axis=0, tiled=True)]
    ppermute x0 -> x14, waiting for transfers between devices: none -> 28.2 us  [the longest x5 20.4 us: cross(): return lax.ppermute(x, 'blk', [(0, 1), (1, 0)])]
    ppermute x0 -> x14, starting transfers between devices: none -> 13.9 us  [the longest x5 7.31 us: cross(): return lax.ppermute(x, 'blk', [(0, 1), (1, 0)])]
    all_to_all x2 -> x0, waiting for transfers between devices: 12.5 us -> none  [the longest x1 6.63 us: local(): lax.all_to_all(result_rows, 'head', split_axis=0, concat_axis=1, tiled=True)]
    dot_general x6 -> x0, matrix products: 9.84 us -> none  [the longest x1 3.5 us: score_pair(): jnp.einsum('qhd,khd->qhk', tangent_heads, key_block, preferred_element_ty...]
    all_to_all x2 -> x0, starting transfers between devices: 6.92 us -> none  [the longest x1 3.46 us: local(): lax.all_to_all(result_rows, 'head', split_axis=0, concat_axis=1, tiled=True)]
    pallas_call x0 -> x10, Pallas kernels: none -> 5.81 us  [the longest x2 2.31 us: whole_head(): pl.pallas_call(kernel, out_shape=[jax.ShapeDtypeStruct((2, piece, 2 * HD)...]
    unnamed x12 -> x20, local copies, waits for them, and re-layouts: 11.2 us -> 5.99 us
  transfers between devices with their start and end apart: 2 -> 14, of which waited for: 2 -> 7; matrix products, arithmetic and copies ran while one was open for 2% -> 0% of each run, Pallas kernels for 0% -> 8%
where the time goes in v1:
time: 55 us; the launch traced here: 54.7 us
  waiting for transfers between devices  28.2 us (51%)
  starting transfers between devices  13.9 us (25%)
  local copies, waits for them, and re-layouts  5.99 us (11%)
  Pallas kernels  5.81 us (11%)
  between operations  0.79 us (1%)
    ppermute x5, waiting for transfers between devices, cross(): return lax.ppermute(x, 'blk', [(0, 1), (1, 0)])  20.4 us
    ppermute x9, waiting for transfers between devices, along(): return lax.ppermute(x, 'head', [(i, i ^ s) for i in range(n_head)])  7.83 us
    ppermute x5, starting transfers between devices, cross(): return lax.ppermute(x, 'blk', [(0, 1), (1, 0)])  7.31 us
    ppermute x9, starting transfers between devices, along(): return lax.ppermute(x, 'head', [(i, i ^ s) for i in range(n_head)])  6.57 us
    unnamed x20, local copies, waits for them, and re-layouts  5.99 us
    pallas_call x2, Pallas kernels, whole_head(): pl.pallas_call(kernel, out_shape=[jax.ShapeDtypeStruct((2, piece, 2 * HD)...  2.31 us
    pallas_call x1, Pallas kernels, shared_first(): pl.pallas_call(kernel, out_shape=[jax.ShapeDtypeStruct((rows, width), jnp...  1.29 us
    pallas_call x1, Pallas kernels, assemble(): pl.pallas_call(kernel, out_shape=[jax.ShapeDtypeStruct((piece, total_widt...  1.21 us
  transfers between devices with their start and end apart: 14, of which 7 were waited for; matrix products, arithmetic and copies ran while one was open for 0% of the time, Pallas kernels for 8%

profile of v1, /device:TPU:0, one launch (start us, length us, event | category | flops | bytes accessed | tf_op | source)
XLA Modules:
  0.0 54.7 jit_solution(6611413860037902459)
XLA Ops:
  0.6 0.0 copy-start
  0.6 1.0 %copy-done = bf16[256,768]{1,0:T(8,128)(2,1)S(1)} copy-done((bf16[256,768]{1,0:T(8,128)(2,1)S(1)}, bf16[256,768]{1,0:T(8,128)(2,1)}, u32[]{:S(2)}) %copy-start) | copy-done | bytes 393240
  1.6 1.0 %copy-done.2 = bf16[256,768]{1,0:T(8,128)(2,1)S(1)} copy-done((bf16[256,768]{1,0:T(8,128)(2,1)S(1)}, bf16[256,768]{1,0:T(8,128)(2,1)}, u32[]{:S(2)}) %copy-start.2) | copy-done | bytes 393240
  2.6 1.0 %copy-done.4 = bf16[256,768]{1,0:T(8,128)(2,1)S(1)} copy-done((bf16[256,768]{1,0:T(8,128)(2,1)S(1)}, bf16[256,768]{1,0:T(8,128)(2,1)}, u32[]{:S(2)}) %copy-start.4) | copy-done | bytes 393240
  3.6 1.0 %copy-done.5 = bf16[256,768]{1,0:T(8,128)(2,1)S(1)} copy-done((bf16[256,768]{1,0:T(8,128)(2,1)S(1)}, bf16[256,768]{1,0:T(8,128)(2,1)}, u32[]{:S(2)}) %copy-start.5) | copy-done | bytes 393240
  4.6 1.0 %copy-done.6 = bf16[256,768]{1,0:T(8,128)(2,1)S(1)} copy-done((bf16[256,768]{1,0:T(8,128)(2,1)S(1)}, bf16[256,768]{1,0:T(8,128)(2,1)}, u32[]{:S(2)}) %copy-start.6) | copy-done | bytes 393240
  5.6 1.0 %copy-done.8 = bf16[256,768]{1,0:T(8,128)(2,1)S(1)} copy-done((bf16[256,768]{1,0:T(8,128)(2,1)S(1)}, bf16[256,768]{1,0:T(8,128)(2,1)}, u32[]{:S(2)}) %copy-start.8) | copy-done | bytes 393240
  6.6 0.1 pack_whole.2
  6.8 0.0 copy-start.1
  6.8 0.0 copy-start.3
  6.8 3.0 %collective-permute-start = (bf16[6,256,128]{2,1,0:T(8,128)(2,1)S(1)}, bf16[6,256,128]{2,1,0:T(8,128)(2,1)S(1)}, u32[]{:S(2)}, u32[]{:S(2)}) collective-permute-start(bf16[6,256,128]{2,1,0:T(8,128)(2,1)S(1)} %pack_whole.2), channel_id=1, source_target_pairs={{0,16},{16,0},{1,17},{17,1},{2,18},{18,2},{3,19},{19,3},{4,20},{20... | collective-permute-start | bytes 1179656 | tf_op jit(solution)/shard_map/ppermute | solution.py:428
  9.8 0.1 pack_whole.3
  9.9 0.1 collective-permute-start.4
  10.0 0.1 pack_shared.2
  10.1 2.1 %collective-permute-start.8 = (bf16[3,256,256]{2,1,0:T(8,128)(2,1)S(1)}, bf16[3,256,256]{2,1,0:T(8,128)(2,1)S(1)}, u32[]{:S(2)}, u32[]{:S(2)}) collective-permute-start(bf16[3,256,256]{2,1,0:T(8,128)(2,1)S(1)} %pack_shared.2), channel_id=1, source_target_pairs={{0,16},{16,0},{1,17},{17,1},{2,18},{18,2},{3,19},{19,3},{4,20},{20... | collective-permute-start | bytes 1179656 | tf_op jit(solution)/shard_map/ppermute | solution.py:428
  12.2 7.6 %collective-permute-done.refs_6_ = bf16[6,256,128]{2,1,0:T(8,128)(2,1)S(1)} collective-permute-done((bf16[6,256,128]{2,1,0:T(8,128)(2,1)S(1)}, bf16[6,256,128]{2,1,0:T(8,128)(2,1)S(1)}, u32[]{:S(2)}, u32[]{:S(2)}) %collective-permute-start) | collective-permute-done | bytes 393248 | tf_op jit(solution)/shard_map/ppermute | solution.py:428
  19.7 1.2 %whole_head.2 = (bf16[2,64,256]{2,1,0:T(8,128)(2,1)S(1)}, bf16[2,64,256]{2,1,0:T(8,128)(2,1)S(1)}, bf16[2,64,256]{2,1,0:T(8,128)(2,1)S(1)}, bf16[2,64,256]{2,1,0:T(8,128)(2,1)S(1)}) custom-call(bf16[256,768]{1,0:T(8,128)(2,1)S(1)} %copy-done.6, bf16[256,768]{1,0:T(8,128)(2,1)S(1)} %copy-done.8, bf16[256,768]{1,0:T(8,128)(2,1)S(1)} %copy-done.1, ...), custom_call_target="tpu_custom_call" | custom-call | tf_op jit(solution)/shard_map/whole_head/pallas_call | solution.py:250
  20.9 0.1 collective-permute-start.1
  21.0 2.1 %collective-permute-start.2 = (bf16[2,64,256]{2,1,0:T(8,128)(2,1)S(1)}, bf16[2,64,256]{2,1,0:T(8,128)(2,1)S(1)}, u32[]{:S(2)}, u32[]{:S(2)}) collective-permute-start(bf16[2,64,256]{2,1,0:T(8,128)(2,1)S(1)} %get-tuple-element.22), channel_id=1, source_target_pairs={{0,8},{4,12},{8,0},{12,4},{1,9},{5,13},{9,1},{13,5},{2,10},{6,14},... | collective-permute-start | bytes 196616 | tf_op jit(solution)/shard_map/ppermute | solution.py:431
  23.1 0.1 collective-permute-start.3
  23.2 5.0 %collective-permute-done.4.refs_6_ = bf16[6,256,128]{2,1,0:T(8,128)(2,1)S(1)} collective-permute-done((bf16[6,256,128]{2,1,0:T(8,128)(2,1)S(1)}, bf16[6,256,128]{2,1,0:T(8,128)(2,1)S(1)}, u32[]{:S(2)}, u32[]{:S(2)}) %collective-permute-start.4) | collective-permute-done | bytes 393248 | tf_op jit(solution)/shard_map/ppermute | solution.py:428
  28.2 1.2 %whole_head.3 = (bf16[2,64,256]{2,1,0:T(8,128)(2,1)S(1)}, bf16[2,64,256]{2,1,0:T(8,128)(2,1)S(1)}, bf16[2,64,256]{2,1,0:T(8,128)(2,1)S(1)}, bf16[2,64,256]{2,1,0:T(8,128)(2,1)S(1)}) custom-call(bf16[256,768]{1,0:T(8,128)(2,1)S(1)} %copy-done.6, bf16[256,768]{1,0:T(8,128)(2,1)S(1)} %copy-done.8, bf16[256,768]{1,0:T(8,128)(2,1)S(1)} %copy-done.1, ...), custom_call_target="tpu_custom_call" | custom-call | tf_op jit(solution)/shard_map/whole_head/pallas_call | solution.py:250
  29.3 0.1 collective-permute-start.5
  29.4 0.0 collective-permute-done.1.refs_1_
  29.4 2.2 %collective-permute-start.6 = (bf16[2,64,256]{2,1,0:T(8,128)(2,1)S(1)}, bf16[2,64,256]{2,1,0:T(8,128)(2,1)S(1)}, u32[]{:S(2)}, u32[]{:S(2)}) collective-permute-start(bf16[2,64,256]{2,1,0:T(8,128)(2,1)S(1)} %get-tuple-element.26), channel_id=1, source_target_pairs={{0,8},{4,12},{8,0},{12,4},{1,9},{5,13},{9,1},{13,5},{2,10},{6,14},... | collective-permute-start | bytes 196616 | tf_op jit(solution)/shard_map/ppermute | solution.py:431
  31.6 0.0 collective-permute-done.2.refs_2_
  31.6 0.1 collective-permute-start.7
  31.7 0.0 collective-permute-done.3.refs_3_
  31.7 0.0 collective-permute-done.5.refs_5_
  31.7 2.5 %collective-permute-done.6.refs_6_ = bf16[2,64,256]{2,1,0:T(8,128)(2,1)S(1)} collective-permute-done((bf16[2,64,256]{2,1,0:T(8,128)(2,1)S(1)}, bf16[2,64,256]{2,1,0:T(8,128)(2,1)S(1)}, u32[]{:S(2)}, u32[]{:S(2)}) %collective-permute-start.6) | collective-permute-done | bytes 65568 | tf_op jit(solution)/shard_map/ppermute | solution.py:431
  34.2 1.4 %collective-permute-done.7.refs_7_ = bf16[2,64,256]{2,1,0:T(8,128)(2,1)S(1)} collective-permute-done((bf16[2,64,256]{2,1,0:T(8,128)(2,1)S(1)}, bf16[2,64,256]{2,1,0:T(8,128)(2,1)S(1)}, u32[]{:S(2)}, u32[]{:S(2)}) %collective-permute-start.7) | collective-permute-done | bytes 65568 | tf_op jit(solution)/shard_map/ppermute | solution.py:431
  35.6 0.4 gather_far.1
  36.0 0.0 copy-start.7
  36.0 0.0 collective-permute-done.8.refs_6_
  36.1 1.6 %collective-permute-start.9 = (bf16[2,4,64,256]{3,2,1,0:T(8,128)(2,1)S(1)}, bf16[2,4,64,256]{3,2,1,0:T(8,128)(2,1)S(1)}, u32[]{:S(2)}, u32[]{:S(2)}) collective-permute-start(bf16[2,4,64,256]{3,2,1,0:T(8,128)(2,1)S(1)} %gather_far.1), channel_id=1, source_target_pairs={{0,16},{16,0},{1,17},{17,1},{2,18},{18,2},{3,19},{19,3},{4,20},{20... | collective-permute-start | bytes 786440 | tf_op jit(solution)/shard_map/ppermute | solution.py:428
  37.6 0.6 %collective-permute-start.10 = (bf16[1,256,256]{2,1,0:T(8,128)(2,1)S(1)}, bf16[1,256,256]{2,1,0:T(8,128)(2,1)S(1)}, u32[]{:S(2)}, u32[]{:S(2)}) collective-permute-start(bf16[1,256,256]{2,1,0:T(8,128)(2,1)S(1)} %pack_shared.3), channel_id=1, source_target_pairs={{0,16},{16,0},{1,17},{17,1},{2,18},{18,2},{3,19},{19,3},{4,20},{20... | collective-permute-start | bytes 393224 | tf_op jit(solution)/shard_map/ppermute | solution.py:428
  38.2 0.0 copy-done.9
  38.2 1.3 %shared_first.1 = (bf16[256,256]{1,0:T(8,128)(2,1)S(1)}, f32[256,256]{1,0:T(8,128)S(1)}, f32[256,256]{1,0:T(8,128)S(1)}, bf16[2,256,256]{2,1,0:T(8,128)(2,1)S(1)}) custom-call(bf16[256,768]{1,0:T(8,128)(2,1)S(1)} %copy-done.7, bf16[256,768]{1,0:T(8,128)(2,1)S(1)} %copy-done.9, bf16[256,768]{1,0:T(8,128)(2,1)S(1)} %copy-done.1, ...), custom_call_target="tpu_custom_call" | custom-call | tf_op jit(solution)/shard_map/shared_first/pallas_call | solution.py:301
  39.5 7.8 %collective-permute-done.10.got = bf16[1,256,256]{2,1,0:T(8,128)(2,1)S(1)} collective-permute-done((bf16[1,256,256]{2,1,0:T(8,128)(2,1)S(1)}, bf16[1,256,256]{2,1,0:T(8,128)(2,1)S(1)}, u32[]{:S(2)}, u32[]{:S(2)}) %collective-permute-start.10) | collective-permute-done | bytes 131104 | tf_op jit(solution)/shard_map/ppermute | solution.py:428
  47.4 0.2 shared_last.1
  47.6 0.1 collective-permute-start.11
  47.7 1.7 %collective-permute-start.12 = (bf16[64,512]{1,0:T(8,128)(2,1)S(1)}, bf16[64,512]{1,0:T(8,128)(2,1)S(1)}, u32[]{:S(2)}, u32[]{:S(2)}) collective-permute-start(bf16[64,512]{1,0:T(8,128)(2,1)S(1)} %get-tuple-element.36), channel_id=1, source_target_pairs={{0,8},{4,12},{8,0},{12,4},{1,9},{5,13},{9,1},{13,5},{2,10},{6,14},... | collective-permute-start | bytes 196616 | tf_op jit(solution)/shard_map/ppermute | solution.py:431
  49.4 0.2 collective-permute-start.13
  49.6 0.0 collective-permute-done.11.refs_10_
  49.6 2.6 %collective-permute-done.12.refs_11_ = bf16[64,512]{1,0:T(8,128)(2,1)S(1)} collective-permute-done((bf16[64,512]{1,0:T(8,128)(2,1)S(1)}, bf16[64,512]{1,0:T(8,128)(2,1)S(1)}, u32[]{:S(2)}, u32[]{:S(2)}) %collective-permute-start.12) | collective-permute-done | bytes 65568 | tf_op jit(solution)/shard_map/ppermute | solution.py:431
  52.2 1.2 %collective-permute-done.13.refs_12_ = bf16[64,512]{1,0:T(8,128)(2,1)S(1)} collective-permute-done((bf16[64,512]{1,0:T(8,128)(2,1)S(1)}, bf16[64,512]{1,0:T(8,128)(2,1)S(1)}, u32[]{:S(2)}, u32[]{:S(2)}) %collective-permute-start.13) | collective-permute-done | bytes 65568 | tf_op jit(solution)/shard_map/ppermute | solution.py:431
  53.5 0.0 collective-permute-done.9.refs_8_
  53.5 1.2 %assemble.1 = (bf16[64,3072]{1,0:T(8,128)(2,1)}, bf16[64,3072]{1,0:T(8,128)(2,1)}) custom-call(bf16[2,64,256]{2,1,0:T(8,128)(2,1)S(1)} %get-tuple-element.20.refs_0_, bf16[2,64,256]{2,1,0:T(8,128)(2,1)S(1)} %collective-permute-done.1.refs_1_, bf16[2,64,256]{2,1,0:T(8,128)(2,1)S(1)} %collective-permute-done.2.refs_2_, ...), custom_call_target="tpu_custom_call" | custom-call | tf_op jit(solution)/shard_map/assemble/pallas_call | solution.py:411
  (10 shorter events, 0.0 us)
Async XLA Ops:
  0.6 1.0 %copy-start = (bf16[256,768]{1,0:T(8,128)(2,1)S(1)}, bf16[256,768]{1,0:T(8,128)(2,1)}, u32[]{:S(2)}) copy-start(bf16[256,768]{1,0:T(8,128)(2,1)} %refs_2_.11) | copy-start | bytes 1179652
  1.6 1.0 %copy-start.2 = (bf16[256,768]{1,0:T(8,128)(2,1)S(1)}, bf16[256,768]{1,0:T(8,128)(2,1)}, u32[]{:S(2)}) copy-start(bf16[256,768]{1,0:T(8,128)(2,1)} %refs_3_.9) | copy-start | bytes 1179652
  2.6 1.0 %copy-start.4 = (bf16[256,768]{1,0:T(8,128)(2,1)S(1)}, bf16[256,768]{1,0:T(8,128)(2,1)}, u32[]{:S(2)}) copy-start(bf16[256,768]{1,0:T(8,128)(2,1)} %refs_4_.9) | copy-start | bytes 1179652
  3.6 1.0 %copy-start.5 = (bf16[256,768]{1,0:T(8,128)(2,1)S(1)}, bf16[256,768]{1,0:T(8,128)(2,1)}, u32[]{:S(2)}) copy-start(bf16[256,768]{1,0:T(8,128)(2,1)} %refs_0_.13) | copy-start | bytes 1179652
  4.6 1.0 %copy-start.6 = (bf16[256,768]{1,0:T(8,128)(2,1)S(1)}, bf16[256,768]{1,0:T(8,128)(2,1)}, u32[]{:S(2)}) copy-start(bf16[256,768]{1,0:T(8,128)(2,1)} %refs_0_.12) | copy-start | bytes 1179652
  5.6 1.0 %copy-start.8 = (bf16[256,768]{1,0:T(8,128)(2,1)S(1)}, bf16[256,768]{1,0:T(8,128)(2,1)}, u32[]{:S(2)}) copy-start(bf16[256,768]{1,0:T(8,128)(2,1)} %refs_1_.11) | copy-start | bytes 1179652
  6.8 3.3 %copy-start.1 = (bf16[256,768]{1,0:T(8,128)(2,1)S(1)}, bf16[256,768]{1,0:T(8,128)(2,1)}, u32[]{:S(2)}) copy-start(bf16[256,768]{1,0:T(8,128)(2,1)} %refs_2_.11) | copy-start | bytes 1179652
  6.8 3.3 %copy-start.3 = (bf16[256,768]{1,0:T(8,128)(2,1)S(1)}, bf16[256,768]{1,0:T(8,128)(2,1)}, u32[]{:S(2)}) copy-start(bf16[256,768]{1,0:T(8,128)(2,1)} %refs_3_.9) | copy-start | bytes 1179652
  6.8 12.9 %collective-permute-start = (bf16[6,256,128]{2,1,0:T(8,128)(2,1)S(1)}, bf16[6,256,128]{2,1,0:T(8,128)(2,1)S(1)}, u32[]{:S(2)}, u32[]{:S(2)}) collective-permute-start(bf16[6,256,128]{2,1,0:T(8,128)(2,1)S(1)} %pack_whole.2), channel_id=1, source_target_pairs={{0,16},{16,0},{1,17},{17,1},{2,18},{18,2},{3,19},{19,3},{4,20},{20... | collective-permute-start | bytes 1179656 | tf_op jit(solution)/shard_map/ppermute | solution.py:428
  9.9 18.2 %collective-permute-start.4 = (bf16[6,256,128]{2,1,0:T(8,128)(2,1)S(1)}, bf16[6,256,128]{2,1,0:T(8,128)(2,1)S(1)}, u32[]{:S(2)}, u32[]{:S(2)}) collective-permute-start(bf16[6,256,128]{2,1,0:T(8,128)(2,1)S(1)} %pack_whole.3), channel_id=1, source_target_pairs={{0,16},{16,0},{1,17},{17,1},{2,18},{18,2},{3,19},{19,3},{4,20},{20... | collective-permute-start | bytes 1179656 | tf_op jit(solution)/shard_map/ppermute | solution.py:428
  10.1 25.9 %collective-permute-start.8 = (bf16[3,256,256]{2,1,0:T(8,128)(2,1)S(1)}, bf16[3,256,256]{2,1,0:T(8,128)(2,1)S(1)}, u32[]{:S(2)}, u32[]{:S(2)}) collective-permute-start(bf16[3,256,256]{2,1,0:T(8,128)(2,1)S(1)} %pack_shared.2), channel_id=1, source_target_pairs={{0,16},{16,0},{1,17},{17,1},{2,18},{18,2},{3,19},{19,3},{4,20},{20... | collective-permute-start | bytes 1179656 | tf_op jit(solution)/shard_map/ppermute | solution.py:428
  20.9 8.5 %collective-permute-start.1 = (bf16[2,64,256]{2,1,0:T(8,128)(2,1)S(1)}, bf16[2,64,256]{2,1,0:T(8,128)(2,1)S(1)}, u32[]{:S(2)}, u32[]{:S(2)}) collective-permute-start(bf16[2,64,256]{2,1,0:T(8,128)(2,1)S(1)} %get-tuple-element.21), channel_id=1, source_target_pairs={{0,4},{4,0},{8,12},{12,8},{1,5},{5,1},{9,13},{13,9},{2,6},{6,2},{1... | collective-permute-start | bytes 196616 | tf_op jit(solution)/shard_map/ppermute | solution.py:431
  21.0 10.6 %collective-permute-start.2 = (bf16[2,64,256]{2,1,0:T(8,128)(2,1)S(1)}, bf16[2,64,256]{2,1,0:T(8,128)(2,1)S(1)}, u32[]{:S(2)}, u32[]{:S(2)}) collective-permute-start(bf16[2,64,256]{2,1,0:T(8,128)(2,1)S(1)} %get-tuple-element.22), channel_id=1, source_target_pairs={{0,8},{4,12},{8,0},{12,4},{1,9},{5,13},{9,1},{13,5},{2,10},{6,14},... | collective-permute-start | bytes 196616 | tf_op jit(solution)/shard_map/ppermute | solution.py:431
  23.1 8.6 %collective-permute-start.3 = (bf16[2,64,256]{2,1,0:T(8,128)(2,1)S(1)}, bf16[2,64,256]{2,1,0:T(8,128)(2,1)S(1)}, u32[]{:S(2)}, u32[]{:S(2)}) collective-permute-start(bf16[2,64,256]{2,1,0:T(8,128)(2,1)S(1)} %get-tuple-element.23), channel_id=1, source_target_pairs={{0,12},{4,8},{8,4},{12,0},{1,13},{5,9},{9,5},{13,1},{2,14},{6,10},... | collective-permute-start | bytes 196616 | tf_op jit(solution)/shard_map/ppermute | solution.py:431
  29.3 2.4 %collective-permute-start.5 = (bf16[2,64,256]{2,1,0:T(8,128)(2,1)S(1)}, bf16[2,64,256]{2,1,0:T(8,128)(2,1)S(1)}, u32[]{:S(2)}, u32[]{:S(2)}) collective-permute-start(bf16[2,64,256]{2,1,0:T(8,128)(2,1)S(1)} %get-tuple-element.25), channel_id=1, source_target_pairs={{0,4},{4,0},{8,12},{12,8},{1,5},{5,1},{9,13},{13,9},{2,6},{6,2},{1... | collective-permute-start | bytes 196616 | tf_op jit(solution)/shard_map/ppermute | solution.py:431
  29.4 4.8 %collective-permute-start.6 = (bf16[2,64,256]{2,1,0:T(8,128)(2,1)S(1)}, bf16[2,64,256]{2,1,0:T(8,128)(2,1)S(1)}, u32[]{:S(2)}, u32[]{:S(2)}) collective-permute-start(bf16[2,64,256]{2,1,0:T(8,128)(2,1)S(1)} %get-tuple-element.26), channel_id=1, source_target_pairs={{0,8},{4,12},{8,0},{12,4},{1,9},{5,13},{9,1},{13,5},{2,10},{6,14},... | collective-permute-start | bytes 196616 | tf_op jit(solution)/shard_map/ppermute | solution.py:431
  31.6 4.1 %collective-permute-start.7 = (bf16[2,64,256]{2,1,0:T(8,128)(2,1)S(1)}, bf16[2,64,256]{2,1,0:T(8,128)(2,1)S(1)}, u32[]{:S(2)}, u32[]{:S(2)}) collective-permute-start(bf16[2,64,256]{2,1,0:T(8,128)(2,1)S(1)} %get-tuple-element.27), channel_id=1, source_target_pairs={{0,12},{4,8},{8,4},{12,0},{1,13},{5,9},{9,5},{13,1},{2,14},{6,10},... | collective-permute-start | bytes 196616 | tf_op jit(solution)/shard_map/ppermute | solution.py:431
  35.6 2.6 %copy-start.9 = (bf16[256,768]{1,0:T(8,128)(2,1)S(1)}, bf16[256,768]{1,0:T(8,128)(2,1)}, u32[]{:S(2)}) copy-start(bf16[256,768]{1,0:T(8,128)(2,1)} %refs_1_.11) | copy-start | bytes 1179652
  36.0 2.2 %copy-start.7 = (bf16[256,768]{1,0:T(8,128)(2,1)S(1)}, bf16[256,768]{1,0:T(8,128)(2,1)}, u32[]{:S(2)}) copy-start(bf16[256,768]{1,0:T(8,128)(2,1)} %refs_0_.12) | copy-start | bytes 1179652
  36.1 17.4 %collective-permute-start.9 = (bf16[2,4,64,256]{3,2,1,0:T(8,128)(2,1)S(1)}, bf16[2,4,64,256]{3,2,1,0:T(8,128)(2,1)S(1)}, u32[]{:S(2)}, u32[]{:S(2)}) collective-permute-start(bf16[2,4,64,256]{3,2,1,0:T(8,128)(2,1)S(1)} %gather_far.1), channel_id=1, source_target_pairs={{0,16},{16,0},{1,17},{17,1},{2,18},{18,2},{3,19},{19,3},{4,20},{20... | collective-permute-start | bytes 786440 | tf_op jit(solution)/shard_map/ppermute | solution.py:428
  37.6 9.8 %collective-permute-start.10 = (bf16[1,256,256]{2,1,0:T(8,128)(2,1)S(1)}, bf16[1,256,256]{2,1,0:T(8,128)(2,1)S(1)}, u32[]{:S(2)}, u32[]{:S(2)}) collective-permute-start(bf16[1,256,256]{2,1,0:T(8,128)(2,1)S(1)} %pack_shared.3), channel_id=1, source_target_pairs={{0,16},{16,0},{1,17},{17,1},{2,18},{18,2},{3,19},{19,3},{4,20},{20... | collective-permute-start | bytes 393224 | tf_op jit(solution)/shard_map/ppermute | solution.py:428
  47.6 1.9 %collective-permute-start.11 = (bf16[64,512]{1,0:T(8,128)(2,1)S(1)}, bf16[64,512]{1,0:T(8,128)(2,1)S(1)}, u32[]{:S(2)}, u32[]{:S(2)}) collective-permute-start(bf16[64,512]{1,0:T(8,128)(2,1)S(1)} %get-tuple-element.35), channel_id=1, source_target_pairs={{0,4},{4,0},{8,12},{12,8},{1,5},{5,1},{9,13},{13,9},{2,6},{6,2},{1... | collective-permute-start | bytes 196616 | tf_op jit(solution)/shard_map/ppermute | solution.py:431
  47.7 4.5 %collective-permute-start.12 = (bf16[64,512]{1,0:T(8,128)(2,1)S(1)}, bf16[64,512]{1,0:T(8,128)(2,1)S(1)}, u32[]{:S(2)}, u32[]{:S(2)}) collective-permute-start(bf16[64,512]{1,0:T(8,128)(2,1)S(1)} %get-tuple-element.36), channel_id=1, source_target_pairs={{0,8},{4,12},{8,0},{12,4},{1,9},{5,13},{9,1},{13,5},{2,10},{6,14},... | collective-permute-start | bytes 196616 | tf_op jit(solution)/shard_map/ppermute | solution.py:431
  49.4 4.0 %collective-permute-start.13 = (bf16[64,512]{1,0:T(8,128)(2,1)S(1)}, bf16[64,512]{1,0:T(8,128)(2,1)S(1)}, u32[]{:S(2)}, u32[]{:S(2)}) collective-permute-start(bf16[64,512]{1,0:T(8,128)(2,1)S(1)} %get-tuple-element.37), channel_id=1, source_target_pairs={{0,12},{4,8},{8,4},{12,0},{1,13},{5,9},{9,5},{13,1},{2,14},{6,10},... | collective-permute-start | bytes 196616 | tf_op jit(solution)/shard_map/ppermute | solution.py:431

commit v2 on v0

--- a/solution.py
+++ b/solution.py
@@ -3,6 +3,8 @@
 import jax
 import jax.numpy as jnp
 from jax import lax
+from jax.experimental import pallas as pl
+from jax.experimental.pallas import tpu as pltpu
 from jax.sharding import PartitionSpec as P
 
 HD = 128
@@ -119,9 +121,333 @@
     return (attended, attended_tangent)
 
 
+def _dot(a, b, dims):
+    return lax.dot_general(a, b, (dims, ((), ())), preferred_element_type=jnp.float32)
+
+
+def _nt(a, b):
+    return _dot(a, b, ((1,), (1,)))
+
+
+def _nn(a, b):
+    return _dot(a, b, ((1,), (0,)))
+
+
+_COST = pl.CostEstimate(flops=1, bytes_accessed=1, transcendentals=0)
+
+_LONG = pl.CostEstimate(flops=3_000_000_000, bytes_accessed=1, transcendentals=0)
+
+
+def _params(mib=24):
+    return pltpu.CompilerParams(vmem_limit_bytes=mib * 2**20)
+
+
+def _one_block(q, dq, k, dk, v, vdv):
+    scaling = HD ** (-0.5)
+    scores = _nt(q, k)
+    change = _nt(jnp.concatenate([dq, q], axis=1), jnp.concatenate([k, dk], axis=1))
+    peak = jnp.max(scores, axis=1, keepdims=True)
+    weights = jnp.exp((scores - peak) * scaling)
+    mixed = weights * (change * scaling)
+    total = jnp.sum(weights, axis=1, keepdims=True)
+    shift = jnp.sum(mixed, axis=1, keepdims=True)
+    inverse = 1.0 / total
+    plain = _nn(weights.astype(jnp.bfloat16), vdv)
+    attended = plain[:, :HD] * inverse
+    tangent = _nn(mixed.astype(jnp.bfloat16), v) + plain[:, HD:]
+    tangent = tangent * inverse - (shift * inverse) * attended
+    return attended.astype(jnp.bfloat16), tangent.astype(jnp.bfloat16)
+
+
+def _col(head):
+    return pl.ds(pl.multiple_of(head * HD, HD), HD)
+
+
+def pack(arrays, g, whole, shared):
+    rows = arrays[0].shape[0]
+    n = len(arrays)
+    parts = 1
+    step = rows // parts
+    n_out = len(whole) + len(shared)
+
+    def kernel(*refs):
+        ins, outs, sem = refs[:n], refs[n : n + n_out], refs[n + n_out]
+        other = 1 - lax.axis_index("blk")
+        copies = []
+        for out, i in zip(outs, whole):
+            at = _col(other * g + i)
+            copies += [(ins[a], at, out, a) for a in range(n)]
+        for out, i in zip(outs[len(whole) :], shared):
+            at = pl.ds((2 * g + i) * HD, HD)
+            copies += [(ins[a], at, out, a - 2) for a in range(2, n)]
+        copies = [
+            pltpu.make_async_copy(
+                source.at[pl.ds(p * step, step), at],
+                out.at[a, pl.ds(p * step, step)],
+                sem.at[c * parts + p],
+            )
+            for c, (source, at, out, a) in enumerate(copies)
+            for p in range(parts)
+        ]
+        for c in copies:
+            c.start()
+        for c in copies:
+            c.wait()
+
+    shapes = [(n, rows, HD)] * len(whole) + [(n - 2, rows, HD)] * len(shared)
+    n_copies = parts * sum(shape[0] for shape in shapes)
+    return pl.pallas_call(
+        kernel,
+        out_shape=[jax.ShapeDtypeStruct(shape, jnp.bfloat16) for shape in shapes],
+        in_specs=[pl.BlockSpec(memory_space=pltpu.HBM)] * n,
+        out_specs=[pl.BlockSpec(memory_space=pl.ANY)] * n_out,
+        scratch_shapes=[pltpu.SemaphoreType.DMA((n_copies,))],
+        compiler_params=_params(),
+        cost_estimate=_COST,
+        name="pack",
+    )(*(pltpu.with_memory_space_constraint(a, pltpu.HBM) for a in arrays))
+
+
+def _copy_in(copies, sems):
+    copies = [
+        pltpu.make_async_copy(source, target, sems.at[at])
+        for at, (source, target) in enumerate(copies)
+    ]
+    for c in copies:
+        c.start()
+    for c in copies:
+        c.wait()
+
+
+def _cut(outs, held, me):
+    piece = outs[0].shape[0]
+    for s, out in enumerate(outs):
+        out[...] = held[pl.ds(pl.multiple_of((me ^ s) * piece, piece), piece), :]
+
+
+def whole_head(own, received, done, g, which, n_head):
+    rows = own[0].shape[0]
+    piece = rows // n_head
+    n = len(own)
+    width = (which + 1) * HD
+    last = which == g - 1
+    n_far = n_head if last else 1
+
+    def kernel(*refs):
+        ins, got, before = refs[:n], refs[n], refs[n + 1 : n + 1 + len(done)]
+        near, *far, mine, held, sems = refs[n + 1 + len(done) :]
+        head = lax.axis_index("blk") * g + which
+        _copy_in([(ins[a].at[:, _col(head)], mine.at[a]) for a in range(n)], sems)
+        k, dk, v, dv = (
+            jnp.concatenate([mine[a], got[a]], axis=0) for a in (2, 3, 4, 5)
+        )
+        vdv = jnp.concatenate([v, dv], axis=1)
+        targets = (near, held if last else far[0])
+        for block, source in enumerate((mine, got)):
+            result = _one_block(source[0], source[1], k, dk, v, vdv)
+            out = targets[block]
+            for o in range(2):
+                if done:
+                    old = before[block][:, o * which * HD : (o + 1) * which * HD]
+                    out[:, o * width : o * width + which * HD] = old
+                out[:, (o + 1) * width - HD : (o + 1) * width] = result[o]
+        if last:
+            _cut(far, held, lax.axis_index("head"))
+
+    vmem = pl.BlockSpec(memory_space=pltpu.VMEM)
+    far_rows = piece if last else rows
+    return pl.pallas_call(
+        kernel,
+        out_shape=[jax.ShapeDtypeStruct((rows, 2 * width), jnp.bfloat16)]
+        + [jax.ShapeDtypeStruct((far_rows, 2 * width), jnp.bfloat16)] * n_far,
+        in_specs=[pl.BlockSpec(memory_space=pl.ANY)] * n + [vmem] * (1 + len(done)),
+        out_specs=[vmem] * (1 + n_far),
+        scratch_shapes=[
+            pltpu.VMEM((n, rows, HD), jnp.bfloat16),
+            pltpu.VMEM((rows, 2 * width), jnp.bfloat16),
+            pltpu.SemaphoreType.DMA((n,)),
+        ],
+        compiler_params=_params(),
+        cost_estimate=_COST,
+        name="whole_head",
+    )(*own, received, *done)
+
+
+def shared_head(own, received, done, which, n_head, cost=_COST):
+    rows = own[0].shape[0]
+    piece = rows // n_head
+    n = len(own)
+    before = sum(d.shape[1] for d in done) // 2
+    width = before + HD
+
+    def kernel(*refs):
+        ins, got, rest = refs[:n], refs[n], refs[n + 1 :]
+        old, outs = rest[: len(done)], rest[len(done) : len(done) + n_head]
+        mine, held, sems = rest[len(done) + n_head :]
+        at = pl.ds(which * HD, HD)
+        _copy_in([(ins[a].at[:, at], mine.at[a]) for a in range(n)], sems)
+        k, dk, v, dv = (
+            jnp.concatenate([mine[2 + a], got[a]], axis=0) for a in range(4)
+        )
+        result = _one_block(mine[0], mine[1], k, dk, v, jnp.concatenate([v, dv], axis=1))
+        for o in range(2):
+            if done:
+                held[:, o * width : o * width + before] = old[0][
+                    :, o * before : (o + 1) * before
+                ]
+            held[:, (o + 1) * width - HD : (o + 1) * width] = result[o]
+        _cut(outs, held, lax.axis_index("head"))
+
+    vmem = pl.BlockSpec(memory_space=pltpu.VMEM)
+    return pl.pallas_call(
+        kernel,
+        out_shape=[jax.ShapeDtypeStruct((piece, 2 * width), jnp.bfloat16)] * n_head,
+        in_specs=[pl.BlockSpec(memory_space=pl.ANY)] * n + [vmem] * (1 + len(done)),
+        out_specs=[vmem] * n_head,
+        scratch_shapes=[
+            pltpu.VMEM((n, rows, HD), jnp.bfloat16),
+            pltpu.VMEM((rows, 2 * width), jnp.bfloat16),
+            pltpu.SemaphoreType.DMA((n,)),
+        ],
+        compiler_params=_params(),
+        cost_estimate=cost,
+        name="shared_head",
+    )(*own, received, *done)
+
+
+def gather_far(pieces):
+    n = len(pieces)
+
+    def kernel(*refs):
+        _copy_in([(refs[s], refs[n].at[s]) for s in range(n)], refs[n + 1])
+
+    return pl.pallas_call(
+        kernel,
+        out_shape=jax.ShapeDtypeStruct((n, *pieces[0].shape), jnp.bfloat16),
+        in_specs=[pl.BlockSpec(memory_space=pl.ANY)] * n,
+        out_specs=pl.BlockSpec(memory_space=pl.ANY),
+        scratch_shapes=[pltpu.SemaphoreType.DMA((n,))],
+        compiler_params=_params(),
+        cost_estimate=_COST,
+        name="gather_far",
+    )(*pieces)
+
+
+def _place(copies, outs, source, o, column, heads):
+    at = pl.ds(pl.multiple_of(column * HD, HD), heads * HD)
+    copies.append((source, outs[o].at[:, at]))
+
+
+def place_near(pieces, g, heads):
+    n = len(pieces)
+    piece, twice = pieces[0].shape
+    width = twice // 2
+
+    def kernel(*refs):
+        ins, outs, sems = refs[:n], refs[n : n + 2], refs[n + 2]
+        me, blk = lax.axis_index("head"), lax.axis_index("blk")
+        copies = []
+        for s in range(n):
+            first = (me ^ s) * heads
+            for o in range(2):
+                whole = ins[s].at[:, pl.ds(o * width, g * HD)]
+                _place(copies, outs, whole, o, first + blk * g, g)
+                if g > 1:
+                    rest = ins[s].at[:, pl.ds(o * width + g * HD, (g - 1) * HD)]
+                    _place(copies, outs, rest, o, first + 2 * g, g - 1)
+        _copy_in(copies, sems)
+
+    full = jax.ShapeDtypeStruct((piece, n * heads * HD), jnp.bfloat16)
+    return pl.pallas_call(
+        kernel,
+        out_shape=[full] * 2,
+        in_specs=[pl.BlockSpec(memory_space=pl.ANY)] * n,
+        out_specs=[pl.BlockSpec(memory_space=pltpu.HBM)] * 2,
+        scratch_shapes=[pltpu.SemaphoreType.DMA((4 * n,))],
+        compiler_params=_params(),
+        cost_estimate=_COST,
+        name="place_near",
+    )(*pieces)
+
+
+def place_last(outputs, crossed, last, g, heads):
+    n = len(last)
+
+    def kernel(*refs):
+        far, ours, outs, sems = refs[2], refs[3 : 3 + n], refs[-3:-1], refs[-1]
+        me, blk = lax.axis_index("head"), lax.axis_index("blk")
+        width = g * HD
+        copies = []
+        for s in range(n):
+            first = (me ^ s) * heads
+            for o in range(2):
+                whole = far.at[s, :, pl.ds(o * width, width)]
+                _place(copies, outs, whole, o, first + (1 - blk) * g, g)
+                rest = ours[s].at[:, pl.ds(o * HD, HD)]
+                _place(copies, outs, rest, o, first + 3 * g - 1, 1)
+        _copy_in(copies, sems)
+
+    return pl.pallas_call(
+        kernel,
+        out_shape=[jax.ShapeDtypeStruct(o.shape, o.dtype) for o in outputs],
+        in_specs=[pl.BlockSpec(memory_space=pltpu.HBM)] * 2
+        + [pl.BlockSpec(memory_space=pl.ANY)] * (1 + n),
+        out_specs=[pl.BlockSpec(memory_space=pltpu.HBM)] * 2,
+        scratch_shapes=[pltpu.SemaphoreType.DMA((4 * n,))],
+        input_output_aliases={0: 0, 1: 1},
+        compiler_params=_params(),
+        cost_estimate=_COST,
+        name="place_last",
+    )(*(pltpu.with_memory_space_constraint(o, pltpu.HBM) for o in outputs), crossed, *last)
+
+
+def paired(n_head, query_rows, key_rows, value_rows, query_tangent, key_tangent, value_tangent):
+    heads = query_rows.shape[1] // HD
+    g = heads // 3
+    own = (query_rows, query_tangent, key_rows, key_tangent, value_rows, value_tangent)
+
+    def cross(x):
+        return lax.ppermute(x, "blk", [(0, 1), (1, 0)])
+
+    def along(x, s):
+        return lax.ppermute(x, "head", [(i, i ^ s) for i in range(n_head)])
+
+    def spread(parts):
+        return [parts[0]] + [along(parts[s], s) for s in range(1, n_head)]
+
+    first = pack(own, g, [0], [])
+    rest = pack(own, g, list(range(1, g)), list(range(g)))
+    whole_in = [cross(p) for p in first + rest[: g - 1]]
+    shared_in = [cross(p) for p in rest[g - 1 :]]
+    done = ()
+    for i in range(g):
+        near, *far = whole_head(own, whole_in[i], done, g, i, n_head)
+        done = (near, *far)
+    far = gather_far(spread(far))
+    done = (near,)
+    for i in range(g):
+        parts = list(shared_head(own, shared_in[i], done, 2 * g + i, n_head, _COST if i + 1 < g else _LONG))
+        done = ()
+        if i == 0:
+            far, parts[0] = lax.optimization_barrier((far, parts[0]))
+            crossed = cross(far)
+            outputs = place_near(spread(parts), g, heads)
+    return place_last(outputs, crossed, spread(parts), g, heads)
+
+
 def solution(mesh):
+    n_head = mesh.shape["head"]
+
+    def one_device(*arrays):
+        heads = arrays[0].shape[1] // HD
+        rows = arrays[0].shape[0]
+        two = mesh.shape["blk"] == 2 and n_head == 4
+        if two and heads == 6 and rows % (16 * n_head) == 0:
+            return paired(n_head, *arrays)
+        return local(*arrays)
+
     return jax.shard_map(
-        local,
+        one_device,
         mesh=mesh,
         in_specs=(
             P(("batch", "blk"), "head"),

time: 93.5 us -> 41.9 us (0.45)
  blocking collectives: 46.5 us -> 0 us
  local copies, waits for them, and re-layouts: 15.8 us -> 0.04 us
  matrix products: 9.84 us -> 0 us
  Pallas kernels: 0 us -> 8.33 us
  starting transfers between devices: 6.92 us -> 13.5 us
  waiting for transfers between devices: 12.5 us -> 19 us
    all_gather x4 -> x0, blocking collectives: 46.5 us -> none  [the longest x1 12.8 us: local(): lax.all_gather(key_rows, 'blk', axis=0, tiled=True)]
    ppermute x0 -> x14, waiting for transfers between devices: none -> 19 us  [the longest x5 16.7 us: cross(): return lax.ppermute(x, 'blk', [(0, 1), (1, 0)])]
    ppermute x0 -> x14, starting transfers between devices: none -> 13.5 us  [the longest x5 6.96 us: cross(): return lax.ppermute(x, 'blk', [(0, 1), (1, 0)])]
    all_to_all x2 -> x0, waiting for transfers between devices: 12.5 us -> none  [the longest x1 6.63 us: local(): lax.all_to_all(result_rows, 'head', split_axis=0, concat_axis=1, tiled=True)]
    unnamed x12, local copies, waits for them, and re-layouts: 11.2 us -> 0.04 us
    dot_general x6 -> x0, matrix products: 9.84 us -> none  [the longest x1 3.5 us: score_pair(): jnp.einsum('qhd,khd->qhk', tangent_heads, key_block, preferred_element_ty...]
    pallas_call x0 -> x9, Pallas kernels: none -> 8.33 us  [the longest x2 2.41 us: pack(): pl.pallas_call(kernel, out_shape=[jax.ShapeDtypeStruct(shape, jnp.bfloat1...]
    all_to_all x2 -> x0, starting transfers between devices: 6.92 us -> none  [the longest x1 3.46 us: local(): lax.all_to_all(result_rows, 'head', split_axis=0, concat_axis=1, tiled=True)]
  transfers between devices with their start and end apart: 2 -> 14, of which waited for: 2 -> 7; matrix products, arithmetic and copies ran while one was open for 2% -> 0% of each run, Pallas kernels for 0% -> 15%
where the time goes in v2:
time: 41.9 us; the launch traced here: 41.7 us
  waiting for transfers between devices  19 us (45%)
  starting transfers between devices  13.5 us (32%)
  Pallas kernels  8.33 us (20%)
  between operations  0.81 us (2%)
    ppermute x5, waiting for transfers between devices, cross(): return lax.ppermute(x, 'blk', [(0, 1), (1, 0)])  16.7 us
    ppermute x5, starting transfers between devices, cross(): return lax.ppermute(x, 'blk', [(0, 1), (1, 0)])  6.96 us
    ppermute x9, starting transfers between devices, along(): return lax.ppermute(x, 'head', [(i, i ^ s) for i in range(n_head)])  6.57 us
    pallas_call x2, Pallas kernels, pack(): pl.pallas_call(kernel, out_shape=[jax.ShapeDtypeStruct(shape, jnp.bfloat1...  2.41 us
    pallas_call x2, Pallas kernels, whole_head(): pl.pallas_call(kernel, out_shape=[jax.ShapeDtypeStruct((rows, 2 * width),...  2.34 us
    ppermute x9, waiting for transfers between devices, along(): return lax.ppermute(x, 'head', [(i, i ^ s) for i in range(n_head)])  2.21 us
    pallas_call x2, Pallas kernels, shared_head(): pl.pallas_call(kernel, out_shape=[jax.ShapeDtypeStruct((piece, 2 * width)...  1.48 us
    pallas_call x1, Pallas kernels, place_near(): pl.pallas_call(kernel, out_shape=[full] * 2, in_specs=[pl.BlockSpec(memor...  0.87 us
  transfers between devices with their start and end apart: 14, of which 7 were waited for; matrix products, arithmetic and copies ran while one was open for 0% of the time, Pallas kernels for 15%

profile of v2, /device:TPU:0, one launch (start us, length us, event | category | flops | bytes accessed | tf_op | source)
XLA Modules:
  0.0 41.7 jit_solution(13758060952590430800)
XLA Ops:
  0.6 1.1 %pack.3 = bf16[6,256,128]{2,1,0:T(8,128)(2,1)S(1)} custom-call(bf16[256,768]{1,0:T(8,128)(2,1)} %refs_0_.11, bf16[256,768]{1,0:T(8,128)(2,1)} %refs_1_.11, bf16[256,768]{1,0:T(8,128)(2,1)} %refs_2_.11, bf16[256,768]{1,0:T(8,128)(2,1)} %refs_3_.11, bf16[256,768]{1,0:T(8,128)(2,1)} %refs_4_.11, bf16[256,768]{1,0:T(8,128)(2,1)} %refs_5_.11), custom_call_target="tpu_custom_call" | custom-call | flops 1 | bytes 1 | tf_op jit(solution)/shard_map/pack/pallas_call | solution.py:199
  1.7 0.0 copy-start
  1.7 0.0 copy-start.1
  1.7 0.0 copy-start.2
  1.7 0.0 copy-start.3
  1.8 0.0 copy-start.4
  1.8 0.0 copy-start.5
  1.8 3.0 %collective-permute-start.1 = (bf16[6,256,128]{2,1,0:T(8,128)(2,1)S(1)}, bf16[6,256,128]{2,1,0:T(8,128)(2,1)S(1)}, u32[]{:S(2)}, u32[]{:S(2)}) collective-permute-start(bf16[6,256,128]{2,1,0:T(8,128)(2,1)S(1)} %pack.3), channel_id=1, source_target_pairs={{0,16},{16,0},{1,17},{17,1},{2,18},{18,2},{3,19},{19,3},{4,20},{20... | collective-permute-start | bytes 1179656 | tf_op jit(solution)/shard_map/ppermute | solution.py:410
  4.8 1.3 %pack.2 = (bf16[6,256,128]{2,1,0:T(8,128)(2,1)S(1)}, bf16[4,256,128]{2,1,0:T(8,128)(2,1)S(1)}, bf16[4,256,128]{2,1,0:T(8,128)(2,1)S(1)}) custom-call(bf16[256,768]{1,0:T(8,128)(2,1)} %refs_0_.11, bf16[256,768]{1,0:T(8,128)(2,1)} %refs_1_.11, bf16[256,768]{1,0:T(8,128)(2,1)} %refs_2_.11, bf16[256,768]{1,0:T(8,128)(2,1)} %refs_3_.11, ...), custom_call_target="tpu_custom_call" | custom-call | flops 1 | bytes 1 | tf_op jit(solution)/shard_map/pack/pallas_call | solution.py:199
  6.1 0.2 collective-permute-start
  6.4 1.9 %collective-permute-start.5 = (bf16[4,256,128]{2,1,0:T(8,128)(2,1)S(1)}, bf16[4,256,128]{2,1,0:T(8,128)(2,1)S(1)}, u32[]{:S(2)}, u32[]{:S(2)}) collective-permute-start(bf16[4,256,128]{2,1,0:T(8,128)(2,1)S(1)} %get-tuple-element.31), channel_id=1, source_target_pairs={{0,16},{16,0},{1,17},{17,1},{2,18},{18,2},{3,19},{19,3},{4,20},{20... | collective-permute-start | bytes 786440 | tf_op jit(solution)/shard_map/ppermute | solution.py:410
  8.2 0.2 collective-permute-start.10
  8.4 6.3 %collective-permute-done.1.refs_6_ = bf16[6,256,128]{2,1,0:T(8,128)(2,1)S(1)} collective-permute-done((bf16[6,256,128]{2,1,0:T(8,128)(2,1)S(1)}, bf16[6,256,128]{2,1,0:T(8,128)(2,1)S(1)}, u32[]{:S(2)}, u32[]{:S(2)}) %collective-permute-start.1) | collective-permute-done | bytes 393248 | tf_op jit(solution)/shard_map/ppermute | solution.py:410
  14.7 0.0 copy-done
  14.7 0.0 copy-done.1
  14.7 0.0 copy-done.2
  14.7 0.0 copy-done.3
  14.8 0.0 copy-done.4
  14.8 1.2 %whole_head.2 = (bf16[256,256]{1,0:T(8,128)(2,1)S(1)}, bf16[256,256]{1,0:T(8,128)(2,1)S(1)}) custom-call(bf16[256,768]{1,0:T(8,128)(2,1)S(1)} %copy-done, bf16[256,768]{1,0:T(8,128)(2,1)S(1)} %copy-done.1, bf16[256,768]{1,0:T(8,128)(2,1)S(1)} %copy-done.2, bf16[256,768]{1,0:T(8,128)(2,1)S(1)} %copy-done.3, bf16[256,768]{1,0:T(8,128)(2,1)S(1)} %copy-done.4, ...), custom_call_target="tpu_custom_call" | custom-call | flops 1 | bytes 1 | tf_op jit(solution)/shard_map/whole_head/pallas_call | solution.py:259
  15.9 7.2 %collective-permute-done.refs_6_ = bf16[6,256,128]{2,1,0:T(8,128)(2,1)S(1)} collective-permute-done((bf16[6,256,128]{2,1,0:T(8,128)(2,1)S(1)}, bf16[6,256,128]{2,1,0:T(8,128)(2,1)S(1)}, u32[]{:S(2)}, u32[]{:S(2)}) %collective-permute-start) | collective-permute-done | bytes 393248 | tf_op jit(solution)/shard_map/ppermute | solution.py:410
  23.2 1.2 %whole_head.3 = (bf16[256,512]{1,0:T(8,128)(2,1)S(1)}, bf16[64,512]{1,0:T(8,128)(2,1)S(1)}, bf16[64,512]{1,0:T(8,128)(2,1)S(1)}, bf16[64,512]{1,0:T(8,128)(2,1)S(1)}, bf16[64,512]{1,0:T(8,128)(2,1)S(1)}) custom-call(bf16[256,768]{1,0:T(8,128)(2,1)S(1)} %copy-done, bf16[256,768]{1,0:T(8,128)(2,1)S(1)} %copy-done.1, bf16[256,768]{1,0:T(8,128)(2,1)S(1)} %copy-done.2, ...), custom_call_target="tpu_custom_call" | custom-call | flops 1 | bytes 1 | tf_op jit(solution)/shard_map/whole_head/pallas_call | solution.py:259
  24.3 0.1 collective-permute-start.2
  24.4 2.2 %collective-permute-start.3 = (bf16[64,512]{1,0:T(8,128)(2,1)S(1)}, bf16[64,512]{1,0:T(8,128)(2,1)S(1)}, u32[]{:S(2)}, u32[]{:S(2)}) collective-permute-start(bf16[64,512]{1,0:T(8,128)(2,1)S(1)} %get-tuple-element.29), channel_id=1, source_target_pairs={{0,8},{4,12},{8,0},{12,4},{1,9},{5,13},{9,1},{13,5},{2,10},{6,14},... | collective-permute-start | bytes 196616 | tf_op jit(solution)/shard_map/ppermute | solution.py:413
  26.6 0.1 collective-permute-start.4
  26.6 2.1 %collective-permute-done.5.refs_6_ = bf16[4,256,128]{2,1,0:T(8,128)(2,1)S(1)} collective-permute-done((bf16[4,256,128]{2,1,0:T(8,128)(2,1)S(1)}, bf16[4,256,128]{2,1,0:T(8,128)(2,1)S(1)}, u32[]{:S(2)}, u32[]{:S(2)}) %collective-permute-start.5) | collective-permute-done | bytes 262176 | tf_op jit(solution)/shard_map/ppermute | solution.py:410
  28.8 0.7 %shared_head.2 = (bf16[64,768]{1,0:T(8,128)(2,1)S(1)}, bf16[64,768]{1,0:T(8,128)(2,1)S(1)}, bf16[64,768]{1,0:T(8,128)(2,1)S(1)}, bf16[64,768]{1,0:T(8,128)(2,1)S(1)}) custom-call(bf16[256,768]{1,0:T(8,128)(2,1)S(1)} %copy-done, bf16[256,768]{1,0:T(8,128)(2,1)S(1)} %copy-done.1, bf16[256,768]{1,0:T(8,128)(2,1)S(1)} %copy-done.2, ...), custom_call_target="tpu_custom_call" | custom-call | flops 1 | bytes 1 | tf_op jit(solution)/shard_map/shared_head/pallas_call | solution.py:302
  29.5 0.1 collective-permute-start.6
  29.6 0.0 collective-permute-done.2.refs_1_
  29.6 2.2 %collective-permute-start.7 = (bf16[64,768]{1,0:T(8,128)(2,1)S(1)}, bf16[64,768]{1,0:T(8,128)(2,1)S(1)}, u32[]{:S(2)}, u32[]{:S(2)}) collective-permute-start(bf16[64,768]{1,0:T(8,128)(2,1)S(1)} %get-tuple-element.36), channel_id=1, source_target_pairs={{0,8},{4,12},{8,0},{12,4},{1,9},{5,13},{9,1},{13,5},{2,10},{6,14},... | collective-permute-start | bytes 294920 | tf_op jit(solution)/shard_map/ppermute | solution.py:413
  31.8 0.0 collective-permute-done.3.refs_2_
  31.8 0.1 collective-permute-start.8
  31.9 0.0 collective-permute-done.4.refs_3_
  31.9 0.4 gather_far.1
  32.3 1.7 %collective-permute-start.9 = (bf16[4,64,512]{2,1,0:T(8,128)(2,1)S(1)}, bf16[4,64,512]{2,1,0:T(8,128)(2,1)S(1)}, u32[]{:S(2)}, u32[]{:S(2)}) collective-permute-start(bf16[4,64,512]{2,1,0:T(8,128)(2,1)S(1)} %gather_far.1), channel_id=1, source_target_pairs={{0,16},{16,0},{1,17},{17,1},{2,18},{18,2},{3,19},{19,3},{4,20},{20... | collective-permute-start | bytes 786440 | tf_op jit(solution)/shard_map/ppermute | solution.py:410
  34.0 0.0 collective-permute-done.10.refs_6_
  34.0 0.7 %shared_head.3 = (bf16[64,256]{1,0:T(8,128)(2,1)S(1)}, bf16[64,256]{1,0:T(8,128)(2,1)S(1)}, bf16[64,256]{1,0:T(8,128)(2,1)S(1)}, bf16[64,256]{1,0:T(8,128)(2,1)S(1)}) custom-call(bf16[256,768]{1,0:T(8,128)(2,1)S(1)} %copy-done, bf16[256,768]{1,0:T(8,128)(2,1)S(1)} %copy-done.1, bf16[256,768]{1,0:T(8,128)(2,1)S(1)} %copy-done.2, ...), custom_call_target="tpu_custom_call" | custom-call | flops 3000000000 | bytes 1 | tf_op jit(solution)/shard_map/shared_head/pallas_call | solution.py:302
  34.7 0.1 collective-permute-start.11
  34.9 0.0 collective-permute-done.6.refs_1_
  34.9 1.5 %collective-permute-start.12 = (bf16[64,256]{1,0:T(8,128)(2,1)S(1)}, bf16[64,256]{1,0:T(8,128)(2,1)S(1)}, u32[]{:S(2)}, u32[]{:S(2)}) collective-permute-start(bf16[64,256]{1,0:T(8,128)(2,1)S(1)} %get-tuple-element.44), channel_id=1, source_target_pairs={{0,8},{4,12},{8,0},{12,4},{1,9},{5,13},{9,1},{13,5},{2,10},{6,14},... | collective-permute-start | bytes 98312 | tf_op jit(solution)/shard_map/ppermute | solution.py:413
  36.4 0.0 collective-permute-done.7.refs_2_
  36.4 0.3 collective-permute-start.13
  36.7 0.3 collective-permute-done.8.refs_3_
  37.0 0.9 %place_near.1 = (bf16[64,3072]{1,0:T(8,128)(2,1)}, bf16[64,3072]{1,0:T(8,128)(2,1)}) custom-call(bf16[64,768]{1,0:T(8,128)(2,1)S(1)} %get-tuple-element.34.refs_0_, bf16[64,768]{1,0:T(8,128)(2,1)S(1)} %collective-permute-done.6.refs_1_, bf16[64,768]{1,0:T(8,128)(2,1)S(1)} %collective-permute-done.7.refs_2_, bf16[64,768]{1,0:T(8,128)(2,1)S(1)} %collective-permute-done.8.refs_3_), custom_call_target="tpu_custom_call" | custom-call | flops 1 | bytes 1 | tf_op jit(solution)/shard_map/place_near/pallas_call | solution.py:361
  37.9 0.0 collective-permute-done.11.refs_4_
  37.9 0.9 %collective-permute-done.12.refs_5_ = bf16[64,256]{1,0:T(8,128)(2,1)S(1)} collective-permute-done((bf16[64,256]{1,0:T(8,128)(2,1)S(1)}, bf16[64,256]{1,0:T(8,128)(2,1)S(1)}, u32[]{:S(2)}, u32[]{:S(2)}) %collective-permute-start.12) | collective-permute-done | bytes 32800 | tf_op jit(solution)/shard_map/ppermute | solution.py:413
  38.8 1.0 %collective-permute-done.13.refs_6_ = bf16[64,256]{1,0:T(8,128)(2,1)S(1)} collective-permute-done((bf16[64,256]{1,0:T(8,128)(2,1)S(1)}, bf16[64,256]{1,0:T(8,128)(2,1)S(1)}, u32[]{:S(2)}, u32[]{:S(2)}) %collective-permute-start.13) | collective-permute-done | bytes 32800 | tf_op jit(solution)/shard_map/ppermute | solution.py:413
  39.7 1.0 %collective-permute-done.9.refs_2_ = bf16[4,64,512]{2,1,0:T(8,128)(2,1)S(1)} collective-permute-done((bf16[4,64,512]{2,1,0:T(8,128)(2,1)S(1)}, bf16[4,64,512]{2,1,0:T(8,128)(2,1)S(1)}, u32[]{:S(2)}, u32[]{:S(2)}) %collective-permute-start.9) | collective-permute-done | bytes 262176 | tf_op jit(solution)/shard_map/ppermute | solution.py:410
  40.8 0.9 %place_last.1 = (bf16[64,3072]{1,0:T(8,128)(2,1)}, bf16[64,3072]{1,0:T(8,128)(2,1)}) custom-call(bf16[64,3072]{1,0:T(8,128)(2,1)} %get-tuple-element.38.refs_0_, bf16[64,3072]{1,0:T(8,128)(2,1)} %get-tuple-element.39.refs_1_, bf16[4,64,512]{2,1,0:T(8,128)(2,1)S(1)} %collective-permute-done.9.refs_2_, ...), custom_call_target="tpu_custom_call", output_to_operand_aliasing={{0}: (0, {}), {1}: (1, {})} | custom-call | flops 1 | bytes 1 | tf_op jit(solution)/shard_map/place_last/pallas_call | solution.py:390
  (1 shorter events, 0.0 us)
Async XLA Ops:
  1.7 13.0 %copy-start = (bf16[256,768]{1,0:T(8,128)(2,1)S(1)}, bf16[256,768]{1,0:T(8,128)(2,1)}, u32[]{:S(2)}) copy-start(bf16[256,768]{1,0:T(8,128)(2,1)} %refs_0_.11) | copy-start | bytes 1179652
  1.7 13.0 %copy-start.1 = (bf16[256,768]{1,0:T(8,128)(2,1)S(1)}, bf16[256,768]{1,0:T(8,128)(2,1)}, u32[]{:S(2)}) copy-start(bf16[256,768]{1,0:T(8,128)(2,1)} %refs_1_.11) | copy-start | bytes 1179652
  1.7 13.0 %copy-start.2 = (bf16[256,768]{1,0:T(8,128)(2,1)S(1)}, bf16[256,768]{1,0:T(8,128)(2,1)}, u32[]{:S(2)}) copy-start(bf16[256,768]{1,0:T(8,128)(2,1)} %refs_2_.11) | copy-start | bytes 1179652
  1.7 13.0 %copy-start.3 = (bf16[256,768]{1,0:T(8,128)(2,1)S(1)}, bf16[256,768]{1,0:T(8,128)(2,1)}, u32[]{:S(2)}) copy-start(bf16[256,768]{1,0:T(8,128)(2,1)} %refs_3_.11) | copy-start | bytes 1179652
  1.8 13.0 %copy-start.4 = (bf16[256,768]{1,0:T(8,128)(2,1)S(1)}, bf16[256,768]{1,0:T(8,128)(2,1)}, u32[]{:S(2)}) copy-start(bf16[256,768]{1,0:T(8,128)(2,1)} %refs_4_.11) | copy-start | bytes 1179652
  1.8 13.0 %copy-start.5 = (bf16[256,768]{1,0:T(8,128)(2,1)S(1)}, bf16[256,768]{1,0:T(8,128)(2,1)}, u32[]{:S(2)}) copy-start(bf16[256,768]{1,0:T(8,128)(2,1)} %refs_5_.11) | copy-start | bytes 1179652
  1.8 12.9 %collective-permute-start.1 = (bf16[6,256,128]{2,1,0:T(8,128)(2,1)S(1)}, bf16[6,256,128]{2,1,0:T(8,128)(2,1)S(1)}, u32[]{:S(2)}, u32[]{:S(2)}) collective-permute-start(bf16[6,256,128]{2,1,0:T(8,128)(2,1)S(1)} %pack.3), channel_id=1, source_target_pairs={{0,16},{16,0},{1,17},{17,1},{2,18},{18,2},{3,19},{19,3},{4,20},{20... | collective-permute-start | bytes 1179656 | tf_op jit(solution)/shard_map/ppermute | solution.py:410
  6.1 17.0 %collective-permute-start = (bf16[6,256,128]{2,1,0:T(8,128)(2,1)S(1)}, bf16[6,256,128]{2,1,0:T(8,128)(2,1)S(1)}, u32[]{:S(2)}, u32[]{:S(2)}) collective-permute-start(bf16[6,256,128]{2,1,0:T(8,128)(2,1)S(1)} %get-tuple-element.24), channel_id=1, source_target_pairs={{0,16},{16,0},{1,17},{17,1},{2,18},{18,2},{3,19},{19,3},{4,20},{20... | collective-permute-start | bytes 1179656 | tf_op jit(solution)/shard_map/ppermute | solution.py:410
  6.4 22.4 %collective-permute-start.5 = (bf16[4,256,128]{2,1,0:T(8,128)(2,1)S(1)}, bf16[4,256,128]{2,1,0:T(8,128)(2,1)S(1)}, u32[]{:S(2)}, u32[]{:S(2)}) collective-permute-start(bf16[4,256,128]{2,1,0:T(8,128)(2,1)S(1)} %get-tuple-element.31), channel_id=1, source_target_pairs={{0,16},{16,0},{1,17},{17,1},{2,18},{18,2},{3,19},{19,3},{4,20},{20... | collective-permute-start | bytes 786440 | tf_op jit(solution)/shard_map/ppermute | solution.py:410
  8.2 25.7 %collective-permute-start.10 = (bf16[4,256,128]{2,1,0:T(8,128)(2,1)S(1)}, bf16[4,256,128]{2,1,0:T(8,128)(2,1)S(1)}, u32[]{:S(2)}, u32[]{:S(2)}) collective-permute-start(bf16[4,256,128]{2,1,0:T(8,128)(2,1)S(1)} %get-tuple-element.41), channel_id=1, source_target_pairs={{0,16},{16,0},{1,17},{17,1},{2,18},{18,2},{3,19},{19,3},{4,20},{20... | collective-permute-start | bytes 786440 | tf_op jit(solution)/shard_map/ppermute | solution.py:410
  24.3 5.3 %collective-permute-start.2 = (bf16[64,512]{1,0:T(8,128)(2,1)S(1)}, bf16[64,512]{1,0:T(8,128)(2,1)S(1)}, u32[]{:S(2)}, u32[]{:S(2)}) collective-permute-start(bf16[64,512]{1,0:T(8,128)(2,1)S(1)} %get-tuple-element.28), channel_id=1, source_target_pairs={{0,4},{4,0},{8,12},{12,8},{1,5},{5,1},{9,13},{13,9},{2,6},{6,2},{1... | collective-permute-start | bytes 196616 | tf_op jit(solution)/shard_map/ppermute | solution.py:413
  24.4 7.3 %collective-permute-start.3 = (bf16[64,512]{1,0:T(8,128)(2,1)S(1)}, bf16[64,512]{1,0:T(8,128)(2,1)S(1)}, u32[]{:S(2)}, u32[]{:S(2)}) collective-permute-start(bf16[64,512]{1,0:T(8,128)(2,1)S(1)} %get-tuple-element.29), channel_id=1, source_target_pairs={{0,8},{4,12},{8,0},{12,4},{1,9},{5,13},{9,1},{13,5},{2,10},{6,14},... | collective-permute-start | bytes 196616 | tf_op jit(solution)/shard_map/ppermute | solution.py:413
  26.6 5.3 %collective-permute-start.4 = (bf16[64,512]{1,0:T(8,128)(2,1)S(1)}, bf16[64,512]{1,0:T(8,128)(2,1)S(1)}, u32[]{:S(2)}, u32[]{:S(2)}) collective-permute-start(bf16[64,512]{1,0:T(8,128)(2,1)S(1)} %get-tuple-element.30), channel_id=1, source_target_pairs={{0,12},{4,8},{8,4},{12,0},{1,13},{5,9},{9,5},{13,1},{2,14},{6,10},... | collective-permute-start | bytes 196616 | tf_op jit(solution)/shard_map/ppermute | solution.py:413
  29.5 5.3 %collective-permute-start.6 = (bf16[64,768]{1,0:T(8,128)(2,1)S(1)}, bf16[64,768]{1,0:T(8,128)(2,1)S(1)}, u32[]{:S(2)}, u32[]{:S(2)}) collective-permute-start(bf16[64,768]{1,0:T(8,128)(2,1)S(1)} %get-tuple-element.35), channel_id=1, source_target_pairs={{0,4},{4,0},{8,12},{12,8},{1,5},{5,1},{9,13},{13,9},{2,6},{6,2},{1... | collective-permute-start | bytes 294920 | tf_op jit(solution)/shard_map/ppermute | solution.py:413
  29.6 6.8 %collective-permute-start.7 = (bf16[64,768]{1,0:T(8,128)(2,1)S(1)}, bf16[64,768]{1,0:T(8,128)(2,1)S(1)}, u32[]{:S(2)}, u32[]{:S(2)}) collective-permute-start(bf16[64,768]{1,0:T(8,128)(2,1)S(1)} %get-tuple-element.36), channel_id=1, source_target_pairs={{0,8},{4,12},{8,0},{12,4},{1,9},{5,13},{9,1},{13,5},{2,10},{6,14},... | collective-permute-start | bytes 294920 | tf_op jit(solution)/shard_map/ppermute | solution.py:413
  31.8 5.2 %collective-permute-start.8 = (bf16[64,768]{1,0:T(8,128)(2,1)S(1)}, bf16[64,768]{1,0:T(8,128)(2,1)S(1)}, u32[]{:S(2)}, u32[]{:S(2)}) collective-permute-start(bf16[64,768]{1,0:T(8,128)(2,1)S(1)} %get-tuple-element.37), channel_id=1, source_target_pairs={{0,12},{4,8},{8,4},{12,0},{1,13},{5,9},{9,5},{13,1},{2,14},{6,10},... | collective-permute-start | bytes 294920 | tf_op jit(solution)/shard_map/ppermute | solution.py:413
  32.3 8.5 %collective-permute-start.9 = (bf16[4,64,512]{2,1,0:T(8,128)(2,1)S(1)}, bf16[4,64,512]{2,1,0:T(8,128)(2,1)S(1)}, u32[]{:S(2)}, u32[]{:S(2)}) collective-permute-start(bf16[4,64,512]{2,1,0:T(8,128)(2,1)S(1)} %gather_far.1), channel_id=1, source_target_pairs={{0,16},{16,0},{1,17},{17,1},{2,18},{18,2},{3,19},{19,3},{4,20},{20... | collective-permute-start | bytes 786440 | tf_op jit(solution)/shard_map/ppermute | solution.py:410
  34.7 3.2 %collective-permute-start.11 = (bf16[64,256]{1,0:T(8,128)(2,1)S(1)}, bf16[64,256]{1,0:T(8,128)(2,1)S(1)}, u32[]{:S(2)}, u32[]{:S(2)}) collective-permute-start(bf16[64,256]{1,0:T(8,128)(2,1)S(1)} %get-tuple-element.43), channel_id=1, source_target_pairs={{0,4},{4,0},{8,12},{12,8},{1,5},{5,1},{9,13},{13,9},{2,6},{6,2},{1... | collective-permute-start | bytes 98312 | tf_op jit(solution)/shard_map/ppermute | solution.py:413
  34.9 3.9 %collective-permute-start.12 = (bf16[64,256]{1,0:T(8,128)(2,1)S(1)}, bf16[64,256]{1,0:T(8,128)(2,1)S(1)}, u32[]{:S(2)}, u32[]{:S(2)}) collective-permute-start(bf16[64,256]{1,0:T(8,128)(2,1)S(1)} %get-tuple-element.44), channel_id=1, source_target_pairs={{0,8},{4,12},{8,0},{12,4},{1,9},{5,13},{9,1},{13,5},{2,10},{6,14},... | collective-permute-start | bytes 98312 | tf_op jit(solution)/shard_map/ppermute | solution.py:413
  36.4 3.4 %collective-permute-start.13 = (bf16[64,256]{1,0:T(8,128)(2,1)S(1)}, bf16[64,256]{1,0:T(8,128)(2,1)S(1)}, u32[]{:S(2)}, u32[]{:S(2)}) collective-permute-start(bf16[64,256]{1,0:T(8,128)(2,1)S(1)} %get-tuple-element.45), channel_id=1, source_target_pairs={{0,12},{4,8},{8,4},{12,0},{1,13},{5,9},{9,5},{13,1},{2,14},{6,10},... | collective-permute-start | bytes 98312 | tf_op jit(solution)/shard_map/ppermute | solution.py:413

commit v3 on v2

--- a/solution.py
+++ b/solution.py
@@ -133,9 +133,11 @@
     return _dot(a, b, ((1,), (0,)))
 
 
-_COST = pl.CostEstimate(flops=1, bytes_accessed=1, transcendentals=0)
-
-_LONG = pl.CostEstimate(flops=3_000_000_000, bytes_accessed=1, transcendentals=0)
+LOG2_E = 1.4426950408889634
+
+
+def _cost(flops):
+    return pl.CostEstimate(flops=flops, bytes_accessed=1, transcendentals=0)
 
 
 def _params(mib=24):
@@ -147,14 +149,14 @@
     scores = _nt(q, k)
     change = _nt(jnp.concatenate([dq, q], axis=1), jnp.concatenate([k, dk], axis=1))
     peak = jnp.max(scores, axis=1, keepdims=True)
-    weights = jnp.exp((scores - peak) * scaling)
-    mixed = weights * (change * scaling)
+    weights = jnp.exp2((scores - peak) * (scaling * LOG2_E))
+    mixed = weights * change
     total = jnp.sum(weights, axis=1, keepdims=True)
-    shift = jnp.sum(mixed, axis=1, keepdims=True)
+    shift = jnp.sum(mixed, axis=1, keepdims=True) * scaling
     inverse = 1.0 / total
     plain = _nn(weights.astype(jnp.bfloat16), vdv)
     attended = plain[:, :HD] * inverse
-    tangent = _nn(mixed.astype(jnp.bfloat16), v) + plain[:, HD:]
+    tangent = _nn(mixed.astype(jnp.bfloat16), v) * scaling + plain[:, HD:]
     tangent = tangent * inverse - (shift * inverse) * attended
     return attended.astype(jnp.bfloat16), tangent.astype(jnp.bfloat16)
 
@@ -203,7 +205,7 @@
         out_specs=[pl.BlockSpec(memory_space=pl.ANY)] * n_out,
         scratch_shapes=[pltpu.SemaphoreType.DMA((n_copies,))],
         compiler_params=_params(),
-        cost_estimate=_COST,
+        cost_estimate=_cost(1),
         name="pack",
     )(*(pltpu.with_memory_space_constraint(a, pltpu.HBM) for a in arrays))
 
@@ -219,118 +221,136 @@
         c.wait()
 
 
-def _cut(outs, held, me):
-    piece = outs[0].shape[0]
-    for s, out in enumerate(outs):
+def _cut(outs, held):
+    keep, beside, across = outs
+    piece = keep.shape[0]
+    me = lax.axis_index("head")
+    for s, out in enumerate((keep, beside, across.at[0], across.at[1])):
         out[...] = held[pl.ds(pl.multiple_of((me ^ s) * piece, piece), piece), :]
 
 
-def whole_head(own, received, done, g, which, n_head):
+def _cut_shapes(rows, width):
+    piece = rows // 4
+    return [
+        jax.ShapeDtypeStruct((*lead, piece, width), jnp.bfloat16) for lead in ((), (), (2,))
+    ]
+
+
+def _sources(keep, beside, across):
+    return keep, beside.at[0], across.at[0], beside.at[1]
+
+
+def join(piece, pair):
+    def kernel(piece, pair, out):
+        out[0] = piece[...]
+        out[1] = pair[1]
+
+    vmem = pl.BlockSpec(memory_space=pltpu.VMEM)
+    return pl.pallas_call(
+        kernel,
+        out_shape=jax.ShapeDtypeStruct(pair.shape, pair.dtype),
+        in_specs=[vmem] * 2,
+        out_specs=vmem,
+        compiler_params=_params(),
+        cost_estimate=_cost(500_000_000),
+        name="join",
+    )(piece, pair)
+
+
+def whole_head(own, received, g, which, near_too):
     rows = own[0].shape[0]
-    piece = rows // n_head
     n = len(own)
-    width = (which + 1) * HD
-    last = which == g - 1
-    n_far = n_head if last else 1
-
-    def kernel(*refs):
-        ins, got, before = refs[:n], refs[n], refs[n + 1 : n + 1 + len(done)]
-        near, *far, mine, held, sems = refs[n + 1 + len(done) :]
-        head = lax.axis_index("blk") * g + which
-        _copy_in([(ins[a].at[:, _col(head)], mine.at[a]) for a in range(n)], sems)
-        k, dk, v, dv = (
-            jnp.concatenate([mine[a], got[a]], axis=0) for a in (2, 3, 4, 5)
+    width = (4 if near_too else 2) * HD
+
+    def kernel(*refs):
+        ins, got, outs, rest = refs[:n], refs[n], refs[n + 1 : n + 4], refs[n + 4 :]
+        held = rest[-1]
+        at = _col(lax.axis_index("blk") * g + which)
+        mine = [ref[:, at] for ref in ins]
+        q, dq, k, dk, v, dv = (
+            jnp.concatenate([mine[a], got[a]], axis=0) for a in range(n)
         )
-        vdv = jnp.concatenate([v, dv], axis=1)
-        targets = (near, held if last else far[0])
-        for block, source in enumerate((mine, got)):
-            result = _one_block(source[0], source[1], k, dk, v, vdv)
-            out = targets[block]
-            for o in range(2):
-                if done:
-                    old = before[block][:, o * which * HD : (o + 1) * which * HD]
-                    out[:, o * width : o * width + which * HD] = old
-                out[:, (o + 1) * width - HD : (o + 1) * width] = result[o]
-        if last:
-            _cut(far, held, lax.axis_index("head"))
+        result = _one_block(q, dq, k, dk, v, jnp.concatenate([v, dv], axis=1))
+        for o in range(2):
+            near, far = result[o][:rows], result[o][rows:]
+            held[:, width - (2 - o) * HD : width - (1 - o) * HD] = far
+            (held if near_too else rest[0])[:, o * HD : (o + 1) * HD] = near
+        _cut(outs, held)
 
     vmem = pl.BlockSpec(memory_space=pltpu.VMEM)
-    far_rows = piece if last else rows
-    return pl.pallas_call(
-        kernel,
-        out_shape=[jax.ShapeDtypeStruct((rows, 2 * width), jnp.bfloat16)]
-        + [jax.ShapeDtypeStruct((far_rows, 2 * width), jnp.bfloat16)] * n_far,
-        in_specs=[pl.BlockSpec(memory_space=pl.ANY)] * n + [vmem] * (1 + len(done)),
-        out_specs=[vmem] * (1 + n_far),
-        scratch_shapes=[
-            pltpu.VMEM((n, rows, HD), jnp.bfloat16),
-            pltpu.VMEM((rows, 2 * width), jnp.bfloat16),
-            pltpu.SemaphoreType.DMA((n,)),
-        ],
-        compiler_params=_params(),
-        cost_estimate=_COST,
+    shapes = _cut_shapes(rows, width)
+    if not near_too:
+        shapes.append(jax.ShapeDtypeStruct((rows, 2 * HD), jnp.bfloat16))
+    return pl.pallas_call(
+        kernel,
+        out_shape=shapes,
+        in_specs=[vmem] * (n + 1),
+        out_specs=[vmem] * len(shapes),
+        scratch_shapes=[pltpu.VMEM((rows, width), jnp.bfloat16)],
+        compiler_params=_params(),
+        cost_estimate=_cost((500_000_000, 2_000_000_000)[which]),
         name="whole_head",
-    )(*own, received, *done)
-
-
-def shared_head(own, received, done, which, n_head, cost=_COST):
+    )(*own, received)
+
+
+def shared_head(own, received, done, which):
     rows = own[0].shape[0]
-    piece = rows // n_head
-    n = len(own)
-    before = sum(d.shape[1] for d in done) // 2
-    width = before + HD
-
-    def kernel(*refs):
-        ins, got, rest = refs[:n], refs[n], refs[n + 1 :]
-        old, outs = rest[: len(done)], rest[len(done) : len(done) + n_head]
-        mine, held, sems = rest[len(done) + n_head :]
-        at = pl.ds(which * HD, HD)
-        _copy_in([(ins[a].at[:, at], mine.at[a]) for a in range(n)], sems)
+    n, m = len(own), len(done)
+    width = (m + 1) * HD
+
+    def kernel(*refs):
+        ins, got, old = refs[:n], refs[n], refs[n + 1 : n + 1 + m]
+        outs, held = refs[n + 1 + m : n + 4 + m], refs[-1]
+        mine = [ref[:, which * HD : (which + 1) * HD] for ref in ins]
         k, dk, v, dv = (
             jnp.concatenate([mine[2 + a], got[a]], axis=0) for a in range(4)
         )
         result = _one_block(mine[0], mine[1], k, dk, v, jnp.concatenate([v, dv], axis=1))
         for o in range(2):
-            if done:
-                held[:, o * width : o * width + before] = old[0][
-                    :, o * before : (o + 1) * before
+            for i in range(m):
+                held[:, o * width + i * HD : o * width + (i + 1) * HD] = old[i][
+                    :, o * HD : (o + 1) * HD
                 ]
             held[:, (o + 1) * width - HD : (o + 1) * width] = result[o]
-        _cut(outs, held, lax.axis_index("head"))
+        _cut(outs, held)
 
     vmem = pl.BlockSpec(memory_space=pltpu.VMEM)
     return pl.pallas_call(
         kernel,
-        out_shape=[jax.ShapeDtypeStruct((piece, 2 * width), jnp.bfloat16)] * n_head,
-        in_specs=[pl.BlockSpec(memory_space=pl.ANY)] * n + [vmem] * (1 + len(done)),
-        out_specs=[vmem] * n_head,
-        scratch_shapes=[
-            pltpu.VMEM((n, rows, HD), jnp.bfloat16),
-            pltpu.VMEM((rows, 2 * width), jnp.bfloat16),
-            pltpu.SemaphoreType.DMA((n,)),
-        ],
-        compiler_params=_params(),
-        cost_estimate=cost,
+        out_shape=_cut_shapes(rows, 2 * width),
+        in_specs=[vmem] * (n + 1 + m),
+        out_specs=[vmem] * 3,
+        scratch_shapes=[pltpu.VMEM((rows, 2 * width), jnp.bfloat16)],
+        compiler_params=_params(),
+        cost_estimate=_cost((3_000_000_000, 2_000_000_000)[which % 2]),
         name="shared_head",
     )(*own, received, *done)
 
 
-def gather_far(pieces):
-    n = len(pieces)
-
-    def kernel(*refs):
-        _copy_in([(refs[s], refs[n].at[s]) for s in range(n)], refs[n + 1])
-
-    return pl.pallas_call(
-        kernel,
-        out_shape=jax.ShapeDtypeStruct((n, *pieces[0].shape), jnp.bfloat16),
-        in_specs=[pl.BlockSpec(memory_space=pl.ANY)] * n,
-        out_specs=pl.BlockSpec(memory_space=pl.ANY),
-        scratch_shapes=[pltpu.SemaphoreType.DMA((n,))],
-        compiler_params=_params(),
-        cost_estimate=_COST,
+def gather_far(first, second):
+    piece = first[0].shape[0]
+
+    def kernel(*refs):
+        firsts, seconds, out = _sources(*refs[:3]), _sources(*refs[3:6]), refs[6]
+        for s in range(4):
+            for o in range(2):
+                out[s, :, 2 * o * HD : (2 * o + 1) * HD] = firsts[s][
+                    :, (2 + o) * HD : (3 + o) * HD
+                ]
+                out[s, :, (2 * o + 1) * HD : (2 * o + 2) * HD] = seconds[s][
+                    :, o * HD : (o + 1) * HD
+                ]
+
+    vmem = pl.BlockSpec(memory_space=pltpu.VMEM)
+    return pl.pallas_call(
+        kernel,
+        out_shape=jax.ShapeDtypeStruct((4, piece, 4 * HD), jnp.bfloat16),
+        in_specs=[vmem] * 6,
+        out_specs=vmem,
+        compiler_params=_params(),
+        cost_estimate=_cost(500_000_000),
         name="gather_far",
-    )(*pieces)
+    )(*first, *second)
 
 
 def _place(copies, outs, source, o, column, heads):
@@ -338,70 +358,66 @@
     copies.append((source, outs[o].at[:, at]))
 
 
-def place_near(pieces, g, heads):
-    n = len(pieces)
-    piece, twice = pieces[0].shape
-    width = twice // 2
-
-    def kernel(*refs):
-        ins, outs, sems = refs[:n], refs[n : n + 2], refs[n + 2]
+def place_near(first, second, g, heads):
+    piece = first[0].shape[0]
+
+    def kernel(*refs):
+        firsts, seconds, outs, sems = _sources(*refs[:3]), _sources(*refs[3:6]), refs[6:8], refs[8]
         me, blk = lax.axis_index("head"), lax.axis_index("blk")
         copies = []
-        for s in range(n):
-            first = (me ^ s) * heads
+        for s in range(4):
+            start = (me ^ s) * heads
             for o in range(2):
-                whole = ins[s].at[:, pl.ds(o * width, g * HD)]
-                _place(copies, outs, whole, o, first + blk * g, g)
-                if g > 1:
-                    rest = ins[s].at[:, pl.ds(o * width + g * HD, (g - 1) * HD)]
-                    _place(copies, outs, rest, o, first + 2 * g, g - 1)
+                lanes = firsts[s].at[:, pl.ds(o * HD, HD)]
+                _place(copies, outs, lanes, o, start + blk * g, 1)
+                for i, column in enumerate((start + blk * g + 1, start + 2 * g)):
+                    lanes = seconds[s].at[:, pl.ds((2 * o + i) * HD, HD)]
+                    _place(copies, outs, lanes, o, column, 1)
         _copy_in(copies, sems)
 
-    full = jax.ShapeDtypeStruct((piece, n * heads * HD), jnp.bfloat16)
+    full = jax.ShapeDtypeStruct((piece, 4 * heads * HD), jnp.bfloat16)
     return pl.pallas_call(
         kernel,
         out_shape=[full] * 2,
-        in_specs=[pl.BlockSpec(memory_space=pl.ANY)] * n,
+        in_specs=[pl.BlockSpec(memory_space=pl.ANY)] * 6,
         out_specs=[pl.BlockSpec(memory_space=pltpu.HBM)] * 2,
-        scratch_shapes=[pltpu.SemaphoreType.DMA((4 * n,))],
-        compiler_params=_params(),
-        cost_estimate=_COST,
+        scratch_shapes=[pltpu.SemaphoreType.DMA((24,))],
+        compiler_params=_params(),
+        cost_estimate=_cost(1),
         name="place_near",
-    )(*pieces)
+    )(*first, *second)
 
 
 def place_last(outputs, crossed, last, g, heads):
-    n = len(last)
-
-    def kernel(*refs):
-        far, ours, outs, sems = refs[2], refs[3 : 3 + n], refs[-3:-1], refs[-1]
+    def kernel(*refs):
+        far, ours, outs, sems = refs[2], _sources(*refs[3:6]), refs[6:8], refs[8]
         me, blk = lax.axis_index("head"), lax.axis_index("blk")
         width = g * HD
         copies = []
-        for s in range(n):
-            first = (me ^ s) * heads
+        for s in range(4):
+            start = (me ^ s) * heads
             for o in range(2):
                 whole = far.at[s, :, pl.ds(o * width, width)]
-                _place(copies, outs, whole, o, first + (1 - blk) * g, g)
+                _place(copies, outs, whole, o, start + (1 - blk) * g, g)
                 rest = ours[s].at[:, pl.ds(o * HD, HD)]
-                _place(copies, outs, rest, o, first + 3 * g - 1, 1)
+                _place(copies, outs, rest, o, start + 3 * g - 1, 1)
         _copy_in(copies, sems)
 
     return pl.pallas_call(
         kernel,
         out_shape=[jax.ShapeDtypeStruct(o.shape, o.dtype) for o in outputs],
         in_specs=[pl.BlockSpec(memory_space=pltpu.HBM)] * 2
-        + [pl.BlockSpec(memory_space=pl.ANY)] * (1 + n),
+        + [pl.BlockSpec(memory_space=pl.ANY)] * 4,
         out_specs=[pl.BlockSpec(memory_space=pltpu.HBM)] * 2,
-        scratch_shapes=[pltpu.SemaphoreType.DMA((4 * n,))],
+        scratch_shapes=[pltpu.SemaphoreType.DMA((16,))],
         input_output_aliases={0: 0, 1: 1},
         compiler_params=_params(),
-        cost_estimate=_COST,
+        cost_estimate=_cost(1),
         name="place_last",
     )(*(pltpu.with_memory_space_constraint(o, pltpu.HBM) for o in outputs), crossed, *last)
 
 
-def paired(n_head, query_rows, key_rows, value_rows, query_tangent, key_tangent, value_tangent):
+def paired(query_rows, key_rows, value_rows, query_tangent, key_tangent, value_tangent):
     heads = query_rows.shape[1] // HD
     g = heads // 3
     own = (query_rows, query_tangent, key_rows, key_tangent, value_rows, value_tangent)
@@ -410,29 +426,24 @@
         return lax.ppermute(x, "blk", [(0, 1), (1, 0)])
 
     def along(x, s):
-        return lax.ppermute(x, "head", [(i, i ^ s) for i in range(n_head)])
+        return lax.ppermute(x, "head", [(i, i ^ s) for i in range(4)])
 
     def spread(parts):
-        return [parts[0]] + [along(parts[s], s) for s in range(1, n_head)]
+        keep, beside, across = parts
+        across = along(across, 2)
+        return keep, along(join(beside, across), 1), across
 
     first = pack(own, g, [0], [])
-    rest = pack(own, g, list(range(1, g)), list(range(g)))
-    whole_in = [cross(p) for p in first + rest[: g - 1]]
-    shared_in = [cross(p) for p in rest[g - 1 :]]
-    done = ()
-    for i in range(g):
-        near, *far = whole_head(own, whole_in[i], done, g, i, n_head)
-        done = (near, *far)
-    far = gather_far(spread(far))
-    done = (near,)
-    for i in range(g):
-        parts = list(shared_head(own, shared_in[i], done, 2 * g + i, n_head, _COST if i + 1 < g else _LONG))
-        done = ()
-        if i == 0:
-            far, parts[0] = lax.optimization_barrier((far, parts[0]))
-            crossed = cross(far)
-            outputs = place_near(spread(parts), g, heads)
-    return place_last(outputs, crossed, spread(parts), g, heads)
+    rest = pack(own, g, [1], [0, 1])
+    whole_in = [cross(p) for p in first + rest[:1]]
+    shared_in = [cross(p) for p in rest[1:]]
+    firsts = spread(whole_head(own, whole_in[0], g, 0, True))
+    *seconds, near = whole_head(own, whole_in[1], g, 1, False)
+    far = gather_far(firsts, spread(seconds))
+    parts = list(shared_head(own, shared_in[0], (near,), 2 * g))
+    outputs = place_near(firsts, spread(parts), g, heads)
+    last = spread(shared_head(own, shared_in[1], (), 2 * g + 1))
+    return place_last(outputs, cross(far), last, g, heads)
 
 
 def solution(mesh):
@@ -443,7 +454,7 @@
         rows = arrays[0].shape[0]
         two = mesh.shape["blk"] == 2 and n_head == 4
         if two and heads == 6 and rows % (16 * n_head) == 0:
-            return paired(n_head, *arrays)
+            return paired(*arrays)
         return local(*arrays)
 
     return jax.shard_map(

time: 41.9 us -> 40.8 us (0.974)
  starting transfers between devices: 13.5 us -> 17.2 us
  waiting for transfers between devices: 19 us -> 15.4 us
  Pallas kernels: 8.33 us -> 7.09 us
    ppermute x5, waiting for transfers between devices: 16.7 us -> 12.2 us  [cross(): return lax.ppermute(x, 'blk', [(0, 1), (1, 0)])]
    ppermute x9 -> x8, starting transfers between devices: 6.57 us -> 9.06 us  [along(): return lax.ppermute(x, 'head', [(i, i ^ s) for i in range(4)])]
    pallas_call x5 -> x9, Pallas kernels: 4.18 us -> 2.85 us  [the longest x2 1.64 us: whole_head(): pl.pallas_call(kernel, out_shape=shapes, in_specs=[vmem] * (n + 1), out_s...]
    ppermute x5, starting transfers between devices: 6.96 us -> 8.17 us  [cross(): return lax.ppermute(x, 'blk', [(0, 1), (1, 0)])]
    ppermute x9 -> x8, waiting for transfers between devices: 2.21 us -> 3.21 us  [along(): return lax.ppermute(x, 'head', [(i, i ^ s) for i in range(4)])]
  transfers between devices with their start and end apart: 14 -> 13, of which waited for: 7 -> 6; matrix products, arithmetic and copies ran while one was open for 0% -> 0% of each run, Pallas kernels for 15% -> 13%
where the time goes in v3:
time: 40.8 us; the launch traced here: 40.6 us
  starting transfers between devices  17.2 us (42%)
  waiting for transfers between devices  15.4 us (38%)
  Pallas kernels  7.09 us (17%)
  between operations  0.83 us (2%)
    ppermute x5, waiting for transfers between devices, cross(): return lax.ppermute(x, 'blk', [(0, 1), (1, 0)])  12.2 us
    ppermute x8, starting transfers between devices, along(): return lax.ppermute(x, 'head', [(i, i ^ s) for i in range(4)])  9.06 us
    ppermute x5, starting transfers between devices, cross(): return lax.ppermute(x, 'blk', [(0, 1), (1, 0)])  8.17 us
    ppermute x8, waiting for transfers between devices, along(): return lax.ppermute(x, 'head', [(i, i ^ s) for i in range(4)])  3.21 us
    pallas_call x2, Pallas kernels, pack(): pl.pallas_call(kernel, out_shape=[jax.ShapeDtypeStruct(shape, jnp.bfloat1...  2.41 us
    pallas_call x2, Pallas kernels, whole_head(): pl.pallas_call(kernel, out_shape=shapes, in_specs=[vmem] * (n + 1), out_s...  1.64 us
    pallas_call x2, Pallas kernels, shared_head(): pl.pallas_call(kernel, out_shape=_cut_shapes(rows, 2 * width), in_specs=[...  1.13 us
    pallas_call x1, Pallas kernels, place_near(): pl.pallas_call(kernel, out_shape=[full] * 2, in_specs=[pl.BlockSpec(memor...  0.96 us
  transfers between devices with their start and end apart: 13, of which 6 were waited for; matrix products, arithmetic and copies ran while one was open for 0% of the time, Pallas kernels for 13%

profile of v3, /device:TPU:0, one launch (start us, length us, event | category | flops | bytes accessed | tf_op | source)
XLA Modules:
  0.0 40.6 jit_solution(10612889394774349883)
XLA Ops:
  0.6 1.1 %pack.2 = bf16[6,256,128]{2,1,0:T(8,128)(2,1)S(1)} custom-call(bf16[256,768]{1,0:T(8,128)(2,1)} %refs_0_.11, bf16[256,768]{1,0:T(8,128)(2,1)} %refs_1_.11, bf16[256,768]{1,0:T(8,128)(2,1)} %refs_2_.11, bf16[256,768]{1,0:T(8,128)(2,1)} %refs_3_.11, bf16[256,768]{1,0:T(8,128)(2,1)} %refs_4_.11, bf16[256,768]{1,0:T(8,128)(2,1)} %refs_5_.11), custom_call_target="tpu_custom_call" | custom-call | flops 1 | bytes 1 | tf_op jit(solution)/shard_map/pack/pallas_call | solution.py:201
  1.7 0.0 copy-start
  1.7 0.0 copy-start.1
  1.7 0.0 copy-start.2
  1.7 0.0 copy-start.3
  1.8 0.0 copy-start.4
  1.8 0.0 copy-start.5
  1.8 3.0 %collective-permute-start = (bf16[6,256,128]{2,1,0:T(8,128)(2,1)S(1)}, bf16[6,256,128]{2,1,0:T(8,128)(2,1)S(1)}, u32[]{:S(2)}, u32[]{:S(2)}) collective-permute-start(bf16[6,256,128]{2,1,0:T(8,128)(2,1)S(1)} %pack.2), channel_id=1, source_target_pairs={{0,16},{16,0},{1,17},{17,1},{2,18},{18,2},{3,19},{19,3},{4,20},{20... | collective-permute-start | bytes 1179656 | tf_op jit(solution)/shard_map/ppermute | solution.py:426
  4.8 1.3 %pack.3 = (bf16[6,256,128]{2,1,0:T(8,128)(2,1)S(1)}, bf16[4,256,128]{2,1,0:T(8,128)(2,1)S(1)}, bf16[4,256,128]{2,1,0:T(8,128)(2,1)S(1)}) custom-call(bf16[256,768]{1,0:T(8,128)(2,1)} %refs_0_.11, bf16[256,768]{1,0:T(8,128)(2,1)} %refs_1_.11, bf16[256,768]{1,0:T(8,128)(2,1)} %refs_2_.11, bf16[256,768]{1,0:T(8,128)(2,1)} %refs_3_.11, ...), custom_call_target="tpu_custom_call" | custom-call | flops 1 | bytes 1 | tf_op jit(solution)/shard_map/pack/pallas_call | solution.py:201
  6.1 0.2 collective-permute-start.4
  6.4 1.9 %collective-permute-start.3 = (bf16[4,256,128]{2,1,0:T(8,128)(2,1)S(1)}, bf16[4,256,128]{2,1,0:T(8,128)(2,1)S(1)}, u32[]{:S(2)}, u32[]{:S(2)}) collective-permute-start(bf16[4,256,128]{2,1,0:T(8,128)(2,1)S(1)} %get-tuple-element.23), channel_id=1, source_target_pairs={{0,16},{16,0},{1,17},{17,1},{2,18},{18,2},{3,19},{19,3},{4,20},{20... | collective-permute-start | bytes 786440 | tf_op jit(solution)/shard_map/ppermute | solution.py:426
  8.2 6.5 %collective-permute-done.refs_6_ = bf16[6,256,128]{2,1,0:T(8,128)(2,1)S(1)} collective-permute-done((bf16[6,256,128]{2,1,0:T(8,128)(2,1)S(1)}, bf16[6,256,128]{2,1,0:T(8,128)(2,1)S(1)}, u32[]{:S(2)}, u32[]{:S(2)}) %collective-permute-start) | collective-permute-done | bytes 393248 | tf_op jit(solution)/shard_map/ppermute | solution.py:426
  14.7 0.0 copy-done
  14.7 0.0 copy-done.1
  14.7 0.0 copy-done.2
  14.7 0.0 copy-done.3
  14.8 0.0 copy-done.4
  14.8 0.0 copy-done.5
  14.8 0.8 %whole_head.2 = (bf16[64,512]{1,0:T(8,128)(2,1)S(1)}, bf16[64,512]{1,0:T(8,128)(2,1)S(1)}, bf16[2,64,512]{2,1,0:T(8,128)(2,1)S(1)}) custom-call(bf16[256,768]{1,0:T(8,128)(2,1)S(1)} %copy-done, bf16[256,768]{1,0:T(8,128)(2,1)S(1)} %copy-done.1, bf16[256,768]{1,0:T(8,128)(2,1)S(1)} %copy-done.2, bf16[256,768]{1,0:T(8,128)(2,1)S(1)} %copy-done.3, ...), custom_call_target="tpu_custom_call" | custom-call | flops 500000000 | bytes 1 | tf_op jit(solution)/shard_map/whole_head/pallas_call | solution.py:284
  15.6 2.2 %collective-permute-start.1 = (bf16[2,64,512]{2,1,0:T(8,128)(2,1)S(1)}, bf16[2,64,512]{2,1,0:T(8,128)(2,1)S(1)}, u32[]{:S(2)}, u32[]{:S(2)}) collective-permute-start(bf16[2,64,512]{2,1,0:T(8,128)(2,1)S(1)} %get-tuple-element.22), channel_id=1, source_target_pairs={{0,8},{4,12},{8,0},{12,4},{1,9},{5,13},{9,1},{13,5},{2,10},{6,14},... | collective-permute-start | bytes 393224 | tf_op jit(solution)/shard_map/ppermute | solution.py:429
  17.8 5.4 %collective-permute-done.4.refs_6_ = bf16[6,256,128]{2,1,0:T(8,128)(2,1)S(1)} collective-permute-done((bf16[6,256,128]{2,1,0:T(8,128)(2,1)S(1)}, bf16[6,256,128]{2,1,0:T(8,128)(2,1)S(1)}, u32[]{:S(2)}, u32[]{:S(2)}) %collective-permute-start.4) | collective-permute-done | bytes 393248 | tf_op jit(solution)/shard_map/ppermute | solution.py:426
  23.2 0.8 %whole_head.3 = (bf16[64,256]{1,0:T(8,128)(2,1)S(1)}, bf16[64,256]{1,0:T(8,128)(2,1)S(1)}, bf16[2,64,256]{2,1,0:T(8,128)(2,1)S(1)}, bf16[256,256]{1,0:T(8,128)(2,1)S(1)}) custom-call(bf16[256,768]{1,0:T(8,128)(2,1)S(1)} %copy-done, bf16[256,768]{1,0:T(8,128)(2,1)S(1)} %copy-done.1, bf16[256,768]{1,0:T(8,128)(2,1)S(1)} %copy-done.2, ...), custom_call_target="tpu_custom_call" | custom-call | flops 2000000000 | bytes 1 | tf_op jit(solution)/shard_map/whole_head/pallas_call | solution.py:284
  24.0 2.1 %collective-permute-start.7 = (bf16[2,64,256]{2,1,0:T(8,128)(2,1)S(1)}, bf16[2,64,256]{2,1,0:T(8,128)(2,1)S(1)}, u32[]{:S(2)}, u32[]{:S(2)}) collective-permute-start(bf16[2,64,256]{2,1,0:T(8,128)(2,1)S(1)} %get-tuple-element.33), channel_id=1, source_target_pairs={{0,8},{4,12},{8,0},{12,4},{1,9},{5,13},{9,1},{13,5},{2,10},{6,14},... | collective-permute-start | bytes 196616 | tf_op jit(solution)/shard_map/ppermute | solution.py:429
  26.1 1.5 %collective-permute-start.10 = (bf16[4,256,128]{2,1,0:T(8,128)(2,1)S(1)}, bf16[4,256,128]{2,1,0:T(8,128)(2,1)S(1)}, u32[]{:S(2)}, u32[]{:S(2)}) collective-permute-start(bf16[4,256,128]{2,1,0:T(8,128)(2,1)S(1)} %get-tuple-element.34), channel_id=1, source_target_pairs={{0,16},{16,0},{1,17},{17,1},{2,18},{18,2},{3,19},{19,3},{4,20},{20... | collective-permute-start | bytes 786440 | tf_op jit(solution)/shard_map/ppermute | solution.py:426
  27.6 0.7 %collective-permute-done.7.pair.refs_5_ = bf16[2,64,256]{2,1,0:T(8,128)(2,1)S(1)} collective-permute-done((bf16[2,64,256]{2,1,0:T(8,128)(2,1)S(1)}, bf16[2,64,256]{2,1,0:T(8,128)(2,1)S(1)}, u32[]{:S(2)}, u32[]{:S(2)}) %collective-permute-start.7) | collective-permute-done | bytes 65568 | tf_op jit(solution)/shard_map/ppermute | solution.py:429
  28.4 0.0 collective-permute-start.8
  28.4 0.0 collective-permute-done.1.pair.refs_2_
  28.4 0.6 %collective-permute-start.2 = (bf16[2,64,512]{2,1,0:T(8,128)(2,1)S(1)}, bf16[2,64,512]{2,1,0:T(8,128)(2,1)S(1)}, u32[]{:S(2)}, u32[]{:S(2)}) collective-permute-start(bf16[2,64,512]{2,1,0:T(8,128)(2,1)S(1)} %join.4), channel_id=1, source_target_pairs={{0,4},{4,0},{8,12},{12,8},{1,5},{5,1},{9,13},{13,9},{2,6},{6,2},{1... | collective-permute-start | bytes 393224 | tf_op jit(solution)/shard_map/ppermute | solution.py:429
  29.0 0.0 collective-permute-done.3.refs_6_
  29.0 0.6 %shared_head.2 = (bf16[64,512]{1,0:T(8,128)(2,1)S(1)}, bf16[64,512]{1,0:T(8,128)(2,1)S(1)}, bf16[2,64,512]{2,1,0:T(8,128)(2,1)S(1)}) custom-call(bf16[256,768]{1,0:T(8,128)(2,1)S(1)} %copy-done, bf16[256,768]{1,0:T(8,128)(2,1)S(1)} %copy-done.1, bf16[256,768]{1,0:T(8,128)(2,1)S(1)} %copy-done.2, bf16[256,768]{1,0:T(8,128)(2,1)S(1)} %copy-done.3, ...), custom_call_target="tpu_custom_call" | custom-call | flops 3000000000 | bytes 1 | tf_op jit(solution)/shard_map/shared_head/pallas_call | solution.py:318
  29.6 2.1 %collective-permute-start.5 = (bf16[2,64,512]{2,1,0:T(8,128)(2,1)S(1)}, bf16[2,64,512]{2,1,0:T(8,128)(2,1)S(1)}, u32[]{:S(2)}, u32[]{:S(2)}) collective-permute-start(bf16[2,64,512]{2,1,0:T(8,128)(2,1)S(1)} %get-tuple-element.28), channel_id=1, source_target_pairs={{0,8},{4,12},{8,0},{12,4},{1,9},{5,13},{9,1},{13,5},{2,10},{6,14},... | collective-permute-start | bytes 393224 | tf_op jit(solution)/shard_map/ppermute | solution.py:429
  31.6 0.0 collective-permute-done.8.refs_4_
  31.6 0.0 collective-permute-done.2.refs_1_
  31.7 1.6 %collective-permute-start.9 = (bf16[4,64,512]{2,1,0:T(8,128)(2,1)S(1)}, bf16[4,64,512]{2,1,0:T(8,128)(2,1)S(1)}, u32[]{:S(2)}, u32[]{:S(2)}) collective-permute-start(bf16[4,64,512]{2,1,0:T(8,128)(2,1)S(1)} %gather_far.1), channel_id=1, source_target_pairs={{0,16},{16,0},{1,17},{17,1},{2,18},{18,2},{3,19},{19,3},{4,20},{20... | collective-permute-start | bytes 786440 | tf_op jit(solution)/shard_map/ppermute | solution.py:426
  33.3 0.3 collective-permute-done.10.refs_6_
  33.6 0.6 %shared_head.3 = (bf16[64,256]{1,0:T(8,128)(2,1)S(1)}, bf16[64,256]{1,0:T(8,128)(2,1)S(1)}, bf16[2,64,256]{2,1,0:T(8,128)(2,1)S(1)}) custom-call(bf16[256,768]{1,0:T(8,128)(2,1)S(1)} %copy-done, bf16[256,768]{1,0:T(8,128)(2,1)S(1)} %copy-done.1, bf16[256,768]{1,0:T(8,128)(2,1)S(1)} %copy-done.2, bf16[256,768]{1,0:T(8,128)(2,1)S(1)} %copy-done.3, ...), custom_call_target="tpu_custom_call" | custom-call | flops 2000000000 | bytes 1 | tf_op jit(solution)/shard_map/shared_head/pallas_call | solution.py:318
  34.1 2.0 %collective-permute-start.11 = (bf16[2,64,256]{2,1,0:T(8,128)(2,1)S(1)}, bf16[2,64,256]{2,1,0:T(8,128)(2,1)S(1)}, u32[]{:S(2)}, u32[]{:S(2)}) collective-permute-start(bf16[2,64,256]{2,1,0:T(8,128)(2,1)S(1)} %get-tuple-element.37), channel_id=1, source_target_pairs={{0,8},{4,12},{8,0},{12,4},{1,9},{5,13},{9,1},{13,5},{2,10},{6,14},... | collective-permute-start | bytes 196616 | tf_op jit(solution)/shard_map/ppermute | solution.py:429
  36.2 0.0 collective-permute-done.5.pair.refs_5_
  36.2 0.1 collective-permute-start.6
  36.3 2.2 %collective-permute-done.11.pair.refs_5_ = bf16[2,64,256]{2,1,0:T(8,128)(2,1)S(1)} collective-permute-done((bf16[2,64,256]{2,1,0:T(8,128)(2,1)S(1)}, bf16[2,64,256]{2,1,0:T(8,128)(2,1)S(1)}, u32[]{:S(2)}, u32[]{:S(2)}) %collective-permute-start.11) | collective-permute-done | bytes 65568 | tf_op jit(solution)/shard_map/ppermute | solution.py:429
  38.5 0.0 collective-permute-start.12
  38.5 0.0 collective-permute-done.6.refs_4_
  38.5 1.0 %place_near.1 = (bf16[64,3072]{1,0:T(8,128)(2,1)}, bf16[64,3072]{1,0:T(8,128)(2,1)}) custom-call(bf16[64,512]{1,0:T(8,128)(2,1)S(1)} %get-tuple-element.20.refs_0_, bf16[2,64,512]{2,1,0:T(8,128)(2,1)S(1)} %collective-permute-done.2.refs_1_, bf16[2,64,512]{2,1,0:T(8,128)(2,1)S(1)} %collective-permute-done.1.pair.refs_2_, ...), custom_call_target="tpu_custom_call" | custom-call | flops 1 | bytes 1 | tf_op jit(solution)/shard_map/place_near/pallas_call | solution.py:379
  39.4 0.3 collective-permute-done.12.refs_4_
  39.7 0.0 collective-permute-done.9.refs_2_
  39.7 0.9 %place_last.1 = (bf16[64,3072]{1,0:T(8,128)(2,1)}, bf16[64,3072]{1,0:T(8,128)(2,1)}) custom-call(bf16[64,3072]{1,0:T(8,128)(2,1)} %get-tuple-element.29.refs_0_, bf16[64,3072]{1,0:T(8,128)(2,1)} %get-tuple-element.30.refs_1_, bf16[4,64,512]{2,1,0:T(8,128)(2,1)S(1)} %collective-permute-done.9.refs_2_, ...), custom_call_target="tpu_custom_call", output_to_operand_aliasing={{0}: (0, {}), {1}: (1, {})} | custom-call | flops 1 | bytes 1 | tf_op jit(solution)/shard_map/place_last/pallas_call | solution.py:406
  (5 shorter events, 0.1 us)
Async XLA Ops:
  1.7 13.0 %copy-start = (bf16[256,768]{1,0:T(8,128)(2,1)S(1)}, bf16[256,768]{1,0:T(8,128)(2,1)}, u32[]{:S(2)}) copy-start(bf16[256,768]{1,0:T(8,128)(2,1)} %refs_0_.11) | copy-start | bytes 1179652
  1.7 13.0 %copy-start.1 = (bf16[256,768]{1,0:T(8,128)(2,1)S(1)}, bf16[256,768]{1,0:T(8,128)(2,1)}, u32[]{:S(2)}) copy-start(bf16[256,768]{1,0:T(8,128)(2,1)} %refs_1_.11) | copy-start | bytes 1179652
  1.7 13.0 %copy-start.2 = (bf16[256,768]{1,0:T(8,128)(2,1)S(1)}, bf16[256,768]{1,0:T(8,128)(2,1)}, u32[]{:S(2)}) copy-start(bf16[256,768]{1,0:T(8,128)(2,1)} %refs_2_.11) | copy-start | bytes 1179652
  1.7 13.0 %copy-start.3 = (bf16[256,768]{1,0:T(8,128)(2,1)S(1)}, bf16[256,768]{1,0:T(8,128)(2,1)}, u32[]{:S(2)}) copy-start(bf16[256,768]{1,0:T(8,128)(2,1)} %refs_3_.11) | copy-start | bytes 1179652
  1.8 13.0 %copy-start.4 = (bf16[256,768]{1,0:T(8,128)(2,1)S(1)}, bf16[256,768]{1,0:T(8,128)(2,1)}, u32[]{:S(2)}) copy-start(bf16[256,768]{1,0:T(8,128)(2,1)} %refs_4_.11) | copy-start | bytes 1179652
  1.8 13.0 %copy-start.5 = (bf16[256,768]{1,0:T(8,128)(2,1)S(1)}, bf16[256,768]{1,0:T(8,128)(2,1)}, u32[]{:S(2)}) copy-start(bf16[256,768]{1,0:T(8,128)(2,1)} %refs_5_.11) | copy-start | bytes 1179652
  1.8 12.9 %collective-permute-start = (bf16[6,256,128]{2,1,0:T(8,128)(2,1)S(1)}, bf16[6,256,128]{2,1,0:T(8,128)(2,1)S(1)}, u32[]{:S(2)}, u32[]{:S(2)}) collective-permute-start(bf16[6,256,128]{2,1,0:T(8,128)(2,1)S(1)} %pack.2), channel_id=1, source_target_pairs={{0,16},{16,0},{1,17},{17,1},{2,18},{18,2},{3,19},{19,3},{4,20},{20... | collective-permute-start | bytes 1179656 | tf_op jit(solution)/shard_map/ppermute | solution.py:426
  6.1 17.0 %collective-permute-start.4 = (bf16[6,256,128]{2,1,0:T(8,128)(2,1)S(1)}, bf16[6,256,128]{2,1,0:T(8,128)(2,1)S(1)}, u32[]{:S(2)}, u32[]{:S(2)}) collective-permute-start(bf16[6,256,128]{2,1,0:T(8,128)(2,1)S(1)} %get-tuple-element.24), channel_id=1, source_target_pairs={{0,16},{16,0},{1,17},{17,1},{2,18},{18,2},{3,19},{19,3},{4,20},{20... | collective-permute-start | bytes 1179656 | tf_op jit(solution)/shard_map/ppermute | solution.py:426
  6.4 22.6 %collective-permute-start.3 = (bf16[4,256,128]{2,1,0:T(8,128)(2,1)S(1)}, bf16[4,256,128]{2,1,0:T(8,128)(2,1)S(1)}, u32[]{:S(2)}, u32[]{:S(2)}) collective-permute-start(bf16[4,256,128]{2,1,0:T(8,128)(2,1)S(1)} %get-tuple-element.23), channel_id=1, source_target_pairs={{0,16},{16,0},{1,17},{17,1},{2,18},{18,2},{3,19},{19,3},{4,20},{20... | collective-permute-start | bytes 786440 | tf_op jit(solution)/shard_map/ppermute | solution.py:426
  15.6 12.8 %collective-permute-start.1 = (bf16[2,64,512]{2,1,0:T(8,128)(2,1)S(1)}, bf16[2,64,512]{2,1,0:T(8,128)(2,1)S(1)}, u32[]{:S(2)}, u32[]{:S(2)}) collective-permute-start(bf16[2,64,512]{2,1,0:T(8,128)(2,1)S(1)} %get-tuple-element.22), channel_id=1, source_target_pairs={{0,8},{4,12},{8,0},{12,4},{1,9},{5,13},{9,1},{13,5},{2,10},{6,14},... | collective-permute-start | bytes 393224 | tf_op jit(solution)/shard_map/ppermute | solution.py:429
  24.0 4.4 %collective-permute-start.7 = (bf16[2,64,256]{2,1,0:T(8,128)(2,1)S(1)}, bf16[2,64,256]{2,1,0:T(8,128)(2,1)S(1)}, u32[]{:S(2)}, u32[]{:S(2)}) collective-permute-start(bf16[2,64,256]{2,1,0:T(8,128)(2,1)S(1)} %get-tuple-element.33), channel_id=1, source_target_pairs={{0,8},{4,12},{8,0},{12,4},{1,9},{5,13},{9,1},{13,5},{2,10},{6,14},... | collective-permute-start | bytes 196616 | tf_op jit(solution)/shard_map/ppermute | solution.py:429
  26.1 7.4 %collective-permute-start.10 = (bf16[4,256,128]{2,1,0:T(8,128)(2,1)S(1)}, bf16[4,256,128]{2,1,0:T(8,128)(2,1)S(1)}, u32[]{:S(2)}, u32[]{:S(2)}) collective-permute-start(bf16[4,256,128]{2,1,0:T(8,128)(2,1)S(1)} %get-tuple-element.34), channel_id=1, source_target_pairs={{0,16},{16,0},{1,17},{17,1},{2,18},{18,2},{3,19},{19,3},{4,20},{20... | collective-permute-start | bytes 786440 | tf_op jit(solution)/shard_map/ppermute | solution.py:426
  28.4 3.3 %collective-permute-start.8 = (bf16[2,64,256]{2,1,0:T(8,128)(2,1)S(1)}, bf16[2,64,256]{2,1,0:T(8,128)(2,1)S(1)}, u32[]{:S(2)}, u32[]{:S(2)}) collective-permute-start(bf16[2,64,256]{2,1,0:T(8,128)(2,1)S(1)} %join.6), channel_id=1, source_target_pairs={{0,4},{4,0},{8,12},{12,8},{1,5},{5,1},{9,13},{13,9},{2,6},{6,2},{1... | collective-permute-start | bytes 196616 | tf_op jit(solution)/shard_map/ppermute | solution.py:429
  28.4 3.2 %collective-permute-start.2 = (bf16[2,64,512]{2,1,0:T(8,128)(2,1)S(1)}, bf16[2,64,512]{2,1,0:T(8,128)(2,1)S(1)}, u32[]{:S(2)}, u32[]{:S(2)}) collective-permute-start(bf16[2,64,512]{2,1,0:T(8,128)(2,1)S(1)} %join.4), channel_id=1, source_target_pairs={{0,4},{4,0},{8,12},{12,8},{1,5},{5,1},{9,13},{13,9},{2,6},{6,2},{1... | collective-permute-start | bytes 393224 | tf_op jit(solution)/shard_map/ppermute | solution.py:429
  29.6 6.6 %collective-permute-start.5 = (bf16[2,64,512]{2,1,0:T(8,128)(2,1)S(1)}, bf16[2,64,512]{2,1,0:T(8,128)(2,1)S(1)}, u32[]{:S(2)}, u32[]{:S(2)}) collective-permute-start(bf16[2,64,512]{2,1,0:T(8,128)(2,1)S(1)} %get-tuple-element.28), channel_id=1, source_target_pairs={{0,8},{4,12},{8,0},{12,4},{1,9},{5,13},{9,1},{13,5},{2,10},{6,14},... | collective-permute-start | bytes 393224 | tf_op jit(solution)/shard_map/ppermute | solution.py:429
  31.7 8.0 %collective-permute-start.9 = (bf16[4,64,512]{2,1,0:T(8,128)(2,1)S(1)}, bf16[4,64,512]{2,1,0:T(8,128)(2,1)S(1)}, u32[]{:S(2)}, u32[]{:S(2)}) collective-permute-start(bf16[4,64,512]{2,1,0:T(8,128)(2,1)S(1)} %gather_far.1), channel_id=1, source_target_pairs={{0,16},{16,0},{1,17},{17,1},{2,18},{18,2},{3,19},{19,3},{4,20},{20... | collective-permute-start | bytes 786440 | tf_op jit(solution)/shard_map/ppermute | solution.py:426
  34.1 4.3 %collective-permute-start.11 = (bf16[2,64,256]{2,1,0:T(8,128)(2,1)S(1)}, bf16[2,64,256]{2,1,0:T(8,128)(2,1)S(1)}, u32[]{:S(2)}, u32[]{:S(2)}) collective-permute-start(bf16[2,64,256]{2,1,0:T(8,128)(2,1)S(1)} %get-tuple-element.37), channel_id=1, source_target_pairs={{0,8},{4,12},{8,0},{12,4},{1,9},{5,13},{9,1},{13,5},{2,10},{6,14},... | collective-permute-start | bytes 196616 | tf_op jit(solution)/shard_map/ppermute | solution.py:429
  36.2 2.3 %collective-permute-start.6 = (bf16[2,64,512]{2,1,0:T(8,128)(2,1)S(1)}, bf16[2,64,512]{2,1,0:T(8,128)(2,1)S(1)}, u32[]{:S(2)}, u32[]{:S(2)}) collective-permute-start(bf16[2,64,512]{2,1,0:T(8,128)(2,1)S(1)} %join.5), channel_id=1, source_target_pairs={{0,4},{4,0},{8,12},{12,8},{1,5},{5,1},{9,13},{13,9},{2,6},{6,2},{1... | collective-permute-start | bytes 393224 | tf_op jit(solution)/shard_map/ppermute | solution.py:429
  38.5 1.3 %collective-permute-start.12 = (bf16[2,64,256]{2,1,0:T(8,128)(2,1)S(1)}, bf16[2,64,256]{2,1,0:T(8,128)(2,1)S(1)}, u32[]{:S(2)}, u32[]{:S(2)}) collective-permute-start(bf16[2,64,256]{2,1,0:T(8,128)(2,1)S(1)} %join.7), channel_id=1, source_target_pairs={{0,4},{4,0},{8,12},{12,8},{1,5},{5,1},{9,13},{13,9},{2,6},{6,2},{1... | collective-permute-start | bytes 196616 | tf_op jit(solution)/shard_map/ppermute | solution.py:429

commit v4 on v3

--- a/solution.py
+++ b/solution.py
@@ -150,13 +150,13 @@
     change = _nt(jnp.concatenate([dq, q], axis=1), jnp.concatenate([k, dk], axis=1))
     peak = jnp.max(scores, axis=1, keepdims=True)
     weights = jnp.exp2((scores - peak) * (scaling * LOG2_E))
-    mixed = weights * change
+    mixed = weights * (change * scaling)
     total = jnp.sum(weights, axis=1, keepdims=True)
-    shift = jnp.sum(mixed, axis=1, keepdims=True) * scaling
+    shift = jnp.sum(mixed, axis=1, keepdims=True)
     inverse = 1.0 / total
     plain = _nn(weights.astype(jnp.bfloat16), vdv)
     attended = plain[:, :HD] * inverse
-    tangent = _nn(mixed.astype(jnp.bfloat16), v) * scaling + plain[:, HD:]
+    tangent = _nn(mixed.astype(jnp.bfloat16), v) + plain[:, HD:]
     tangent = tangent * inverse - (shift * inverse) * attended
     return attended.astype(jnp.bfloat16), tangent.astype(jnp.bfloat16)
 

time: 40.8 us -> 40.9 us (level)
  no operation moved by 1% of the time
where the time goes in v4:
time: 40.9 us; the launch traced here: 40.7 us
  starting transfers between devices  17.2 us (42%)
  waiting for transfers between devices  15.4 us (38%)
  Pallas kernels  7.17 us (18%)
  between operations  0.83 us (2%)
    ppermute x5, waiting for transfers between devices, cross(): return lax.ppermute(x, 'blk', [(0, 1), (1, 0)])  12.2 us
    ppermute x8, starting transfers between devices, along(): return lax.ppermute(x, 'head', [(i, i ^ s) for i in range(4)])  9.04 us
    ppermute x5, starting transfers between devices, cross(): return lax.ppermute(x, 'blk', [(0, 1), (1, 0)])  8.15 us
    ppermute x8, waiting for transfers between devices, along(): return lax.ppermute(x, 'head', [(i, i ^ s) for i in range(4)])  3.25 us
    pallas_call x2, Pallas kernels, pack(): pl.pallas_call(kernel, out_shape=[jax.ShapeDtypeStruct(shape, jnp.bfloat1...  2.41 us
    pallas_call x2, Pallas kernels, whole_head(): pl.pallas_call(kernel, out_shape=shapes, in_specs=[vmem] * (n + 1), out_s...  1.71 us
    pallas_call x2, Pallas kernels, shared_head(): pl.pallas_call(kernel, out_shape=_cut_shapes(rows, 2 * width), in_specs=[...  1.15 us
    pallas_call x1, Pallas kernels, place_near(): pl.pallas_call(kernel, out_shape=[full] * 2, in_specs=[pl.BlockSpec(memor...  0.96 us
  transfers between devices with their start and end apart: 13, of which 6 were waited for; matrix products, arithmetic and copies ran while one was open for 0% of the time, Pallas kernels for 13%

profile of v4, /device:TPU:0, one launch (start us, length us, event | category | flops | bytes accessed | tf_op | source)
XLA Modules:
  0.0 40.7 jit_solution(9584397197665394275)
XLA Ops:
  0.6 1.1 %pack.2 = bf16[6,256,128]{2,1,0:T(8,128)(2,1)S(1)} custom-call(bf16[256,768]{1,0:T(8,128)(2,1)} %refs_0_.11, bf16[256,768]{1,0:T(8,128)(2,1)} %refs_1_.11, bf16[256,768]{1,0:T(8,128)(2,1)} %refs_2_.11, bf16[256,768]{1,0:T(8,128)(2,1)} %refs_3_.11, bf16[256,768]{1,0:T(8,128)(2,1)} %refs_4_.11, bf16[256,768]{1,0:T(8,128)(2,1)} %refs_5_.11), custom_call_target="tpu_custom_call" | custom-call | flops 1 | bytes 1 | tf_op jit(solution)/shard_map/pack/pallas_call | solution.py:201
  1.7 0.0 copy-start
  1.7 0.0 copy-start.1
  1.7 0.0 copy-start.2
  1.7 0.0 copy-start.3
  1.8 0.0 copy-start.4
  1.8 0.0 copy-start.5
  1.8 3.0 %collective-permute-start = (bf16[6,256,128]{2,1,0:T(8,128)(2,1)S(1)}, bf16[6,256,128]{2,1,0:T(8,128)(2,1)S(1)}, u32[]{:S(2)}, u32[]{:S(2)}) collective-permute-start(bf16[6,256,128]{2,1,0:T(8,128)(2,1)S(1)} %pack.2), channel_id=1, source_target_pairs={{0,16},{16,0},{1,17},{17,1},{2,18},{18,2},{3,19},{19,3},{4,20},{20... | collective-permute-start | bytes 1179656 | tf_op jit(solution)/shard_map/ppermute | solution.py:426
  4.8 1.3 %pack.3 = (bf16[6,256,128]{2,1,0:T(8,128)(2,1)S(1)}, bf16[4,256,128]{2,1,0:T(8,128)(2,1)S(1)}, bf16[4,256,128]{2,1,0:T(8,128)(2,1)S(1)}) custom-call(bf16[256,768]{1,0:T(8,128)(2,1)} %refs_0_.11, bf16[256,768]{1,0:T(8,128)(2,1)} %refs_1_.11, bf16[256,768]{1,0:T(8,128)(2,1)} %refs_2_.11, bf16[256,768]{1,0:T(8,128)(2,1)} %refs_3_.11, ...), custom_call_target="tpu_custom_call" | custom-call | flops 1 | bytes 1 | tf_op jit(solution)/shard_map/pack/pallas_call | solution.py:201
  6.1 0.2 collective-permute-start.4
  6.4 1.9 %collective-permute-start.3 = (bf16[4,256,128]{2,1,0:T(8,128)(2,1)S(1)}, bf16[4,256,128]{2,1,0:T(8,128)(2,1)S(1)}, u32[]{:S(2)}, u32[]{:S(2)}) collective-permute-start(bf16[4,256,128]{2,1,0:T(8,128)(2,1)S(1)} %get-tuple-element.23), channel_id=1, source_target_pairs={{0,16},{16,0},{1,17},{17,1},{2,18},{18,2},{3,19},{19,3},{4,20},{20... | collective-permute-start | bytes 786440 | tf_op jit(solution)/shard_map/ppermute | solution.py:426
  8.2 6.5 %collective-permute-done.refs_6_ = bf16[6,256,128]{2,1,0:T(8,128)(2,1)S(1)} collective-permute-done((bf16[6,256,128]{2,1,0:T(8,128)(2,1)S(1)}, bf16[6,256,128]{2,1,0:T(8,128)(2,1)S(1)}, u32[]{:S(2)}, u32[]{:S(2)}) %collective-permute-start) | collective-permute-done | bytes 393248 | tf_op jit(solution)/shard_map/ppermute | solution.py:426
  14.7 0.0 copy-done
  14.7 0.0 copy-done.1
  14.7 0.0 copy-done.2
  14.7 0.0 copy-done.3
  14.8 0.0 copy-done.4
  14.8 0.0 copy-done.5
  14.8 0.9 %whole_head.2 = (bf16[64,512]{1,0:T(8,128)(2,1)S(1)}, bf16[64,512]{1,0:T(8,128)(2,1)S(1)}, bf16[2,64,512]{2,1,0:T(8,128)(2,1)S(1)}) custom-call(bf16[256,768]{1,0:T(8,128)(2,1)S(1)} %copy-done, bf16[256,768]{1,0:T(8,128)(2,1)S(1)} %copy-done.1, bf16[256,768]{1,0:T(8,128)(2,1)S(1)} %copy-done.2, bf16[256,768]{1,0:T(8,128)(2,1)S(1)} %copy-done.3, ...), custom_call_target="tpu_custom_call" | custom-call | flops 500000000 | bytes 1 | tf_op jit(solution)/shard_map/whole_head/pallas_call | solution.py:284
  15.6 2.2 %collective-permute-start.1 = (bf16[2,64,512]{2,1,0:T(8,128)(2,1)S(1)}, bf16[2,64,512]{2,1,0:T(8,128)(2,1)S(1)}, u32[]{:S(2)}, u32[]{:S(2)}) collective-permute-start(bf16[2,64,512]{2,1,0:T(8,128)(2,1)S(1)} %get-tuple-element.22), channel_id=1, source_target_pairs={{0,8},{4,12},{8,0},{12,4},{1,9},{5,13},{9,1},{13,5},{2,10},{6,14},... | collective-permute-start | bytes 393224 | tf_op jit(solution)/shard_map/ppermute | solution.py:429
  17.8 5.4 %collective-permute-done.4.refs_6_ = bf16[6,256,128]{2,1,0:T(8,128)(2,1)S(1)} collective-permute-done((bf16[6,256,128]{2,1,0:T(8,128)(2,1)S(1)}, bf16[6,256,128]{2,1,0:T(8,128)(2,1)S(1)}, u32[]{:S(2)}, u32[]{:S(2)}) %collective-permute-start.4) | collective-permute-done | bytes 393248 | tf_op jit(solution)/shard_map/ppermute | solution.py:426
  23.2 0.8 %whole_head.3 = (bf16[64,256]{1,0:T(8,128)(2,1)S(1)}, bf16[64,256]{1,0:T(8,128)(2,1)S(1)}, bf16[2,64,256]{2,1,0:T(8,128)(2,1)S(1)}, bf16[256,256]{1,0:T(8,128)(2,1)S(1)}) custom-call(bf16[256,768]{1,0:T(8,128)(2,1)S(1)} %copy-done, bf16[256,768]{1,0:T(8,128)(2,1)S(1)} %copy-done.1, bf16[256,768]{1,0:T(8,128)(2,1)S(1)} %copy-done.2, ...), custom_call_target="tpu_custom_call" | custom-call | flops 2000000000 | bytes 1 | tf_op jit(solution)/shard_map/whole_head/pallas_call | solution.py:284
  24.0 2.1 %collective-permute-start.7 = (bf16[2,64,256]{2,1,0:T(8,128)(2,1)S(1)}, bf16[2,64,256]{2,1,0:T(8,128)(2,1)S(1)}, u32[]{:S(2)}, u32[]{:S(2)}) collective-permute-start(bf16[2,64,256]{2,1,0:T(8,128)(2,1)S(1)} %get-tuple-element.33), channel_id=1, source_target_pairs={{0,8},{4,12},{8,0},{12,4},{1,9},{5,13},{9,1},{13,5},{2,10},{6,14},... | collective-permute-start | bytes 196616 | tf_op jit(solution)/shard_map/ppermute | solution.py:429
  26.2 1.5 %collective-permute-start.10 = (bf16[4,256,128]{2,1,0:T(8,128)(2,1)S(1)}, bf16[4,256,128]{2,1,0:T(8,128)(2,1)S(1)}, u32[]{:S(2)}, u32[]{:S(2)}) collective-permute-start(bf16[4,256,128]{2,1,0:T(8,128)(2,1)S(1)} %get-tuple-element.34), channel_id=1, source_target_pairs={{0,16},{16,0},{1,17},{17,1},{2,18},{18,2},{3,19},{19,3},{4,20},{20... | collective-permute-start | bytes 786440 | tf_op jit(solution)/shard_map/ppermute | solution.py:426
  27.7 0.7 %collective-permute-done.7.pair.refs_5_ = bf16[2,64,256]{2,1,0:T(8,128)(2,1)S(1)} collective-permute-done((bf16[2,64,256]{2,1,0:T(8,128)(2,1)S(1)}, bf16[2,64,256]{2,1,0:T(8,128)(2,1)S(1)}, u32[]{:S(2)}, u32[]{:S(2)}) %collective-permute-start.7) | collective-permute-done | bytes 65568 | tf_op jit(solution)/shard_map/ppermute | solution.py:429
  28.4 0.0 collective-permute-start.8
  28.4 0.0 collective-permute-done.1.pair.refs_2_
  28.5 0.6 %collective-permute-start.2 = (bf16[2,64,512]{2,1,0:T(8,128)(2,1)S(1)}, bf16[2,64,512]{2,1,0:T(8,128)(2,1)S(1)}, u32[]{:S(2)}, u32[]{:S(2)}) collective-permute-start(bf16[2,64,512]{2,1,0:T(8,128)(2,1)S(1)} %join.4), channel_id=1, source_target_pairs={{0,4},{4,0},{8,12},{12,8},{1,5},{5,1},{9,13},{13,9},{2,6},{6,2},{1... | collective-permute-start | bytes 393224 | tf_op jit(solution)/shard_map/ppermute | solution.py:429
  29.0 0.0 collective-permute-done.3.refs_6_
  29.0 0.6 %shared_head.2 = (bf16[64,512]{1,0:T(8,128)(2,1)S(1)}, bf16[64,512]{1,0:T(8,128)(2,1)S(1)}, bf16[2,64,512]{2,1,0:T(8,128)(2,1)S(1)}) custom-call(bf16[256,768]{1,0:T(8,128)(2,1)S(1)} %copy-done, bf16[256,768]{1,0:T(8,128)(2,1)S(1)} %copy-done.1, bf16[256,768]{1,0:T(8,128)(2,1)S(1)} %copy-done.2, bf16[256,768]{1,0:T(8,128)(2,1)S(1)} %copy-done.3, ...), custom_call_target="tpu_custom_call" | custom-call | flops 3000000000 | bytes 1 | tf_op jit(solution)/shard_map/shared_head/pallas_call | solution.py:318
  29.6 2.1 %collective-permute-start.5 = (bf16[2,64,512]{2,1,0:T(8,128)(2,1)S(1)}, bf16[2,64,512]{2,1,0:T(8,128)(2,1)S(1)}, u32[]{:S(2)}, u32[]{:S(2)}) collective-permute-start(bf16[2,64,512]{2,1,0:T(8,128)(2,1)S(1)} %get-tuple-element.28), channel_id=1, source_target_pairs={{0,8},{4,12},{8,0},{12,4},{1,9},{5,13},{9,1},{13,5},{2,10},{6,14},... | collective-permute-start | bytes 393224 | tf_op jit(solution)/shard_map/ppermute | solution.py:429
  31.7 0.0 collective-permute-done.8.refs_4_
  31.7 0.0 collective-permute-done.2.refs_1_
  31.7 1.6 %collective-permute-start.9 = (bf16[4,64,512]{2,1,0:T(8,128)(2,1)S(1)}, bf16[4,64,512]{2,1,0:T(8,128)(2,1)S(1)}, u32[]{:S(2)}, u32[]{:S(2)}) collective-permute-start(bf16[4,64,512]{2,1,0:T(8,128)(2,1)S(1)} %gather_far.1), channel_id=1, source_target_pairs={{0,16},{16,0},{1,17},{17,1},{2,18},{18,2},{3,19},{19,3},{4,20},{20... | collective-permute-start | bytes 786440 | tf_op jit(solution)/shard_map/ppermute | solution.py:426
  33.3 0.3 collective-permute-done.10.refs_6_
  33.6 0.6 %shared_head.3 = (bf16[64,256]{1,0:T(8,128)(2,1)S(1)}, bf16[64,256]{1,0:T(8,128)(2,1)S(1)}, bf16[2,64,256]{2,1,0:T(8,128)(2,1)S(1)}) custom-call(bf16[256,768]{1,0:T(8,128)(2,1)S(1)} %copy-done, bf16[256,768]{1,0:T(8,128)(2,1)S(1)} %copy-done.1, bf16[256,768]{1,0:T(8,128)(2,1)S(1)} %copy-done.2, bf16[256,768]{1,0:T(8,128)(2,1)S(1)} %copy-done.3, ...), custom_call_target="tpu_custom_call" | custom-call | flops 2000000000 | bytes 1 | tf_op jit(solution)/shard_map/shared_head/pallas_call | solution.py:318
  34.1 2.0 %collective-permute-start.11 = (bf16[2,64,256]{2,1,0:T(8,128)(2,1)S(1)}, bf16[2,64,256]{2,1,0:T(8,128)(2,1)S(1)}, u32[]{:S(2)}, u32[]{:S(2)}) collective-permute-start(bf16[2,64,256]{2,1,0:T(8,128)(2,1)S(1)} %get-tuple-element.37), channel_id=1, source_target_pairs={{0,8},{4,12},{8,0},{12,4},{1,9},{5,13},{9,1},{13,5},{2,10},{6,14},... | collective-permute-start | bytes 196616 | tf_op jit(solution)/shard_map/ppermute | solution.py:429
  36.2 0.0 collective-permute-done.5.pair.refs_5_
  36.2 0.1 collective-permute-start.6
  36.3 2.2 %collective-permute-done.11.pair.refs_5_ = bf16[2,64,256]{2,1,0:T(8,128)(2,1)S(1)} collective-permute-done((bf16[2,64,256]{2,1,0:T(8,128)(2,1)S(1)}, bf16[2,64,256]{2,1,0:T(8,128)(2,1)S(1)}, u32[]{:S(2)}, u32[]{:S(2)}) %collective-permute-start.11) | collective-permute-done | bytes 65568 | tf_op jit(solution)/shard_map/ppermute | solution.py:429
  38.5 0.0 collective-permute-start.12
  38.5 0.0 collective-permute-done.6.refs_4_
  38.5 1.0 %place_near.1 = (bf16[64,3072]{1,0:T(8,128)(2,1)}, bf16[64,3072]{1,0:T(8,128)(2,1)}) custom-call(bf16[64,512]{1,0:T(8,128)(2,1)S(1)} %get-tuple-element.20.refs_0_, bf16[2,64,512]{2,1,0:T(8,128)(2,1)S(1)} %collective-permute-done.2.refs_1_, bf16[2,64,512]{2,1,0:T(8,128)(2,1)S(1)} %collective-permute-done.1.pair.refs_2_, ...), custom_call_target="tpu_custom_call" | custom-call | flops 1 | bytes 1 | tf_op jit(solution)/shard_map/place_near/pallas_call | solution.py:379
  39.5 0.3 collective-permute-done.12.refs_4_
  39.7 0.0 collective-permute-done.9.refs_2_
  39.8 0.9 %place_last.1 = (bf16[64,3072]{1,0:T(8,128)(2,1)}, bf16[64,3072]{1,0:T(8,128)(2,1)}) custom-call(bf16[64,3072]{1,0:T(8,128)(2,1)} %get-tuple-element.29.refs_0_, bf16[64,3072]{1,0:T(8,128)(2,1)} %get-tuple-element.30.refs_1_, bf16[4,64,512]{2,1,0:T(8,128)(2,1)S(1)} %collective-permute-done.9.refs_2_, ...), custom_call_target="tpu_custom_call", output_to_operand_aliasing={{0}: (0, {}), {1}: (1, {})} | custom-call | flops 1 | bytes 1 | tf_op jit(solution)/shard_map/place_last/pallas_call | solution.py:406
  (5 shorter events, 0.1 us)
Async XLA Ops:
  1.7 13.0 %copy-start = (bf16[256,768]{1,0:T(8,128)(2,1)S(1)}, bf16[256,768]{1,0:T(8,128)(2,1)}, u32[]{:S(2)}) copy-start(bf16[256,768]{1,0:T(8,128)(2,1)} %refs_0_.11) | copy-start | bytes 1179652
  1.7 13.0 %copy-start.1 = (bf16[256,768]{1,0:T(8,128)(2,1)S(1)}, bf16[256,768]{1,0:T(8,128)(2,1)}, u32[]{:S(2)}) copy-start(bf16[256,768]{1,0:T(8,128)(2,1)} %refs_1_.11) | copy-start | bytes 1179652
  1.7 13.0 %copy-start.2 = (bf16[256,768]{1,0:T(8,128)(2,1)S(1)}, bf16[256,768]{1,0:T(8,128)(2,1)}, u32[]{:S(2)}) copy-start(bf16[256,768]{1,0:T(8,128)(2,1)} %refs_2_.11) | copy-start | bytes 1179652
  1.7 13.0 %copy-start.3 = (bf16[256,768]{1,0:T(8,128)(2,1)S(1)}, bf16[256,768]{1,0:T(8,128)(2,1)}, u32[]{:S(2)}) copy-start(bf16[256,768]{1,0:T(8,128)(2,1)} %refs_3_.11) | copy-start | bytes 1179652
  1.8 13.0 %copy-start.4 = (bf16[256,768]{1,0:T(8,128)(2,1)S(1)}, bf16[256,768]{1,0:T(8,128)(2,1)}, u32[]{:S(2)}) copy-start(bf16[256,768]{1,0:T(8,128)(2,1)} %refs_4_.11) | copy-start | bytes 1179652
  1.8 13.0 %copy-start.5 = (bf16[256,768]{1,0:T(8,128)(2,1)S(1)}, bf16[256,768]{1,0:T(8,128)(2,1)}, u32[]{:S(2)}) copy-start(bf16[256,768]{1,0:T(8,128)(2,1)} %refs_5_.11) | copy-start | bytes 1179652
  1.8 12.9 %collective-permute-start = (bf16[6,256,128]{2,1,0:T(8,128)(2,1)S(1)}, bf16[6,256,128]{2,1,0:T(8,128)(2,1)S(1)}, u32[]{:S(2)}, u32[]{:S(2)}) collective-permute-start(bf16[6,256,128]{2,1,0:T(8,128)(2,1)S(1)} %pack.2), channel_id=1, source_target_pairs={{0,16},{16,0},{1,17},{17,1},{2,18},{18,2},{3,19},{19,3},{4,20},{20... | collective-permute-start | bytes 1179656 | tf_op jit(solution)/shard_map/ppermute | solution.py:426
  6.1 17.0 %collective-permute-start.4 = (bf16[6,256,128]{2,1,0:T(8,128)(2,1)S(1)}, bf16[6,256,128]{2,1,0:T(8,128)(2,1)S(1)}, u32[]{:S(2)}, u32[]{:S(2)}) collective-permute-start(bf16[6,256,128]{2,1,0:T(8,128)(2,1)S(1)} %get-tuple-element.24), channel_id=1, source_target_pairs={{0,16},{16,0},{1,17},{17,1},{2,18},{18,2},{3,19},{19,3},{4,20},{20... | collective-permute-start | bytes 1179656 | tf_op jit(solution)/shard_map/ppermute | solution.py:426
  6.4 22.6 %collective-permute-start.3 = (bf16[4,256,128]{2,1,0:T(8,128)(2,1)S(1)}, bf16[4,256,128]{2,1,0:T(8,128)(2,1)S(1)}, u32[]{:S(2)}, u32[]{:S(2)}) collective-permute-start(bf16[4,256,128]{2,1,0:T(8,128)(2,1)S(1)} %get-tuple-element.23), channel_id=1, source_target_pairs={{0,16},{16,0},{1,17},{17,1},{2,18},{18,2},{3,19},{19,3},{4,20},{20... | collective-permute-start | bytes 786440 | tf_op jit(solution)/shard_map/ppermute | solution.py:426
  15.6 12.8 %collective-permute-start.1 = (bf16[2,64,512]{2,1,0:T(8,128)(2,1)S(1)}, bf16[2,64,512]{2,1,0:T(8,128)(2,1)S(1)}, u32[]{:S(2)}, u32[]{:S(2)}) collective-permute-start(bf16[2,64,512]{2,1,0:T(8,128)(2,1)S(1)} %get-tuple-element.22), channel_id=1, source_target_pairs={{0,8},{4,12},{8,0},{12,4},{1,9},{5,13},{9,1},{13,5},{2,10},{6,14},... | collective-permute-start | bytes 393224 | tf_op jit(solution)/shard_map/ppermute | solution.py:429
  24.0 4.4 %collective-permute-start.7 = (bf16[2,64,256]{2,1,0:T(8,128)(2,1)S(1)}, bf16[2,64,256]{2,1,0:T(8,128)(2,1)S(1)}, u32[]{:S(2)}, u32[]{:S(2)}) collective-permute-start(bf16[2,64,256]{2,1,0:T(8,128)(2,1)S(1)} %get-tuple-element.33), channel_id=1, source_target_pairs={{0,8},{4,12},{8,0},{12,4},{1,9},{5,13},{9,1},{13,5},{2,10},{6,14},... | collective-permute-start | bytes 196616 | tf_op jit(solution)/shard_map/ppermute | solution.py:429
  26.2 7.4 %collective-permute-start.10 = (bf16[4,256,128]{2,1,0:T(8,128)(2,1)S(1)}, bf16[4,256,128]{2,1,0:T(8,128)(2,1)S(1)}, u32[]{:S(2)}, u32[]{:S(2)}) collective-permute-start(bf16[4,256,128]{2,1,0:T(8,128)(2,1)S(1)} %get-tuple-element.34), channel_id=1, source_target_pairs={{0,16},{16,0},{1,17},{17,1},{2,18},{18,2},{3,19},{19,3},{4,20},{20... | collective-permute-start | bytes 786440 | tf_op jit(solution)/shard_map/ppermute | solution.py:426
  28.4 3.3 %collective-permute-start.8 = (bf16[2,64,256]{2,1,0:T(8,128)(2,1)S(1)}, bf16[2,64,256]{2,1,0:T(8,128)(2,1)S(1)}, u32[]{:S(2)}, u32[]{:S(2)}) collective-permute-start(bf16[2,64,256]{2,1,0:T(8,128)(2,1)S(1)} %join.6), channel_id=1, source_target_pairs={{0,4},{4,0},{8,12},{12,8},{1,5},{5,1},{9,13},{13,9},{2,6},{6,2},{1... | collective-permute-start | bytes 196616 | tf_op jit(solution)/shard_map/ppermute | solution.py:429
  28.5 3.2 %collective-permute-start.2 = (bf16[2,64,512]{2,1,0:T(8,128)(2,1)S(1)}, bf16[2,64,512]{2,1,0:T(8,128)(2,1)S(1)}, u32[]{:S(2)}, u32[]{:S(2)}) collective-permute-start(bf16[2,64,512]{2,1,0:T(8,128)(2,1)S(1)} %join.4), channel_id=1, source_target_pairs={{0,4},{4,0},{8,12},{12,8},{1,5},{5,1},{9,13},{13,9},{2,6},{6,2},{1... | collective-permute-start | bytes 393224 | tf_op jit(solution)/shard_map/ppermute | solution.py:429
  29.6 6.6 %collective-permute-start.5 = (bf16[2,64,512]{2,1,0:T(8,128)(2,1)S(1)}, bf16[2,64,512]{2,1,0:T(8,128)(2,1)S(1)}, u32[]{:S(2)}, u32[]{:S(2)}) collective-permute-start(bf16[2,64,512]{2,1,0:T(8,128)(2,1)S(1)} %get-tuple-element.28), channel_id=1, source_target_pairs={{0,8},{4,12},{8,0},{12,4},{1,9},{5,13},{9,1},{13,5},{2,10},{6,14},... | collective-permute-start | bytes 393224 | tf_op jit(solution)/shard_map/ppermute | solution.py:429
  31.7 8.0 %collective-permute-start.9 = (bf16[4,64,512]{2,1,0:T(8,128)(2,1)S(1)}, bf16[4,64,512]{2,1,0:T(8,128)(2,1)S(1)}, u32[]{:S(2)}, u32[]{:S(2)}) collective-permute-start(bf16[4,64,512]{2,1,0:T(8,128)(2,1)S(1)} %gather_far.1), channel_id=1, source_target_pairs={{0,16},{16,0},{1,17},{17,1},{2,18},{18,2},{3,19},{19,3},{4,20},{20... | collective-permute-start | bytes 786440 | tf_op jit(solution)/shard_map/ppermute | solution.py:426
  34.1 4.3 %collective-permute-start.11 = (bf16[2,64,256]{2,1,0:T(8,128)(2,1)S(1)}, bf16[2,64,256]{2,1,0:T(8,128)(2,1)S(1)}, u32[]{:S(2)}, u32[]{:S(2)}) collective-permute-start(bf16[2,64,256]{2,1,0:T(8,128)(2,1)S(1)} %get-tuple-element.37), channel_id=1, source_target_pairs={{0,8},{4,12},{8,0},{12,4},{1,9},{5,13},{9,1},{13,5},{2,10},{6,14},... | collective-permute-start | bytes 196616 | tf_op jit(solution)/shard_map/ppermute | solution.py:429
  36.2 2.3 %collective-permute-start.6 = (bf16[2,64,512]{2,1,0:T(8,128)(2,1)S(1)}, bf16[2,64,512]{2,1,0:T(8,128)(2,1)S(1)}, u32[]{:S(2)}, u32[]{:S(2)}) collective-permute-start(bf16[2,64,512]{2,1,0:T(8,128)(2,1)S(1)} %join.5), channel_id=1, source_target_pairs={{0,4},{4,0},{8,12},{12,8},{1,5},{5,1},{9,13},{13,9},{2,6},{6,2},{1... | collective-permute-start | bytes 393224 | tf_op jit(solution)/shard_map/ppermute | solution.py:429
  38.5 1.3 %collective-permute-start.12 = (bf16[2,64,256]{2,1,0:T(8,128)(2,1)S(1)}, bf16[2,64,256]{2,1,0:T(8,128)(2,1)S(1)}, u32[]{:S(2)}, u32[]{:S(2)}) collective-permute-start(bf16[2,64,256]{2,1,0:T(8,128)(2,1)S(1)} %join.7), channel_id=1, source_target_pairs={{0,4},{4,0},{8,12},{12,8},{1,5},{5,1},{9,13},{13,9},{2,6},{6,2},{1... | collective-permute-start | bytes 196616 | tf_op jit(solution)/shard_map/ppermute | solution.py:429

commit v5 on v4

--- a/solution.py
+++ b/solution.py
@@ -221,11 +221,11 @@
         c.wait()
 
 
-def _cut(outs, held):
-    keep, beside, across = outs
+def _cut(outs, held, order=(0, 1, 2, 3)):
+    keep, single, pair = outs
     piece = keep.shape[0]
     me = lax.axis_index("head")
-    for s, out in enumerate((keep, beside, across.at[0], across.at[1])):
+    for s, out in zip(order, (keep, single, pair.at[0], pair.at[1])):
         out[...] = held[pl.ds(pl.multiple_of((me ^ s) * piece, piece), piece), :]
 
 
@@ -252,7 +252,7 @@
         in_specs=[vmem] * 2,
         out_specs=vmem,
         compiler_params=_params(),
-        cost_estimate=_cost(500_000_000),
+        cost_estimate=_cost(1),
         name="join",
     )(piece, pair)
 
@@ -288,12 +288,12 @@
         out_specs=[vmem] * len(shapes),
         scratch_shapes=[pltpu.VMEM((rows, width), jnp.bfloat16)],
         compiler_params=_params(),
-        cost_estimate=_cost((500_000_000, 2_000_000_000)[which]),
+        cost_estimate=_cost((500000001, 2000000001)[which]),
         name="whole_head",
     )(*own, received)
 
 
-def shared_head(own, received, done, which):
+def shared_head(own, received, done, which, order):
     rows = own[0].shape[0]
     n, m = len(own), len(done)
     width = (m + 1) * HD
@@ -312,7 +312,7 @@
                     :, o * HD : (o + 1) * HD
                 ]
             held[:, (o + 1) * width - HD : (o + 1) * width] = result[o]
-        _cut(outs, held)
+        _cut(outs, held, order)
 
     vmem = pl.BlockSpec(memory_space=pltpu.VMEM)
     return pl.pallas_call(
@@ -322,7 +322,7 @@
         out_specs=[vmem] * 3,
         scratch_shapes=[pltpu.VMEM((rows, 2 * width), jnp.bfloat16)],
         compiler_params=_params(),
-        cost_estimate=_cost((3_000_000_000, 2_000_000_000)[which % 2]),
+        cost_estimate=_cost((5000000001, 2000000001)[which % 2]),
         name="shared_head",
     )(*own, received, *done)
 
@@ -348,7 +348,7 @@
         in_specs=[vmem] * 6,
         out_specs=vmem,
         compiler_params=_params(),
-        cost_estimate=_cost(500_000_000),
+        cost_estimate=_cost(500000001),
         name="gather_far",
     )(*first, *second)
 
@@ -390,7 +390,8 @@
 
 def place_last(outputs, crossed, last, g, heads):
     def kernel(*refs):
-        far, ours, outs, sems = refs[2], _sources(*refs[3:6]), refs[6:8], refs[8]
+        far, outs, sems = refs[2], refs[6:8], refs[8]
+        ours = refs[3], refs[4].at[0], refs[5].at[0], refs[5].at[1]
         me, blk = lax.axis_index("head"), lax.axis_index("blk")
         width = g * HD
         copies = []
@@ -440,9 +441,12 @@
     firsts = spread(whole_head(own, whole_in[0], g, 0, True))
     *seconds, near = whole_head(own, whole_in[1], g, 1, False)
     far = gather_far(firsts, spread(seconds))
-    parts = list(shared_head(own, shared_in[0], (near,), 2 * g))
+    parts = list(shared_head(own, shared_in[0], (near,), 2 * g, (0, 1, 2, 3)))
+    far, parts[0] = lax.optimization_barrier((far, parts[0]))
     outputs = place_near(firsts, spread(parts), g, heads)
-    last = spread(shared_head(own, shared_in[1], (), 2 * g + 1))
+    keep, across, beside = shared_head(own, shared_in[1], (), 2 * g + 1, (0, 2, 1, 3))
+    beside = along(beside, 1)
+    last = keep, beside, along(join(across, beside), 2)
     return place_last(outputs, cross(far), last, g, heads)
 
 

time: 40.9 us -> 41.2 us (level)
  no operation moved by 1% of the time
where the time goes in v5:
time: 41.2 us; the launch traced here: 40.9 us
  starting transfers between devices  17.2 us (42%)
  waiting for transfers between devices  15.7 us (38%)
  Pallas kernels  7.16 us (17%)
  between operations  0.83 us (2%)
    ppermute x5, waiting for transfers between devices, cross(): return lax.ppermute(x, 'blk', [(0, 1), (1, 0)])  12.1 us
    ppermute x8, starting transfers between devices, along(): return lax.ppermute(x, 'head', [(i, i ^ s) for i in range(4)])  9.02 us
    ppermute x5, starting transfers between devices, cross(): return lax.ppermute(x, 'blk', [(0, 1), (1, 0)])  8.15 us
    ppermute x8, waiting for transfers between devices, along(): return lax.ppermute(x, 'head', [(i, i ^ s) for i in range(4)])  3.59 us
    pallas_call x2, Pallas kernels, pack(): pl.pallas_call(kernel, out_shape=[jax.ShapeDtypeStruct(shape, jnp.bfloat1...  2.41 us
    pallas_call x2, Pallas kernels, whole_head(): pl.pallas_call(kernel, out_shape=shapes, in_specs=[vmem] * (n + 1), out_s...  1.71 us
    pallas_call x2, Pallas kernels, shared_head(): pl.pallas_call(kernel, out_shape=_cut_shapes(rows, 2 * width), in_specs=[...  1.15 us
    pallas_call x1, Pallas kernels, place_near(): pl.pallas_call(kernel, out_shape=[full] * 2, in_specs=[pl.BlockSpec(memor...  0.94 us
  transfers between devices with their start and end apart: 13, of which 6 were waited for; matrix products, arithmetic and copies ran while one was open for 0% of the time, Pallas kernels for 13%

profile of v5, /device:TPU:0, one launch (start us, length us, event | category | flops | bytes accessed | tf_op | source)
XLA Modules:
  0.0 40.9 jit_solution(11174787085890694387)
XLA Ops:
  0.6 1.1 %pack.2 = bf16[6,256,128]{2,1,0:T(8,128)(2,1)S(1)} custom-call(bf16[256,768]{1,0:T(8,128)(2,1)} %refs_0_.11, bf16[256,768]{1,0:T(8,128)(2,1)} %refs_1_.11, bf16[256,768]{1,0:T(8,128)(2,1)} %refs_2_.11, bf16[256,768]{1,0:T(8,128)(2,1)} %refs_3_.11, bf16[256,768]{1,0:T(8,128)(2,1)} %refs_4_.11, bf16[256,768]{1,0:T(8,128)(2,1)} %refs_5_.11), custom_call_target="tpu_custom_call" | custom-call | flops 1 | bytes 1 | tf_op jit(solution)/shard_map/pack/pallas_call | solution.py:201
  1.7 0.0 copy-start
  1.7 0.0 copy-start.1
  1.7 0.0 copy-start.2
  1.7 0.0 copy-start.3
  1.8 0.0 copy-start.4
  1.8 0.0 copy-start.5
  1.8 3.0 %collective-permute-start = (bf16[6,256,128]{2,1,0:T(8,128)(2,1)S(1)}, bf16[6,256,128]{2,1,0:T(8,128)(2,1)S(1)}, u32[]{:S(2)}, u32[]{:S(2)}) collective-permute-start(bf16[6,256,128]{2,1,0:T(8,128)(2,1)S(1)} %pack.2), channel_id=1, source_target_pairs={{0,16},{16,0},{1,17},{17,1},{2,18},{18,2},{3,19},{19,3},{4,20},{20... | collective-permute-start | bytes 1179656 | tf_op jit(solution)/shard_map/ppermute | solution.py:427
  4.8 1.3 %pack.3 = (bf16[6,256,128]{2,1,0:T(8,128)(2,1)S(1)}, bf16[4,256,128]{2,1,0:T(8,128)(2,1)S(1)}, bf16[4,256,128]{2,1,0:T(8,128)(2,1)S(1)}) custom-call(bf16[256,768]{1,0:T(8,128)(2,1)} %refs_0_.11, bf16[256,768]{1,0:T(8,128)(2,1)} %refs_1_.11, bf16[256,768]{1,0:T(8,128)(2,1)} %refs_2_.11, bf16[256,768]{1,0:T(8,128)(2,1)} %refs_3_.11, ...), custom_call_target="tpu_custom_call" | custom-call | flops 1 | bytes 1 | tf_op jit(solution)/shard_map/pack/pallas_call | solution.py:201
  6.1 0.2 collective-permute-start.3
  6.4 1.9 %collective-permute-start.6 = (bf16[4,256,128]{2,1,0:T(8,128)(2,1)S(1)}, bf16[4,256,128]{2,1,0:T(8,128)(2,1)S(1)}, u32[]{:S(2)}, u32[]{:S(2)}) collective-permute-start(bf16[4,256,128]{2,1,0:T(8,128)(2,1)S(1)} %get-tuple-element.29), channel_id=1, source_target_pairs={{0,16},{16,0},{1,17},{17,1},{2,18},{18,2},{3,19},{19,3},{4,20},{20... | collective-permute-start | bytes 786440 | tf_op jit(solution)/shard_map/ppermute | solution.py:427
  8.2 6.5 %collective-permute-done.refs_6_ = bf16[6,256,128]{2,1,0:T(8,128)(2,1)S(1)} collective-permute-done((bf16[6,256,128]{2,1,0:T(8,128)(2,1)S(1)}, bf16[6,256,128]{2,1,0:T(8,128)(2,1)S(1)}, u32[]{:S(2)}, u32[]{:S(2)}) %collective-permute-start) | collective-permute-done | bytes 393248 | tf_op jit(solution)/shard_map/ppermute | solution.py:427
  14.7 0.0 copy-done
  14.7 0.0 copy-done.1
  14.7 0.0 copy-done.2
  14.7 0.0 copy-done.3
  14.8 0.0 copy-done.4
  14.8 0.0 copy-done.5
  14.8 0.9 %whole_head.2 = (bf16[64,512]{1,0:T(8,128)(2,1)S(1)}, bf16[64,512]{1,0:T(8,128)(2,1)S(1)}, bf16[2,64,512]{2,1,0:T(8,128)(2,1)S(1)}) custom-call(bf16[256,768]{1,0:T(8,128)(2,1)S(1)} %copy-done, bf16[256,768]{1,0:T(8,128)(2,1)S(1)} %copy-done.1, bf16[256,768]{1,0:T(8,128)(2,1)S(1)} %copy-done.2, bf16[256,768]{1,0:T(8,128)(2,1)S(1)} %copy-done.3, ...), custom_call_target="tpu_custom_call" | custom-call | flops 500000000 | bytes 1 | tf_op jit(solution)/shard_map/whole_head/pallas_call | solution.py:284
  15.6 2.2 %collective-permute-start.1 = (bf16[2,64,512]{2,1,0:T(8,128)(2,1)S(1)}, bf16[2,64,512]{2,1,0:T(8,128)(2,1)S(1)}, u32[]{:S(2)}, u32[]{:S(2)}) collective-permute-start(bf16[2,64,512]{2,1,0:T(8,128)(2,1)S(1)} %get-tuple-element.24), channel_id=1, source_target_pairs={{0,8},{4,12},{8,0},{12,4},{1,9},{5,13},{9,1},{13,5},{2,10},{6,14},... | collective-permute-start | bytes 393224 | tf_op jit(solution)/shard_map/ppermute | solution.py:430
  17.8 5.4 %collective-permute-done.3.refs_6_ = bf16[6,256,128]{2,1,0:T(8,128)(2,1)S(1)} collective-permute-done((bf16[6,256,128]{2,1,0:T(8,128)(2,1)S(1)}, bf16[6,256,128]{2,1,0:T(8,128)(2,1)S(1)}, u32[]{:S(2)}, u32[]{:S(2)}) %collective-permute-start.3) | collective-permute-done | bytes 393248 | tf_op jit(solution)/shard_map/ppermute | solution.py:427
  23.2 0.8 %whole_head.3 = (bf16[64,256]{1,0:T(8,128)(2,1)S(1)}, bf16[64,256]{1,0:T(8,128)(2,1)S(1)}, bf16[2,64,256]{2,1,0:T(8,128)(2,1)S(1)}, bf16[256,256]{1,0:T(8,128)(2,1)S(1)}) custom-call(bf16[256,768]{1,0:T(8,128)(2,1)S(1)} %copy-done, bf16[256,768]{1,0:T(8,128)(2,1)S(1)} %copy-done.1, bf16[256,768]{1,0:T(8,128)(2,1)S(1)} %copy-done.2, ...), custom_call_target="tpu_custom_call" | custom-call | flops 2000000000 | bytes 1 | tf_op jit(solution)/shard_map/whole_head/pallas_call | solution.py:284
  24.0 2.1 %collective-permute-start.4 = (bf16[2,64,256]{2,1,0:T(8,128)(2,1)S(1)}, bf16[2,64,256]{2,1,0:T(8,128)(2,1)S(1)}, u32[]{:S(2)}, u32[]{:S(2)}) collective-permute-start(bf16[2,64,256]{2,1,0:T(8,128)(2,1)S(1)} %get-tuple-element.28), channel_id=1, source_target_pairs={{0,8},{4,12},{8,0},{12,4},{1,9},{5,13},{9,1},{13,5},{2,10},{6,14},... | collective-permute-start | bytes 196616 | tf_op jit(solution)/shard_map/ppermute | solution.py:430
  26.2 1.5 %collective-permute-start.10 = (bf16[4,256,128]{2,1,0:T(8,128)(2,1)S(1)}, bf16[4,256,128]{2,1,0:T(8,128)(2,1)S(1)}, u32[]{:S(2)}, u32[]{:S(2)}) collective-permute-start(bf16[4,256,128]{2,1,0:T(8,128)(2,1)S(1)} %get-tuple-element.38), channel_id=1, source_target_pairs={{0,16},{16,0},{1,17},{17,1},{2,18},{18,2},{3,19},{19,3},{4,20},{20... | collective-permute-start | bytes 786440 | tf_op jit(solution)/shard_map/ppermute | solution.py:427
  27.7 0.7 %collective-permute-done.4.pair.refs_5_ = bf16[2,64,256]{2,1,0:T(8,128)(2,1)S(1)} collective-permute-done((bf16[2,64,256]{2,1,0:T(8,128)(2,1)S(1)}, bf16[2,64,256]{2,1,0:T(8,128)(2,1)S(1)}, u32[]{:S(2)}, u32[]{:S(2)}) %collective-permute-start.4) | collective-permute-done | bytes 65568 | tf_op jit(solution)/shard_map/ppermute | solution.py:430
  28.4 0.0 collective-permute-start.5
  28.4 0.0 collective-permute-done.1.pair.refs_2_
  28.5 0.6 %collective-permute-start.2 = (bf16[2,64,512]{2,1,0:T(8,128)(2,1)S(1)}, bf16[2,64,512]{2,1,0:T(8,128)(2,1)S(1)}, u32[]{:S(2)}, u32[]{:S(2)}) collective-permute-start(bf16[2,64,512]{2,1,0:T(8,128)(2,1)S(1)} %join.4), channel_id=1, source_target_pairs={{0,4},{4,0},{8,12},{12,8},{1,5},{5,1},{9,13},{13,9},{2,6},{6,2},{1... | collective-permute-start | bytes 393224 | tf_op jit(solution)/shard_map/ppermute | solution.py:430
  29.0 0.0 collective-permute-done.6.refs_6_
  29.0 0.6 %shared_head.2 = (bf16[64,512]{1,0:T(8,128)(2,1)S(1)}, bf16[64,512]{1,0:T(8,128)(2,1)S(1)}, bf16[2,64,512]{2,1,0:T(8,128)(2,1)S(1)}) custom-call(bf16[256,768]{1,0:T(8,128)(2,1)S(1)} %copy-done, bf16[256,768]{1,0:T(8,128)(2,1)S(1)} %copy-done.1, bf16[256,768]{1,0:T(8,128)(2,1)S(1)} %copy-done.2, bf16[256,768]{1,0:T(8,128)(2,1)S(1)} %copy-done.3, ...), custom_call_target="tpu_custom_call" | custom-call | flops 5000000000 | bytes 1 | tf_op jit(solution)/shard_map/shared_head/pallas_call | solution.py:318
  29.6 2.1 %collective-permute-start.7 = (bf16[2,64,512]{2,1,0:T(8,128)(2,1)S(1)}, bf16[2,64,512]{2,1,0:T(8,128)(2,1)S(1)}, u32[]{:S(2)}, u32[]{:S(2)}) collective-permute-start(bf16[2,64,512]{2,1,0:T(8,128)(2,1)S(1)} %get-tuple-element.34), channel_id=1, source_target_pairs={{0,8},{4,12},{8,0},{12,4},{1,9},{5,13},{9,1},{13,5},{2,10},{6,14},... | collective-permute-start | bytes 393224 | tf_op jit(solution)/shard_map/ppermute | solution.py:430
  31.7 0.0 collective-permute-done.5.refs_4_
  31.7 0.0 collective-permute-done.2.refs_1_
  31.7 1.6 %collective-permute-start.9 = (bf16[4,64,512]{2,1,0:T(8,128)(2,1)S(1)}, bf16[4,64,512]{2,1,0:T(8,128)(2,1)S(1)}, u32[]{:S(2)}, u32[]{:S(2)}) collective-permute-start(bf16[4,64,512]{2,1,0:T(8,128)(2,1)S(1)} %gather_far.1), channel_id=1, source_target_pairs={{0,16},{16,0},{1,17},{17,1},{2,18},{18,2},{3,19},{19,3},{4,20},{20... | collective-permute-start | bytes 786440 | tf_op jit(solution)/shard_map/ppermute | solution.py:427
  33.3 0.3 collective-permute-done.10.refs_6_
  33.6 0.6 %shared_head.3 = (bf16[64,256]{1,0:T(8,128)(2,1)S(1)}, bf16[64,256]{1,0:T(8,128)(2,1)S(1)}, bf16[2,64,256]{2,1,0:T(8,128)(2,1)S(1)}) custom-call(bf16[256,768]{1,0:T(8,128)(2,1)S(1)} %copy-done, bf16[256,768]{1,0:T(8,128)(2,1)S(1)} %copy-done.1, bf16[256,768]{1,0:T(8,128)(2,1)S(1)} %copy-done.2, bf16[256,768]{1,0:T(8,128)(2,1)S(1)} %copy-done.3, ...), custom_call_target="tpu_custom_call" | custom-call | flops 2000000000 | bytes 1 | tf_op jit(solution)/shard_map/shared_head/pallas_call | solution.py:318
  34.1 0.1 collective-permute-start.11
  34.2 1.2 %collective-permute-done.7.pair.refs_5_ = bf16[2,64,512]{2,1,0:T(8,128)(2,1)S(1)} collective-permute-done((bf16[2,64,512]{2,1,0:T(8,128)(2,1)S(1)}, bf16[2,64,512]{2,1,0:T(8,128)(2,1)S(1)}, u32[]{:S(2)}, u32[]{:S(2)}) %collective-permute-start.7) | collective-permute-done | bytes 131104 | tf_op jit(solution)/shard_map/ppermute | solution.py:430
  35.4 0.1 collective-permute-start.8
  35.5 0.0 collective-permute-done.11.pair.refs_4_
  35.5 1.9 %collective-permute-start.12 = (bf16[2,64,256]{2,1,0:T(8,128)(2,1)S(1)}, bf16[2,64,256]{2,1,0:T(8,128)(2,1)S(1)}, u32[]{:S(2)}, u32[]{:S(2)}) collective-permute-start(bf16[2,64,256]{2,1,0:T(8,128)(2,1)S(1)} %join.7), channel_id=1, source_target_pairs={{0,8},{4,12},{8,0},{12,4},{1,9},{5,13},{9,1},{13,5},{2,10},{6,14},... | collective-permute-start | bytes 196616 | tf_op jit(solution)/shard_map/ppermute | solution.py:430
  37.4 0.0 collective-permute-done.8.refs_4_
  37.4 0.9 %place_near.1 = (bf16[64,3072]{1,0:T(8,128)(2,1)}, bf16[64,3072]{1,0:T(8,128)(2,1)}) custom-call(bf16[64,512]{1,0:T(8,128)(2,1)S(1)} %get-tuple-element.22.refs_0_, bf16[2,64,512]{2,1,0:T(8,128)(2,1)S(1)} %collective-permute-done.2.refs_1_, bf16[2,64,512]{2,1,0:T(8,128)(2,1)S(1)} %collective-permute-done.1.pair.refs_2_, ...), custom_call_target="tpu_custom_call" | custom-call | flops 1 | bytes 1 | tf_op jit(solution)/shard_map/place_near/pallas_call | solution.py:379
  38.4 1.7 %collective-permute-done.12.refs_5_ = bf16[2,64,256]{2,1,0:T(8,128)(2,1)S(1)} collective-permute-done((bf16[2,64,256]{2,1,0:T(8,128)(2,1)S(1)}, bf16[2,64,256]{2,1,0:T(8,128)(2,1)S(1)}, u32[]{:S(2)}, u32[]{:S(2)}) %collective-permute-start.12) | collective-permute-done | bytes 65568 | tf_op jit(solution)/shard_map/ppermute | solution.py:430
  40.1 0.0 collective-permute-done.9.refs_2_
  40.1 0.9 %place_last.1 = (bf16[64,3072]{1,0:T(8,128)(2,1)}, bf16[64,3072]{1,0:T(8,128)(2,1)}) custom-call(bf16[64,3072]{1,0:T(8,128)(2,1)} %get-tuple-element.35.refs_0_, bf16[64,3072]{1,0:T(8,128)(2,1)} %get-tuple-element.36.refs_1_, bf16[4,64,512]{2,1,0:T(8,128)(2,1)S(1)} %collective-permute-done.9.refs_2_, ...), custom_call_target="tpu_custom_call", output_to_operand_aliasing={{0}: (0, {}), {1}: (1, {})} | custom-call | flops 1 | bytes 1 | tf_op jit(solution)/shard_map/place_last/pallas_call | solution.py:407
  (5 shorter events, 0.1 us)
Async XLA Ops:
  1.7 13.0 %copy-start = (bf16[256,768]{1,0:T(8,128)(2,1)S(1)}, bf16[256,768]{1,0:T(8,128)(2,1)}, u32[]{:S(2)}) copy-start(bf16[256,768]{1,0:T(8,128)(2,1)} %refs_0_.11) | copy-start | bytes 1179652
  1.7 13.0 %copy-start.1 = (bf16[256,768]{1,0:T(8,128)(2,1)S(1)}, bf16[256,768]{1,0:T(8,128)(2,1)}, u32[]{:S(2)}) copy-start(bf16[256,768]{1,0:T(8,128)(2,1)} %refs_1_.11) | copy-start | bytes 1179652
  1.7 13.0 %copy-start.2 = (bf16[256,768]{1,0:T(8,128)(2,1)S(1)}, bf16[256,768]{1,0:T(8,128)(2,1)}, u32[]{:S(2)}) copy-start(bf16[256,768]{1,0:T(8,128)(2,1)} %refs_2_.11) | copy-start | bytes 1179652
  1.7 13.0 %copy-start.3 = (bf16[256,768]{1,0:T(8,128)(2,1)S(1)}, bf16[256,768]{1,0:T(8,128)(2,1)}, u32[]{:S(2)}) copy-start(bf16[256,768]{1,0:T(8,128)(2,1)} %refs_3_.11) | copy-start | bytes 1179652
  1.8 13.0 %copy-start.4 = (bf16[256,768]{1,0:T(8,128)(2,1)S(1)}, bf16[256,768]{1,0:T(8,128)(2,1)}, u32[]{:S(2)}) copy-start(bf16[256,768]{1,0:T(8,128)(2,1)} %refs_4_.11) | copy-start | bytes 1179652
  1.8 13.0 %copy-start.5 = (bf16[256,768]{1,0:T(8,128)(2,1)S(1)}, bf16[256,768]{1,0:T(8,128)(2,1)}, u32[]{:S(2)}) copy-start(bf16[256,768]{1,0:T(8,128)(2,1)} %refs_5_.11) | copy-start | bytes 1179652
  1.8 12.9 %collective-permute-start = (bf16[6,256,128]{2,1,0:T(8,128)(2,1)S(1)}, bf16[6,256,128]{2,1,0:T(8,128)(2,1)S(1)}, u32[]{:S(2)}, u32[]{:S(2)}) collective-permute-start(bf16[6,256,128]{2,1,0:T(8,128)(2,1)S(1)} %pack.2), channel_id=1, source_target_pairs={{0,16},{16,0},{1,17},{17,1},{2,18},{18,2},{3,19},{19,3},{4,20},{20... | collective-permute-start | bytes 1179656 | tf_op jit(solution)/shard_map/ppermute | solution.py:427
  6.1 17.0 %collective-permute-start.3 = (bf16[6,256,128]{2,1,0:T(8,128)(2,1)S(1)}, bf16[6,256,128]{2,1,0:T(8,128)(2,1)S(1)}, u32[]{:S(2)}, u32[]{:S(2)}) collective-permute-start(bf16[6,256,128]{2,1,0:T(8,128)(2,1)S(1)} %get-tuple-element.25), channel_id=1, source_target_pairs={{0,16},{16,0},{1,17},{17,1},{2,18},{18,2},{3,19},{19,3},{4,20},{20... | collective-permute-start | bytes 1179656 | tf_op jit(solution)/shard_map/ppermute | solution.py:427
  6.4 22.6 %collective-permute-start.6 = (bf16[4,256,128]{2,1,0:T(8,128)(2,1)S(1)}, bf16[4,256,128]{2,1,0:T(8,128)(2,1)S(1)}, u32[]{:S(2)}, u32[]{:S(2)}) collective-permute-start(bf16[4,256,128]{2,1,0:T(8,128)(2,1)S(1)} %get-tuple-element.29), channel_id=1, source_target_pairs={{0,16},{16,0},{1,17},{17,1},{2,18},{18,2},{3,19},{19,3},{4,20},{20... | collective-permute-start | bytes 786440 | tf_op jit(solution)/shard_map/ppermute | solution.py:427
  15.6 12.8 %collective-permute-start.1 = (bf16[2,64,512]{2,1,0:T(8,128)(2,1)S(1)}, bf16[2,64,512]{2,1,0:T(8,128)(2,1)S(1)}, u32[]{:S(2)}, u32[]{:S(2)}) collective-permute-start(bf16[2,64,512]{2,1,0:T(8,128)(2,1)S(1)} %get-tuple-element.24), channel_id=1, source_target_pairs={{0,8},{4,12},{8,0},{12,4},{1,9},{5,13},{9,1},{13,5},{2,10},{6,14},... | collective-permute-start | bytes 393224 | tf_op jit(solution)/shard_map/ppermute | solution.py:430
  24.0 4.4 %collective-permute-start.4 = (bf16[2,64,256]{2,1,0:T(8,128)(2,1)S(1)}, bf16[2,64,256]{2,1,0:T(8,128)(2,1)S(1)}, u32[]{:S(2)}, u32[]{:S(2)}) collective-permute-start(bf16[2,64,256]{2,1,0:T(8,128)(2,1)S(1)} %get-tuple-element.28), channel_id=1, source_target_pairs={{0,8},{4,12},{8,0},{12,4},{1,9},{5,13},{9,1},{13,5},{2,10},{6,14},... | collective-permute-start | bytes 196616 | tf_op jit(solution)/shard_map/ppermute | solution.py:430
  26.2 7.4 %collective-permute-start.10 = (bf16[4,256,128]{2,1,0:T(8,128)(2,1)S(1)}, bf16[4,256,128]{2,1,0:T(8,128)(2,1)S(1)}, u32[]{:S(2)}, u32[]{:S(2)}) collective-permute-start(bf16[4,256,128]{2,1,0:T(8,128)(2,1)S(1)} %get-tuple-element.38), channel_id=1, source_target_pairs={{0,16},{16,0},{1,17},{17,1},{2,18},{18,2},{3,19},{19,3},{4,20},{20... | collective-permute-start | bytes 786440 | tf_op jit(solution)/shard_map/ppermute | solution.py:427
  28.4 3.3 %collective-permute-start.5 = (bf16[2,64,256]{2,1,0:T(8,128)(2,1)S(1)}, bf16[2,64,256]{2,1,0:T(8,128)(2,1)S(1)}, u32[]{:S(2)}, u32[]{:S(2)}) collective-permute-start(bf16[2,64,256]{2,1,0:T(8,128)(2,1)S(1)} %join.5), channel_id=1, source_target_pairs={{0,4},{4,0},{8,12},{12,8},{1,5},{5,1},{9,13},{13,9},{2,6},{6,2},{1... | collective-permute-start | bytes 196616 | tf_op jit(solution)/shard_map/ppermute | solution.py:430
  28.5 3.2 %collective-permute-start.2 = (bf16[2,64,512]{2,1,0:T(8,128)(2,1)S(1)}, bf16[2,64,512]{2,1,0:T(8,128)(2,1)S(1)}, u32[]{:S(2)}, u32[]{:S(2)}) collective-permute-start(bf16[2,64,512]{2,1,0:T(8,128)(2,1)S(1)} %join.4), channel_id=1, source_target_pairs={{0,4},{4,0},{8,12},{12,8},{1,5},{5,1},{9,13},{13,9},{2,6},{6,2},{1... | collective-permute-start | bytes 393224 | tf_op jit(solution)/shard_map/ppermute | solution.py:430
  29.6 5.8 %collective-permute-start.7 = (bf16[2,64,512]{2,1,0:T(8,128)(2,1)S(1)}, bf16[2,64,512]{2,1,0:T(8,128)(2,1)S(1)}, u32[]{:S(2)}, u32[]{:S(2)}) collective-permute-start(bf16[2,64,512]{2,1,0:T(8,128)(2,1)S(1)} %get-tuple-element.34), channel_id=1, source_target_pairs={{0,8},{4,12},{8,0},{12,4},{1,9},{5,13},{9,1},{13,5},{2,10},{6,14},... | collective-permute-start | bytes 393224 | tf_op jit(solution)/shard_map/ppermute | solution.py:430
  31.7 8.3 %collective-permute-start.9 = (bf16[4,64,512]{2,1,0:T(8,128)(2,1)S(1)}, bf16[4,64,512]{2,1,0:T(8,128)(2,1)S(1)}, u32[]{:S(2)}, u32[]{:S(2)}) collective-permute-start(bf16[4,64,512]{2,1,0:T(8,128)(2,1)S(1)} %gather_far.1), channel_id=1, source_target_pairs={{0,16},{16,0},{1,17},{17,1},{2,18},{18,2},{3,19},{19,3},{4,20},{20... | collective-permute-start | bytes 786440 | tf_op jit(solution)/shard_map/ppermute | solution.py:427
  34.1 1.3 %collective-permute-start.11 = (bf16[2,64,256]{2,1,0:T(8,128)(2,1)S(1)}, bf16[2,64,256]{2,1,0:T(8,128)(2,1)S(1)}, u32[]{:S(2)}, u32[]{:S(2)}) collective-permute-start(bf16[2,64,256]{2,1,0:T(8,128)(2,1)S(1)} %get-tuple-element.40), channel_id=1, source_target_pairs={{0,4},{4,0},{8,12},{12,8},{1,5},{5,1},{9,13},{13,9},{2,6},{6,2},{1... | collective-permute-start | bytes 196616 | tf_op jit(solution)/shard_map/ppermute | solution.py:430
  35.4 2.0 %collective-permute-start.8 = (bf16[2,64,512]{2,1,0:T(8,128)(2,1)S(1)}, bf16[2,64,512]{2,1,0:T(8,128)(2,1)S(1)}, u32[]{:S(2)}, u32[]{:S(2)}) collective-permute-start(bf16[2,64,512]{2,1,0:T(8,128)(2,1)S(1)} %join.6), channel_id=1, source_target_pairs={{0,4},{4,0},{8,12},{12,8},{1,5},{5,1},{9,13},{13,9},{2,6},{6,2},{1... | collective-permute-start | bytes 393224 | tf_op jit(solution)/shard_map/ppermute | solution.py:430
  35.5 4.5 %collective-permute-start.12 = (bf16[2,64,256]{2,1,0:T(8,128)(2,1)S(1)}, bf16[2,64,256]{2,1,0:T(8,128)(2,1)S(1)}, u32[]{:S(2)}, u32[]{:S(2)}) collective-permute-start(bf16[2,64,256]{2,1,0:T(8,128)(2,1)S(1)} %join.7), channel_id=1, source_target_pairs={{0,8},{4,12},{8,0},{12,4},{1,9},{5,13},{9,1},{13,5},{2,10},{6,14},... | collective-permute-start | bytes 196616 | tf_op jit(solution)/shard_map/ppermute | solution.py:430
